TPU v7x, 32 devices: a whole 2x2x4 slice. The times are simulated.
32 devices in a mesh: pipe: 4 (over y, core), tensor: 4 (over z), dp: 2 (over x).
Axes of the slice: x: 2, y: 2, z: 4, core: 2. Of those that a mesh axis runs over, the one named last changes fastest.
Arguments:
- narrowing_projection_weights: bfloat16 [4, 4, 5120, 256], P('pipe', None, 'tensor'), may hold values from -0.078125 to 0.078125
- widening_projection_weights: bfloat16 [4, 4, 256, 5120], P('pipe', None, None, 'tensor'), may hold values from -0.375 to 0.375
- scaling_multipliers: float32 [4, 4, 5120], P('pipe', None, 'tensor'), may hold values from 0.5 to 1.5
- slot_entry_activation: bfloat16 [4, 4, 64, 5120], P('pipe', None, 'dp', 'tensor'), may hold values from -15 to 15
- retained_section_entries: bfloat16 [2, 4, 4, 64, 5120], P(None, 'pipe', None, 'dp', 'tensor'), may hold values from -15 to 15
- slot_result_sensitivity: bfloat16 [4, 4, 64, 5120], P('pipe', None, 'dp', 'tensor'), may hold values from -4 to 4
- fresh_micro_batches: bfloat16 [1, 2, 64, 5120], P(None, None, 'dp', 'tensor'), may hold values from -15 to 15
- latest_result_sensitivity: bfloat16 [1, 2, 64, 5120], P(None, None, 'dp', 'tensor'), may hold values from -4 to 4
Outputs:
- section_outputs: bfloat16 [4, 4, 64, 5120], P('pipe', None, 'dp', 'tensor')
- input_grads: bfloat16 [4, 4, 64, 5120], P('pipe', None, 'dp', 'tensor')
- grad_down: float32 [4, 2, 5120, 256], P('pipe', None, ('tensor', 'dp'))
- grad_up: float32 [4, 2, 256, 5120], P('pipe', None, 'dp', 'tensor')
All inputs are finite; a program needn't handle non-finite values.
Results may differ from a plain program's by a relative error of at most 0.025.
Values may be sent and summed in bfloat16 or wider, within the bound.
No kernel may reach another device: no remote copies, remote signals or barrier semaphores. Data moves between devices by JAX's collectives and lax.ppermute only.
A program may use at most 64 MiB of HBM per device.

v0:
```python
import jax
import jax.numpy as jnp
from jax import lax
from jax.sharding import PartitionSpec as P

D = 5120


eps = 1e-06


def extended(cells, sides, width):
    for axis, dim in sides:
        count = lax.axis_size(axis)
        ends = count - 1
        head = lax.slice_in_dim(cells, 0, width, axis=dim)
        tail = lax.slice_in_dim(cells, cells.shape[dim] - width, cells.shape[dim], axis=dim)
        cells = jnp.concatenate(
            [
                lax.ppermute(tail, axis, [(i, (i + 1) % count) for i in range(ends)]),
                cells,
                lax.ppermute(head, axis, [((i + 1) % count, i) for i in range(ends)]),
            ],
            axis=dim,
        )
    return cells


def partner(value, axis, stride):
    mask = 2**stride
    pairs = [(source, source ^ mask) for source in range(lax.axis_size(axis))]
    return lax.ppermute(value, axis, pairs)


def per_device(
    narrowing_projection_weights,
    widening_projection_weights,
    scaling_multipliers,
    slot_entry_activation,
    retained_section_entries,
    slot_result_sensitivity,
    fresh_micro_batches,
    latest_result_sensitivity,
):
    holders = lax.axis_size("pipe")
    position = lax.axis_index("pipe")
    at_start = position == 0
    at_end = position == holders - 1
    w_down = narrowing_projection_weights[0]
    w_up = widening_projection_weights[0]
    gain_rows = scaling_multipliers[0]
    entry_activation_lines = slot_entry_activation[0]
    upstream = slot_result_sensitivity[0]
    grad_down = jnp.zeros(w_down.shape, jnp.float32)
    grad_up = jnp.zeros(w_up.shape, jnp.float32)
    ticks = retained_section_entries.shape[0]
    result_activation_lines = entry_activation_lines
    rows_grad = upstream
    for tick_index in range(ticks):
        stacked = jnp.stack([entry_activation_lines, retained_section_entries[tick_index, 0]])
        widened = stacked.astype(jnp.float32)
        scaled = (widened * gain_rows[None, :, None, :]).astype(jnp.bfloat16)
        part_latent = jnp.einsum(
            "csnd,sdr->csnr", scaled, w_down, preferred_element_type=jnp.float32
        )
        part_squares = jnp.sum(widened * widened, axis=-1)
        part_grad = jnp.einsum("snd,srd->snr", upstream, w_up, preferred_element_type=jnp.float32)
        latent, squares = (
            lax.psum(part_latent.astype(jnp.bfloat16), "tensor").astype(jnp.float32),
            lax.psum(part_squares.astype(jnp.bfloat16), "tensor").astype(jnp.float32),
        )
        hidden_rank_gradient = lax.psum(part_grad.astype(jnp.bfloat16), "tensor").astype(
            jnp.float32
        )
        factor = 1.0 / jnp.sqrt(squares / D + eps)
        preact = latent * factor[..., None]
        active = jax.nn.silu(preact).astype(jnp.bfloat16)
        result_activation_lines = (
            widened[0]
            + jnp.einsum("snr,srd->snd", active[0], w_up, preferred_element_type=jnp.float32)
        ).astype(jnp.bfloat16)
        sigmoid_z = jax.nn.sigmoid(preact[1])
        preact_grad = hidden_rank_gradient * sigmoid_z * (1.0 + preact[1] * (1.0 - sigmoid_z))
        latent_step = (preact_grad * factor[1][..., None]).astype(jnp.bfloat16)
        gradient_squares = -0.5 * factor[1] ** 3 / D * jnp.sum(preact_grad * latent[1], axis=-1)
        feature_grad = (
            jnp.einsum("snr,sdr->snd", latent_step, w_down, preferred_element_type=jnp.float32)
            * gain_rows[:, None, :]
        )
        rows_grad = (
            feature_grad
            + 2.0 * widened[1] * gradient_squares[..., None]
            + upstream.astype(jnp.float32)
        ).astype(jnp.bfloat16)
        grad_down = grad_down + jnp.einsum(
            "snd,snr->sdr", scaled[1], latent_step, preferred_element_type=jnp.float32
        )
        grad_up = grad_up + jnp.einsum(
            "snr,snd->srd", active[1], upstream, preferred_element_type=jnp.float32
        )
        if tick_index + 1 < ticks:
            to_lower = jnp.stack(
                [result_activation_lines[1], result_activation_lines[2], rows_grad[0], rows_grad[3]]
            )
            to_upper = jnp.stack(
                [result_activation_lines[0], result_activation_lines[3], rows_grad[1], rows_grad[2]]
            )
            padded = extended(jnp.stack([to_lower, to_upper]), (("pipe", 0),), 1)
            from_below = padded[0]
            from_above = padded[3]
            entering = fresh_micro_batches[tick_index]
            arriving = latest_result_sensitivity[tick_index]
            entry_activation_lines = jnp.stack(
                [
                    jnp.where(at_start, entering[0], from_below[0]),
                    jnp.where(at_end, result_activation_lines[0], from_above[0]),
                    jnp.where(at_end, entering[1], from_above[1]),
                    jnp.where(at_start, result_activation_lines[2], from_below[1]),
                ]
            )
            upstream = jnp.stack(
                [
                    jnp.where(at_end, rows_grad[1], from_above[2]),
                    jnp.where(at_start, arriving[0], from_below[2]),
                    jnp.where(at_start, rows_grad[3], from_below[3]),
                    jnp.where(at_end, arriving[1], from_above[3]),
                ]
            )
    summed_down, summed_up = (
        lax.psum_scatter(
            grad_down.astype(jnp.bfloat16), "dp", scatter_dimension=1, tiled=True
        ).astype(jnp.float32),
        lax.psum_scatter(
            grad_up.astype(jnp.bfloat16), "dp", scatter_dimension=1, tiled=True
        ).astype(jnp.float32),
    )
    far_down = summed_down[2:]
    far_up = summed_up[2:]
    count_down = far_down.size
    flattened = jnp.concatenate([far_down.reshape(-1), far_up.reshape(-1)])
    for bit_index in range(holders.bit_length() - 1):
        flattened = partner(flattened.astype(jnp.bfloat16), "pipe", bit_index).astype(
            flattened.dtype
        )
    mirrored_down = flattened[:count_down].reshape(far_down.shape)
    mirrored_up = flattened[count_down:].reshape(far_up.shape)
    total_down = summed_down[:2] + mirrored_down
    total_up = summed_up[:2] + mirrored_up
    return (result_activation_lines[None], rows_grad[None], total_down[None], total_up[None])


def solution(mesh):
    return jax.shard_map(
        per_device,
        mesh=mesh,
        in_specs=(
            P("pipe", None, "tensor", None),
            P("pipe", None, None, "tensor"),
            P("pipe", None, "tensor"),
            P("pipe", None, "dp", "tensor"),
            P(None, "pipe", None, "dp", "tensor"),
            P("pipe", None, "dp", "tensor"),
            P(None, None, "dp", "tensor"),
            P(None, None, "dp", "tensor"),
        ),
        out_specs=(
            P("pipe", None, "dp", "tensor"),
            P("pipe", None, "dp", "tensor"),
            P("pipe", None, ("tensor", "dp"), None),
            P("pipe", None, "dp", "tensor"),
        ),
        check_vma=False,
    )
```

profile of v0, /device:TPU:0, one launch (start us, length us, event | category | flops | bytes accessed | tf_op | source)
XLA Modules:
  0.0 258.4 jit_solution(10038259662542239829)
XLA Ops:
  7.2 2.0 slice_bitcast_fusion.9
  9.3 3.4 %fusion.70 = bf16[4,32,256]{2,1,0:T(8,128)(2,1)} fusion(bf16[1,4,256,1280]{3,2,1,0:T(8,128)(2,1)} %param.9, bf16[1,4,32,1280]{3,2,1,0:T(8,128)(2,1)S(1)} %copy-done.5), kind=kOutput, calls=%fused_computation.43 | convolution fusion | flops 83918848 | bytes 3014656 | tf_op jit(solution)/shard_map/snd,srd->snr/dot_general | solution.py:67
  12.9 1.2 fusion.64
  14.2 2.2 maximum_convert_fusion
  16.4 13.4 %psum.43 = bf16[2,4,32]{2,1,0:T(4,128)(2,1)S(1)} all-reduce(bf16[2,4,32]{2,1,0:T(4,128)(2,1)S(1)} %get-tuple-element.14), channel_id=1, replica_groups=mesh['pipe'=4,'tensor'=4,'dp'=2] {'tensor'}, use_global_device_ids=true, to_apply=%region_2.0 | all-reduce | flops 256 | bytes 1024 | tf_op jit(solution)/shard_map/psum | solution.py:70
  29.9 22.1 %all-reduce.7.cloned.1.call-done = (bf16[2,4,32,256]{3,2,0,1:T(8,128)(2,1)}, bf16[4,32,256]{2,1,0:T(8,128)(2,1)}) async-done(((bf16[2,4,32,256]{3,2,0,1:T(8,128)(2,1)}, bf16[4,32,256]{2,1,0:T(8,128)(2,1)}), (bf16[2,4,32,256]{3,2,0,1:T(8,128)(2,1)}, bf16[4,32,256]{2,1,0:T(8,128)(2,1)})) %all-reduce.7.cloned.1.call-update) | async-done | bytes 196624 | tf_op jit(solution)/shard_map/psum | solution.py:69
  54.6 2.5 fusion.43
  58.4 1.3 collective-permute-start.1
  59.8 3.2 %collective-permute-start = (bf16[1,4,32,1280]{3,2,1,0:T(8,128)(2,1)S(1)}, bf16[1,4,32,1280]{3,2,1,0:T(8,128)(2,1)S(1)}, u32[]{:S(2)}, u32[]{:S(2)}) collective-permute-start(bf16[1,4,32,1280]{3,2,1,0:T(8,128)(2,1)S(1)} %maximum_bitcast_fusion), channel_id=1, source_target_pairs={{0,8},{8,16},{16,24},{1,9},{9,17},{17,25},{2,10},{10,18},{18,26},{... | collective-permute-start | bytes 983048 | tf_op jit(solution)/shard_map/ppermute | solution.py:20
  63.0 3.2 %fusion.79 = f32[4,1280,256]{2,1,0:T(8,128)} fusion(bf16[2,4,32,1280]{3,2,1,0:T(8,128)(2,1)S(1)} %get-tuple-element.15, f32[4,32]{1,0:T(4,128)S(1)} %slice_bitcast_fusion.27, f32[2,4,32,256]{3,2,1,0:T(8,128)S(1)} %get-tuple-element.9, bf16[4,32,256]{2,1,0:T(8,128)(2,1)S(1)} %copy-done.28), kind=kOutput, calls=%fused_computation.56 | convolution fusion | flops 84246528 | bytes 5769216 | tf_op jit(solution)/shard_map/snd,snr->sdr/dot_general | solution.py:95
  67.8 10.6 %psum.46 = bf16[2,4,32]{2,1,0:T(4,128)(2,1)S(1)} all-reduce(bf16[2,4,32]{2,1,0:T(4,128)(2,1)S(1)} %get-tuple-element.13), channel_id=1, replica_groups=mesh['pipe'=4,'tensor'=4,'dp'=2] {'tensor'}, use_global_device_ids=true, to_apply=%region_7.8 | all-reduce | flops 256 | bytes 1024 | tf_op jit(solution)/shard_map/psum | solution.py:70
  78.4 1.2 fusion.67
  80.2 1.5 fusion.73
  81.8 35.7 %all-reduce.5.cloned.1.call-done = (bf16[2,4,32,256]{3,2,1,0:T(8,128)(2,1)}, bf16[4,32,256]{2,1,0:T(8,128)(2,1)}) async-done(((bf16[2,4,32,256]{3,2,1,0:T(8,128)(2,1)}, bf16[4,32,256]{2,1,0:T(8,128)(2,1)}), (bf16[2,4,32,256]{3,2,1,0:T(8,128)(2,1)}, bf16[4,32,256]{2,1,0:T(8,128)(2,1)})) %all-reduce.5.cloned.1.call-update) | async-done | bytes 196624 | tf_op jit(solution)/shard_map/psum | solution.py:69
  117.5 1.7 broadcast_multiply_fusion
  119.2 5.0 %add_convert_fusion.1 = bf16[4,1280,256]{2,1,0:T(8,128)(2,1)} fusion(f32[4,1280,256]{2,1,0:T(8,128)} %fusion.79, bf16[2,4,32,1280]{3,2,1,0:T(8,128)(2,1)S(1)} %get-tuple-element.12, f32[4,32]{1,0:T(4,128)S(1)} %slice_bitcast_fusion.26, f32[2,4,32,256]{3,2,1,0:T(8,128)S(1)} %get-tuple-element.32, bf16[4,32,256]{2,1,0:T(8,128)(2,1)} %get-tuple-element.5), kind=kOutput, calls=%fused_computation.1 | convolution fusion | flops 86867968 | bytes 8390656 | tf_op jit(solution)/shard_map/snd,snr->sdr/dot_general | solution.py:95
  125.1 1.8 fusion.80
  126.9 2.4 add_convert_fusion
  129.3 32.3 %reduce-scatter.3.cloned.1.call-done = bf16[4,640,256]{2,1,0:T(8,128)(2,1)} async-done(((bf16[4,1280,256]{2,1,0:T(8,128)(2,1)}), bf16[4,640,256]{2,1,0:T(8,128)(2,1)}) %reduce-scatter.3.cloned.1.call-update) | async-done | bytes 1310736 | tf_op jit(solution)/shard_map/reduce_scatter | solution.py:130
  163.4 38.1 %reduce-scatter.5.cloned.1.call-done = bf16[4,128,1280]{2,1,0:T(8,128)(2,1)} async-done(((bf16[4,256,1280]{2,1,0:T(8,128)(2,1)}), bf16[4,128,1280]{2,1,0:T(8,128)(2,1)}) %reduce-scatter.5.cloned.1.call-update) | async-done | bytes 1310736 | tf_op jit(solution)/shard_map/reduce_scatter | solution.py:133
  201.4 2.0 slice.264
  203.4 2.5 reshape.171
  205.9 1.3 pad_maximum_fusion
  207.3 3.0 %collective-permute-done.2 = bf16[655360]{0:T(1024)(128)(2,1)S(1)} collective-permute-done((bf16[655360]{0:T(1024)(128)(2,1)S(1)}, bf16[655360]{0:T(1024)(128)(2,1)S(1)}, u32[]{:S(2)}, u32[]{:S(2)}) %collective-permute-start.2) | collective-permute-done | bytes 1310752 | tf_op jit(solution)/shard_map/ppermute | solution.py:32
  210.3 1.5 collective-permute-start.3
  212.2 1.3 fusion.55
  213.5 1.6 fusion.52
  215.1 26.0 %collective-permute-done.3 = bf16[655360]{0:T(1024)(128)(2,1)S(1)} collective-permute-done((bf16[655360]{0:T(1024)(128)(2,1)S(1)}, bf16[655360]{0:T(1024)(128)(2,1)S(1)}, u32[]{:S(2)}, u32[]{:S(2)}) %collective-permute-start.3) | collective-permute-done | bytes 1310752 | tf_op jit(solution)/shard_map/ppermute | solution.py:32
  241.1 1.7 fusion.101
  242.8 2.5 slice.229
  245.3 2.6 %slice.225 = f32[2,640,256]{2,1,0:T(8,128)} reshape(f32[327680]{0:T(1024)} %get-tuple-element.11) | data formatting | bytes 2621440 | tf_op jit(solution)/shard_map/slice | solution.py:145
  247.9 2.8 %add_bitcast_fusion = f32[1,2,128,1280]{3,2,1,0:T(8,128)} fusion(f32[2,128,1280]{2,1,0:T(8,128)} %slice.229, bf16[4,128,1280]{2,1,0:T(8,128)(2,1)} %reduce-scatter.5.cloned.1.call-done), kind=kLoop, calls=%fused_computation.33 | loop fusion | flops 655360 | bytes 3276800 | tf_op jit(solution)/shard_map/broadcast_in_dim | solution.py:149
  (113 shorter events, 10.7 us)
Async XLA Ops:
  7.2 5.8 %copy-start = (bf16[1,4,1280,256]{3,2,1,0:T(8,128)(2,1)S(1)}, bf16[1,4,1280,256]{3,2,1,0:T(8,128)(2,1)}, u32[]{:S(2)}) copy-start(bf16[1,4,1280,256]{3,2,1,0:T(8,128)(2,1)} %param.8) | copy-start | bytes 7864324
  7.2 44.8 %all-reduce.7.cloned.1.call-start = ((), (), s32[]{:S(2)}) async-start(), calls=%async_computation.5 | async-start | bytes 393216 | tf_op jit(solution)/shard_map/psum | solution.py:69
  9.3 3.4 %copy-start.10 = (bf16[1,4,32,1280]{3,2,1,0:T(8,128)(2,1)}, bf16[1,4,32,1280]{3,2,1,0:T(8,128)(2,1)S(1)}, u32[]{:S(2)}) copy-start(bf16[1,4,32,1280]{3,2,1,0:T(8,128)(2,1)S(1)} %get-tuple-element.16) | copy-start | bytes 983044
  9.3 3.4 %copy-start.26 = (bf16[1,4,32,1280]{3,2,1,0:T(8,128)(2,1)S(1)}, bf16[1,4,32,1280]{3,2,1,0:T(8,128)(2,1)}, u32[]{:S(2)}) copy-start(bf16[1,4,32,1280]{3,2,1,0:T(8,128)(2,1)} %param.11) | copy-start | bytes 983044
  9.3 3.4 %copy-start.33 = (f32[1,4,1280]{2,1,0:T(4,128)S(1)}, f32[1,4,1280]{2,1,0:T(4,128)}, u32[]{:S(2)}) copy-start(f32[1,4,1280]{2,1,0:T(4,128)} %param.10) | copy-start | bytes 61444
  14.2 103.3 %all-reduce.5.cloned.1.call-start = ((), (), s32[]{:S(2)}) async-start(), calls=%async_computation.4 | async-start | bytes 393216 | tf_op jit(solution)/shard_map/psum | solution.py:69
  54.6 2.6 %copy-start.28 = (bf16[4,32,256]{2,1,0:T(8,128)(2,1)S(1)}, bf16[4,32,256]{2,1,0:T(8,128)(2,1)}, u32[]{:S(2)}) copy-start(bf16[4,32,256]{2,1,0:T(8,128)(2,1)} %get-tuple-element.7) | copy-start | bytes 196612
  54.6 2.8 %copy-start.4 = (f32[2,4,32,1280]{3,2,1,0:T(8,128)S(1)}, f32[2,4,32,1280]{3,2,1,0:T(8,128)}, u32[]{:S(2)}) copy-start(f32[2,4,32,1280]{3,2,1,0:T(8,128)} %maximum_convert_fusion) | copy-start | bytes 3932164
  54.6 2.8 %copy-start.6 = (bf16[1,4,32,1280]{3,2,1,0:T(8,128)(2,1)S(1)}, bf16[1,4,32,1280]{3,2,1,0:T(8,128)(2,1)}, u32[]{:S(2)}) copy-start(bf16[1,4,32,1280]{3,2,1,0:T(8,128)(2,1)} %param.13) | copy-start | bytes 983044
  58.4 7.8 %collective-permute-start.1 = (bf16[1,4,32,1280]{3,2,1,0:T(8,128)(2,1)S(1)}, bf16[1,4,32,1280]{3,2,1,0:T(8,128)(2,1)S(1)}, u32[]{:S(2)}, u32[]{:S(2)}) collective-permute-start(bf16[1,4,32,1280]{3,2,1,0:T(8,128)(2,1)S(1)} %maximum_bitcast_fusion.1), channel_id=1, source_target_pairs={{8,0},{16,8},{24,16},{9,1},{17,9},{25,17},{10,2},{18,10},{26,18},{... | collective-permute-start | bytes 983048 | tf_op jit(solution)/shard_map/ppermute | solution.py:22
  59.8 6.5 %copy-start.35 = (bf16[1,2,32,1280]{3,2,1,0:T(8,128)(2,1)S(1)}, bf16[1,2,32,1280]{3,2,1,0:T(8,128)(2,1)}, u32[]{:S(2)}) copy-start(bf16[1,2,32,1280]{3,2,1,0:T(8,128)(2,1)} %param.15) | copy-start | bytes 491524
  59.8 6.5 %copy-start.36 = (bf16[1,2,32,1280]{3,2,1,0:T(8,128)(2,1)S(1)}, bf16[1,2,32,1280]{3,2,1,0:T(8,128)(2,1)}, u32[]{:S(2)}) copy-start(bf16[1,2,32,1280]{3,2,1,0:T(8,128)(2,1)} %param.14) | copy-start | bytes 491524
  59.8 6.4 %collective-permute-start = (bf16[1,4,32,1280]{3,2,1,0:T(8,128)(2,1)S(1)}, bf16[1,4,32,1280]{3,2,1,0:T(8,128)(2,1)S(1)}, u32[]{:S(2)}, u32[]{:S(2)}) collective-permute-start(bf16[1,4,32,1280]{3,2,1,0:T(8,128)(2,1)S(1)} %maximum_bitcast_fusion), channel_id=1, source_target_pairs={{0,8},{8,16},{16,24},{1,9},{9,17},{17,25},{2,10},{10,18},{18,26},{... | collective-permute-start | bytes 983048 | tf_op jit(solution)/shard_map/ppermute | solution.py:20
  66.3 13.3 %copy-start.14 = (bf16[1,32,1280]{2,1,0:T(8,128)(2,1)}, bf16[1,32,1280]{2,1,0:T(8,128)(2,1)S(1)}, u32[]{:S(2)}) copy-start(bf16[1,32,1280]{2,1,0:T(8,128)(2,1)S(1)} %get-tuple-element.18) | copy-start | bytes 245764
  66.3 13.3 %copy-start.17 = (bf16[1,32,1280]{2,1,0:T(8,128)(2,1)}, bf16[1,32,1280]{2,1,0:T(8,128)(2,1)S(1)}, u32[]{:S(2)}) copy-start(bf16[1,32,1280]{2,1,0:T(8,128)(2,1)S(1)} %get-tuple-element.19) | copy-start | bytes 245764
  67.0 12.6 %copy-start.20 = (bf16[1,32,1280]{2,1,0:T(8,128)(2,1)}, bf16[1,32,1280]{2,1,0:T(8,128)(2,1)S(1)}, u32[]{:S(2)}) copy-start(bf16[1,32,1280]{2,1,0:T(8,128)(2,1)S(1)} %get-tuple-element.24) | copy-start | bytes 245764
  81.7 79.9 %reduce-scatter.3.cloned.1.call-start = ((), (), s32[]{:S(2)}) async-start(), calls=%async_computation.2 | async-start | bytes 3932160 | tf_op jit(solution)/shard_map/reduce_scatter | solution.py:130
  124.1 2.7 %copy-start.15 = (bf16[1,32,1280]{2,1,0:T(8,128)(2,1)S(1)}, bf16[1,32,1280]{2,1,0:T(8,128)(2,1)}, u32[]{:S(2)}) copy-start(bf16[1,32,1280]{2,1,0:T(8,128)(2,1)} %copy-done.14) | copy-start | bytes 245764
  124.1 2.7 %copy-start.18 = (bf16[1,32,1280]{2,1,0:T(8,128)(2,1)S(1)}, bf16[1,32,1280]{2,1,0:T(8,128)(2,1)}, u32[]{:S(2)}) copy-start(bf16[1,32,1280]{2,1,0:T(8,128)(2,1)} %copy-done.17) | copy-start | bytes 245764
  124.2 2.7 %copy-start.21 = (bf16[1,32,1280]{2,1,0:T(8,128)(2,1)S(1)}, bf16[1,32,1280]{2,1,0:T(8,128)(2,1)}, u32[]{:S(2)}) copy-start(bf16[1,32,1280]{2,1,0:T(8,128)(2,1)} %copy-done.20) | copy-start | bytes 245764
  124.2 2.7 %copy-start.24 = (bf16[1,32,1280]{2,1,0:T(8,128)(2,1)S(1)}, bf16[1,32,1280]{2,1,0:T(8,128)(2,1)}, u32[]{:S(2)}) copy-start(bf16[1,32,1280]{2,1,0:T(8,128)(2,1)} %get-tuple-element.27) | copy-start | bytes 245764
  124.2 77.2 %reduce-scatter.5.cloned.1.call-start = ((), (), s32[]{:S(2)}) async-start(), calls=%async_computation.3 | async-start | bytes 3932160 | tf_op jit(solution)/shard_map/reduce_scatter | solution.py:133
  205.9 5.9 %copy-start.9 = (bf16[1,4,32,1280]{3,2,1,0:T(8,128)(2,1)S(1)}, bf16[1,4,32,1280]{3,2,1,0:T(8,128)(2,1)}, u32[]{:S(2)}) copy-start(bf16[1,4,32,1280]{3,2,1,0:T(8,128)(2,1)} %get-tuple-element.17) | copy-start | bytes 983044
  205.9 5.9 %copy-start.12 = (bf16[1,4,32,1280]{3,2,1,0:T(8,128)(2,1)S(1)}, bf16[1,4,32,1280]{3,2,1,0:T(8,128)(2,1)}, u32[]{:S(2)}) copy-start(bf16[1,4,32,1280]{3,2,1,0:T(8,128)(2,1)} %copy-done.11) | copy-start | bytes 983044
  205.9 6.0 %copy-start.32 = (bf16[2,4,32,256]{3,2,1,0:T(8,128)(2,1)S(1)}, bf16[2,4,32,256]{3,2,1,0:T(8,128)(2,1)}, u32[]{:S(2)}) copy-start(bf16[2,4,32,256]{3,2,1,0:T(8,128)(2,1)} %get-tuple-element.4) | copy-start | bytes 393220
  205.9 6.0 %copy-start.27 = (bf16[4,32,256]{2,1,0:T(8,128)(2,1)S(1)}, bf16[4,32,256]{2,1,0:T(8,128)(2,1)}, u32[]{:S(2)}) copy-start(bf16[4,32,256]{2,1,0:T(8,128)(2,1)} %get-tuple-element.5) | copy-start | bytes 196612
  205.9 6.2 %copy-start.31 = (bf16[2,4,32,256]{3,2,1,0:T(8,128)(2,1)S(1)}, bf16[2,4,32,256]{3,2,1,0:T(8,128)(2,1)}, u32[]{:S(2)}) copy-start(bf16[2,4,32,256]{3,2,1,0:T(8,128)(2,1)} %get-tuple-element.33) | copy-start | bytes 393220
  207.2 4.9 %copy-start.2 = (bf16[1,4,256,1280]{3,2,1,0:T(8,128)(2,1)S(1)}, bf16[1,4,256,1280]{3,2,1,0:T(8,128)(2,1)}, u32[]{:S(2)}) copy-start(bf16[1,4,256,1280]{3,2,1,0:T(8,128)(2,1)} %param.9) | copy-start | bytes 7864324
  207.2 3.1 %collective-permute-start.2 = (bf16[655360]{0:T(1024)(128)(2,1)S(1)}, bf16[655360]{0:T(1024)(128)(2,1)S(1)}, u32[]{:S(2)}, u32[]{:S(2)}) collective-permute-start(bf16[655360]{0:T(1024)(128)(2,1)S(1)} %pad_maximum_fusion), channel_id=1, source_target_pairs={{0,8},{8,0},{16,24},{24,16},{1,9},{9,1},{17,25},{25,17},{2,10},{10... | collective-permute-start | bytes 3932168 | tf_op jit(solution)/shard_map/ppermute | solution.py:32
  210.3 30.8 %collective-permute-start.3 = (bf16[655360]{0:T(1024)(128)(2,1)S(1)}, bf16[655360]{0:T(1024)(128)(2,1)S(1)}, u32[]{:S(2)}, u32[]{:S(2)}) collective-permute-start(bf16[655360]{0:T(1024)(128)(2,1)S(1)} %collective-permute-done.2), channel_id=1, source_target_pairs={{0,16},{8,24},{16,0},{24,8},{1,17},{9,25},{17,1},{25,9},{2,18},{10... | collective-permute-start | bytes 3932168 | tf_op jit(solution)/shard_map/ppermute | solution.py:32
  247.9 2.8 %copy-start.3 = (f32[2,640,256]{2,1,0:T(8,128)S(1)}, f32[2,640,256]{2,1,0:T(8,128)}, u32[]{:S(2)}) copy-start(f32[2,640,256]{2,1,0:T(8,128)} %slice.225) | copy-start | bytes 3932164
  247.9 2.8 %copy-start.13 = (bf16[4,640,256]{2,1,0:T(8,128)(2,1)S(1)}, bf16[4,640,256]{2,1,0:T(8,128)(2,1)}, u32[]{:S(2)}) copy-start(bf16[4,640,256]{2,1,0:T(8,128)(2,1)} %reduce-scatter.3.cloned.1.call-done) | copy-start | bytes 3932164
  (14 other events, 18.5 us)
Sparse Core Ops, SparseCore 0:
  14.3 37.6 all-reduce.6
  81.8 35.5 all-reduce.4
  124.3 37.3 reduce-scatter.2
  163.8 37.5 reduce-scatter.4
where the time goes:
time: 259 us; the launch traced here: 258 us
  waiting for transfers between devices  157 us (61%)
  matrix products  25.9 us (10%)
  blocking collectives  24 us (9%)
  local copies, waits for them, and re-layouts  17.7 us (7%)
  between operations  14.2 us (5%)
  other arithmetic  13 us (5%)
  starting transfers between devices  6.2 us (2%)
    psum x2, waiting for transfers between devices, per_device(): lax.psum(part_latent.astype(jnp.bfloat16), 'tensor').astype(jnp.float32)  57.8 us
    reduce_scatter x1, waiting for transfers between devices, per_device(): lax.psum_scatter(grad_up.astype(jnp.bfloat16), 'dp', scatter_dimension=1,...  38.1 us
    reduce_scatter x1, waiting for transfers between devices, per_device(): lax.psum_scatter(grad_down.astype(jnp.bfloat16), 'dp', scatter_dimension=...  32.3 us
    ppermute x2, waiting for transfers between devices, partner(): return lax.ppermute(value, axis, pairs)  29.1 us
    psum x2, blocking collectives, per_device(): lax.psum(part_squares.astype(jnp.bfloat16), 'tensor').astype(jnp.float32)  24 us
    dot_general x2, matrix products, per_device(): jnp.einsum('snd,snr->sdr', scaled[1], latent_step, preferred_element_type...  8.19 us
  transfers between devices with their start and end apart: 8, of which 6 were waited for; matrix products, arithmetic and copies ran while one was open for 5% of the time, Pallas kernels for 0%

commit v1 on v0

v1 whole, which is shorter than its diff:
```python
import functools
import math

import jax
import jax.numpy as jnp
from jax import lax
from jax.experimental import pallas as pl
from jax.experimental.pallas import tpu as pltpu
from jax.sharding import PartitionSpec as P

D = 5120
EPS = 1e-06
LANES = 128
F32 = jnp.float32
BF16 = jnp.bfloat16

NN = (((1,), (0,)), ((), ()))
NT = (((1,), (1,)), ((), ()))
TN = (((0,), (0,)), ((), ()))


def dot(a, b, dims=NN):
    return lax.dot_general(a, b, dims, preferred_element_type=F32)


def params():
    return pltpu.CompilerParams(vmem_limit_bytes=48 * 2**20)


def on_lanes(columns, rows):
    lane = lax.broadcasted_iota(jnp.int32, (rows, LANES), 1)
    out = jnp.zeros((rows, LANES), F32)
    for index, column in enumerate(columns):
        out = jnp.where(lane == index, column, out)
    return out


def squares_of(rows):
    return jnp.sum(rows * rows, axis=-1, keepdims=True)


def whole(shape):
    return pl.BlockSpec(shape, lambda s, *_: (0,) * len(shape))


def deal(table, outs, place, chunk):
    for k, out in enumerate(outs):
        start = pl.multiple_of((place ^ k) * chunk, chunk)
        out[...] = table[pl.ds(start, chunk), :]


def first_partials_body(
    parts, chunk, info, x_ref, kept_ref, dy_ref, gain_ref, down_ref, up_ref, *rest
):
    outs, table = rest[:parts], rest[parts]
    s = pl.program_id(0)
    rows = x_ref.shape[0]
    ticks = kept_ref.shape[0]
    gain = gain_ref[...]
    streams = [x_ref[...].astype(F32)] + [kept_ref[t].astype(F32) for t in range(ticks)]
    scaled = jnp.concatenate([(v * gain).astype(BF16) for v in streams], axis=0)
    latent = dot(scaled, down_ref[...])
    grad = dot(dy_ref[...], up_ref[...], NT)
    pieces = [latent[i * rows : (i + 1) * rows] for i in range(ticks + 1)]
    pieces += [grad, on_lanes([squares_of(v) for v in streams], rows)]
    start = pl.multiple_of(s * rows, rows)
    table[pl.ds(start, rows), :] = jnp.concatenate(pieces, axis=1).astype(BF16)

    @pl.when(s == pl.num_programs(0) - 1)
    def _():
        deal(table, outs, info[0], chunk)


def first_partials(info, parts, x, kept, dy, gain, w_down, w_up):
    slots, rows, feats = x.shape
    ticks = kept.shape[0]
    rank = w_down.shape[-1]
    chunk = slots * rows // parts
    width = (ticks + 2) * rank + LANES
    per_slot = pl.BlockSpec((None, rows, feats), lambda s, *_: (s, 0, 0))
    return pl.pallas_call(
        functools.partial(first_partials_body, parts, chunk),
        grid_spec=pltpu.PrefetchScalarGridSpec(
            num_scalar_prefetch=1,
            grid=(slots,),
            in_specs=[
                per_slot,
                pl.BlockSpec((ticks, None, rows, feats), lambda s, *_: (0, s, 0, 0)),
                per_slot,
                pl.BlockSpec((None, 1, feats), lambda s, *_: (s, 0, 0)),
                pl.BlockSpec((None, feats, rank), lambda s, *_: (s, 0, 0)),
                pl.BlockSpec((None, rank, feats), lambda s, *_: (s, 0, 0)),
            ],
            out_specs=[whole((chunk, width))] * parts,
            scratch_shapes=[pltpu.VMEM((slots * rows, width), BF16)],
        ),
        out_shape=[jax.ShapeDtypeStruct((chunk, width), BF16)] * parts,
        compiler_params=params(),
        name="first_partials",
    )(info, x, kept, dy, gain, w_down, w_up)


def total(refs):
    value = refs[0][...].astype(F32)
    for ref in refs[1:]:
        value = value + ref[...].astype(F32)
    return value


def scale_of(squares):
    return 1.0 / jnp.sqrt(squares / D + EPS)


def logistic(z):
    return 1.0 / (1.0 + jnp.exp(-z))


def latent_grads(da, u, r, rank):
    z = u * r
    gate = logistic(z)
    dz = da * gate * (1.0 + z * (1.0 - gate))
    dss = (-0.5 / D) * r * r * r * jnp.sum(dz * u, axis=-1, keepdims=True)
    return dz * r, dss


def first_latents_body(parts, ticks, rank, *refs):
    ins, (out, held) = refs[:parts], refs[parts:]
    value = total(ins)
    chunk = value.shape[0]
    base = (ticks + 2) * rank
    streams = []
    for i in range(ticks + 1):
        u = value[:, i * rank : (i + 1) * rank]
        r = scale_of(value[:, base + i : base + i + 1])
        streams.append((u, r))
    da = value[:, (ticks + 1) * rank : base]
    du, dss = latent_grads(da, *streams[1], rank)
    actives = [u * r * logistic(u * r) for u, r in streams]
    tail = on_lanes([dss], chunk)
    out[...] = jnp.concatenate([actives[0], du, tail] + actives[1:], axis=1).astype(BF16)
    pieces = []
    for u, r in streams[2:]:
        pieces += [u, on_lanes([r], chunk)]
    held[...] = jnp.concatenate(pieces, axis=1)


def first_latents(parts, ticks, rank, received):
    chunk = received[0].shape[0]
    return pl.pallas_call(
        functools.partial(first_latents_body, parts, ticks, rank),
        out_shape=[
            jax.ShapeDtypeStruct((chunk, (ticks + 2) * rank + LANES), BF16),
            jax.ShapeDtypeStruct((chunk, (ticks - 1) * (rank + LANES)), F32),
        ],
        compiler_params=params(),
        name="first_latents",
    )(*received)


def later_latents_body(parts, rank, *refs):
    ins, held, out = refs[:parts], refs[parts], refs[parts + 1]
    value = total(ins)
    chunk = value.shape[0]
    z = value[:, :rank] * scale_of(value[:, 2 * rank : 2 * rank + 1])
    du, dss = latent_grads(
        value[:, rank : 2 * rank], held[:, :rank], held[:, rank : rank + 1], rank
    )
    pieces = [z * logistic(z), du, on_lanes([dss], chunk)]
    out[...] = jnp.concatenate(pieces, axis=1).astype(BF16)


def later_latents(parts, rank, received, held):
    chunk = received[0].shape[0]
    return pl.pallas_call(
        functools.partial(later_latents_body, parts, rank),
        out_shape=jax.ShapeDtypeStruct((chunk, 2 * rank + LANES), BF16),
        compiler_params=params(),
        name="later_latents",
    )(*received, held)


def gather_table(ins, table, place, chunk):
    for k, ref in enumerate(ins):
        start = pl.multiple_of((place ^ k) * chunk, chunk)
        table[pl.ds(start, chunk), :] = ref[...]


def slot_results(s, table, rank, x_ref, kept_ref, dy_ref, gain_ref, down_ref, up_ref):
    rows = x_ref.shape[0]
    own = table[pl.ds(pl.multiple_of(s * rows, rows), rows), :]
    active = own[:, :rank]
    du = own[:, rank : 2 * rank]
    dss = own[:, 2 * rank : 2 * rank + 1].astype(F32)
    y = x_ref[...].astype(F32) + dot(active, up_ref[...])
    dh = dot(du, down_ref[...], NT) * gain_ref[...]
    dh = dh + 2.0 * kept_ref[...].astype(F32) * dss + dy_ref[...].astype(F32)
    return y.astype(BF16), dh.astype(BF16), own


def middle_results_body(parts, chunk, rank, info, *refs):
    ins, refs = refs[:parts], refs[parts:]
    weights, (first, second, du_out, active_out, table) = refs[:6], refs[6:]
    s = pl.program_id(0)

    @pl.when(s == 0)
    def _():
        gather_table(ins, table, info[0], chunk)

    y, dh, own = slot_results(s, table, rank, *weights)
    du_out[...] = own[:, rank : 2 * rank]
    for t in range(active_out.shape[0]):
        base = 2 * rank + LANES + t * rank
        active_out[t] = own[:, base : base + rank]
    outer = jnp.logical_or(s == 0, s == 3).astype(jnp.int32)
    half = lax.shift_right_logical(s, 1)

    @pl.when(outer != info[1])
    def _():
        first[half] = y
        second[half + 2] = dh

    @pl.when(outer == info[1])
    def _():
        second[half] = y
        first[half + 2] = dh


def middle_results(info, parts, ticks, received, x, kept, dy, gain, w_down, w_up):
    slots, rows, feats = x.shape
    rank = w_down.shape[-1]
    chunk, width = received[0].shape
    per_slot = pl.BlockSpec((None, rows, feats), lambda s, *_: (s, 0, 0))
    return pl.pallas_call(
        functools.partial(middle_results_body, parts, chunk, rank),
        grid_spec=pltpu.PrefetchScalarGridSpec(
            num_scalar_prefetch=1,
            grid=(slots,),
            in_specs=[whole((chunk, width))] * parts
            + [
                per_slot,
                pl.BlockSpec((None, None, rows, feats), lambda s, *_: (0, s, 0, 0)),
                per_slot,
                pl.BlockSpec((None, 1, feats), lambda s, *_: (s, 0, 0)),
                pl.BlockSpec((None, feats, rank), lambda s, *_: (s, 0, 0)),
                pl.BlockSpec((None, rank, feats), lambda s, *_: (s, 0, 0)),
            ],
            out_specs=[
                whole((slots, rows, feats)),
                whole((slots, rows, feats)),
                pl.BlockSpec((None, rows, rank), lambda s, *_: (s, 0, 0)),
                pl.BlockSpec((ticks, None, rows, rank), lambda s, *_: (0, s, 0, 0)),
            ],
            scratch_shapes=[pltpu.VMEM((slots * rows, width), BF16)],
        ),
        out_shape=[
            jax.ShapeDtypeStruct((slots, rows, feats), BF16),
            jax.ShapeDtypeStruct((slots, rows, feats), BF16),
            jax.ShapeDtypeStruct((slots, rows, rank), BF16),
            jax.ShapeDtypeStruct((ticks, slots, rows, rank), BF16),
        ],
        compiler_params=params(),
        name="middle_results",
    )(info, *received, x, kept, dy, gain, w_down, w_up)


def later_partials_body(parts, chunk, info, *refs):
    xa, xb, ga, gb, own_x, own_g, fresh, arriving = (ref[...] for ref in refs[:8])
    gain_ref, down_ref, up_ref = refs[8:11]
    outs, (x_out, g_out, table) = refs[11 : 11 + parts], refs[11 + parts :]
    s = pl.program_id(0)
    rows = x_out.shape[0]
    outer = jnp.logical_or(s == 0, s == 3).astype(jnp.int32)
    even_slot = (s & 1) == 0
    edge = info[2] == 1
    xb = jnp.where(edge, jnp.where(even_slot, fresh, own_x), xb)
    gb = jnp.where(edge, jnp.where(even_slot, own_g, arriving), gb)
    x = jnp.where(outer == info[1], xa, xb)
    g = jnp.where(outer == info[1], gb, ga)
    x_out[...] = x
    g_out[...] = g
    wide = x.astype(F32)
    latent = dot((wide * gain_ref[...]).astype(BF16), down_ref[...])
    grad = dot(g, up_ref[...], NT)
    pieces = [latent, grad, on_lanes([squares_of(wide)], rows)]
    start = pl.multiple_of(s * rows, rows)
    table[pl.ds(start, rows), :] = jnp.concatenate(pieces, axis=1).astype(BF16)

    @pl.when(s == pl.num_programs(0) - 1)
    def _():
        deal(table, outs, info[0], chunk)


def later_partials(info, parts, first, second, own, fresh, arriving, gain, w_down, w_up):
    slots, rows, feats = first.shape
    rank = w_down.shape[-1]
    chunk = slots * rows // parts
    width = 2 * rank + LANES
    act = pl.BlockSpec((None, rows, feats), lambda s, *_: (s // 2, 0, 0))
    sens = pl.BlockSpec((None, rows, feats), lambda s, *_: (2 + s // 2, 0, 0))
    per_slot = pl.BlockSpec((None, rows, feats), lambda s, *_: (s, 0, 0))
    return pl.pallas_call(
        functools.partial(later_partials_body, parts, chunk),
        grid_spec=pltpu.PrefetchScalarGridSpec(
            num_scalar_prefetch=1,
            grid=(slots,),
            in_specs=[
                act,
                act,
                sens,
                sens,
                act,
                sens,
                act,
                act,
                pl.BlockSpec((None, 1, feats), lambda s, *_: (s, 0, 0)),
                pl.BlockSpec((None, feats, rank), lambda s, *_: (s, 0, 0)),
                pl.BlockSpec((None, rank, feats), lambda s, *_: (s, 0, 0)),
            ],
            out_specs=[whole((chunk, width))] * parts + [per_slot, per_slot],
            scratch_shapes=[pltpu.VMEM((slots * rows, width), BF16)],
        ),
        out_shape=[jax.ShapeDtypeStruct((chunk, width), BF16)] * parts
        + [jax.ShapeDtypeStruct((slots, rows, feats), BF16)] * 2,
        compiler_params=params(),
        name="later_partials",
    )(info, first, second, first, second, own, own, fresh, arriving, gain, w_down, w_up)


def last_results_body(parts, chunk, rank, info, *refs):
    ins, refs = refs[:parts], refs[parts:]
    weights, (y_out, dh_out, du_out, table) = refs[:6], refs[6:]
    s = pl.program_id(0)

    @pl.when(s == 0)
    def _():
        gather_table(ins, table, info[0], chunk)

    y, dh, own = slot_results(s, table, rank, *weights)
    y_out[...] = y
    dh_out[...] = dh
    du_out[...] = own[:, rank : 2 * rank]


def last_results(info, parts, tick, received, x, kept, dy, gain, w_down, w_up):
    slots, rows, feats = x.shape
    rank = w_down.shape[-1]
    chunk, width = received[0].shape
    per_slot = pl.BlockSpec((None, rows, feats), lambda s, *_: (s, 0, 0))
    return pl.pallas_call(
        functools.partial(last_results_body, parts, chunk, rank),
        grid_spec=pltpu.PrefetchScalarGridSpec(
            num_scalar_prefetch=1,
            grid=(slots,),
            in_specs=[whole((chunk, width))] * parts
            + [
                per_slot,
                pl.BlockSpec((None, None, rows, feats), lambda s, *_: (tick, s, 0, 0)),
                per_slot,
                pl.BlockSpec((None, 1, feats), lambda s, *_: (s, 0, 0)),
                pl.BlockSpec((None, feats, rank), lambda s, *_: (s, 0, 0)),
                pl.BlockSpec((None, rank, feats), lambda s, *_: (s, 0, 0)),
            ],
            out_specs=[
                per_slot,
                per_slot,
                pl.BlockSpec((None, rows, rank), lambda s, *_: (s, 0, 0)),
            ],
            scratch_shapes=[pltpu.VMEM((slots * rows, width), BF16)],
        ),
        out_shape=[
            jax.ShapeDtypeStruct((slots, rows, feats), BF16),
            jax.ShapeDtypeStruct((slots, rows, feats), BF16),
            jax.ShapeDtypeStruct((slots, rows, rank), BF16),
        ],
        compiler_params=params(),
        name="last_results",
    )(info, *received, x, kept, dy, gain, w_down, w_up)


def weight_grads(sources, ticks):
    specs, operands, layout = [], [], []
    for source in sources:
        for array in source:
            if array.ndim == 4:
                spec = pl.BlockSpec(
                    (array.shape[0], None) + array.shape[2:], lambda j: (0, j, 0, 0)
                )
            else:
                spec = pl.BlockSpec((None,) + array.shape[1:], lambda j: (j, 0, 0))
            specs.append(spec)
            operands.append(array)
    hg, dy0, act, du0, dy1, du1 = sources[0]

    def body(*refs):
        ins, (down_out, up_out) = refs[:-2], refs[-2:]
        hgs, dus, acts, dys = [], [], [], []
        for index in range(len(sources)):
            h, d0, a, l0, d1, l1 = ins[6 * index : 6 * index + 6]
            for t in range(ticks):
                hgs.append(h[t])
                acts.append(a[t])
                dus.append(l0[...] if t == 0 else l1[...])
                dys.append(d0[...] if t == 0 else d1[...])
        stack = functools.partial(jnp.concatenate, axis=0)
        down_out[...] = dot(stack(hgs), stack(dus), TN)
        up_out[...] = dot(stack(acts), stack(dys), TN)

    feats, rank = hg.shape[-1], du0.shape[-1]
    some_rank, all_feats = act.shape[-1], dy0.shape[-1]
    return pl.pallas_call(
        body,
        grid=(2,),
        in_specs=specs,
        out_specs=[
            pl.BlockSpec((None, feats, rank), lambda j: (j, 0, 0)),
            pl.BlockSpec((None, some_rank, all_feats), lambda j: (j, 0, 0)),
        ],
        out_shape=[
            jax.ShapeDtypeStruct((2, feats, rank), F32),
            jax.ShapeDtypeStruct((2, some_rank, all_feats), F32),
        ],
        compiler_params=params(),
        name="weight_grads",
    )(*operands)


def share(array, axis, count, index):
    size = array.shape[axis] // count
    return lax.dynamic_slice_in_dim(array, index * size, size, axis=axis)


def packed(arrays, width):
    pieces = []
    for array in arrays:
        for start in range(0, array.shape[-1], width):
            piece = lax.slice_in_dim(array, start, start + width, axis=array.ndim - 1)
            pieces.append(piece.reshape(-1, width))
    return jnp.concatenate(pieces, axis=0)


def unpacked(value, shapes):
    width = value.shape[-1]
    out, start = [], 0
    for shape in shapes:
        count, pieces = math.prod(shape[:-1]), []
        for _ in range(shape[-1] // width):
            pieces.append(value[start : start + count].reshape(shape[:-1] + (width,)))
            start += count
        out.append(pieces[0] if len(pieces) == 1 else jnp.concatenate(pieces, axis=-1))
    return out


def per_device(w_down, w_up, gains, entry, kept, upstream, fresh, arriving):
    holders, parts, groups = (lax.axis_size(a) for a in ("pipe", "tensor", "dp"))
    position = lax.axis_index("pipe")
    place = lax.axis_index("tensor")
    group = lax.axis_index("dp")
    w_down, w_up, gains = w_down[0], w_up[0], gains[0]
    x, kept, dy = entry[0], kept[:, 0], upstream[0]
    slots, rows, feats = x.shape
    ticks = kept.shape[0]
    rank = w_down.shape[-1]
    gain = gains[:, None, :]
    odd = position % 2
    edge = jnp.logical_or(position == 0, position == holders - 1)
    info = jnp.stack([place, odd, edge]).astype(jnp.int32)

    def around(arrays):
        return [arrays[0]] + [
            lax.ppermute(arrays[k], "tensor", [(i, i ^ k) for i in range(parts)])
            for k in range(1, parts)
        ]

    def relayed(near, far):
        out = []
        for k in range(1, groups):
            out.append(lax.ppermute(near(k), "dp", [(i, i ^ k) for i in range(groups)]))
        for k in range(groups):
            pairs = [
                (d * groups + i, (holders - 1 - d) * groups + (i ^ k))
                for d in range(holders)
                for i in range(groups)
            ]
            out.append(lax.ppermute(far(k), ("pipe", "dp"), pairs))
        return out

    dealt = first_partials(info, parts, x, kept, dy, gain, w_down, w_up)
    received = around(dealt)
    message, held = first_latents(parts, ticks, rank, received)
    received = around([message] * parts)
    first, second, du0, actives = middle_results(
        info, parts, ticks, received, x, kept, dy, gain, w_down, w_up
    )

    wide = feats // groups
    scaled = (kept.astype(F32) * gain[None]).astype(BF16)

    def early(lo):
        return lambda k: packed(
            [share(scaled[:, lo : lo + 2], 3, groups, group ^ k), dy[lo : lo + 2]], wide
        )

    early_in = relayed(early(0), early(2))

    swap = [(i, i ^ 1) for i in range(holders)]
    cross = [p for i in range(1, holders - 1, 2) for p in ((i, i + 1), (i + 1, i))]
    from_first = lax.ppermute(first, "pipe", swap)
    from_second = lax.ppermute(second, "pipe", cross) if cross else second
    *dealt, x1, g1 = later_partials(
        info, parts, from_first, from_second, second, fresh[0], arriving[0], gain, w_down, w_up
    )

    some = rank // groups

    def middle(lo):
        return lambda k: packed(
            [
                share(actives[:, lo : lo + 2], 3, groups, group ^ k),
                du0[lo : lo + 2],
                g1[lo : lo + 2],
            ],
            some,
        )

    received = around(dealt)
    middle_in = relayed(middle(0), middle(2))
    message = later_latents(parts, rank, received, held)
    received = around([message] * parts)
    y, dh, du1 = last_results(
        info, parts, ticks - 1, received, x1, kept, g1, gain, w_down, w_up
    )
    late_in = relayed(lambda k: du1[:2], lambda k: du1[2:])

    sources = [
        (
            share(scaled[:, :2], 3, groups, group),
            dy[:2],
            share(actives[:, :2], 3, groups, group),
            du0[:2],
            g1[:2],
            du1[:2],
        )
    ]
    for e, m, l in zip(early_in, middle_in, late_in):
        hg, dy0 = unpacked(e, [(ticks, 2, rows, wide), (2, rows, feats)])
        act, first_du, dy1 = unpacked(
            m, [(ticks, 2, rows, some), (2, rows, rank), (2, rows, feats)]
        )
        sources.append((hg, dy0, act, first_du, dy1, l))
    grad_down, grad_up = weight_grads(sources, ticks)
    return y[None], dh[None], grad_down[None], grad_up[None]


def solution(mesh):
    return jax.shard_map(
        per_device,
        mesh=mesh,
        in_specs=(
            P("pipe", None, "tensor", None),
            P("pipe", None, None, "tensor"),
            P("pipe", None, "tensor"),
            P("pipe", None, "dp", "tensor"),
            P(None, "pipe", None, "dp", "tensor"),
            P("pipe", None, "dp", "tensor"),
            P(None, None, "dp", "tensor"),
            P(None, None, "dp", "tensor"),
        ),
        out_specs=(
            P("pipe", None, "dp", "tensor"),
            P("pipe", None, "dp", "tensor"),
            P("pipe", None, ("tensor", "dp"), None),
            P("pipe", None, "dp", "tensor"),
        ),
        check_vma=False,
    )
```

time: 259 us -> 81.3 us (0.31)
  waiting for transfers between devices: 157 us -> 11.9 us
  matrix products: 25.9 us -> 0 us
  blocking collectives: 24 us -> 0 us
  starting transfers between devices: 6.2 us -> 28.8 us
  Pallas kernels: 0 us -> 21.4 us
  between operations: 14.2 us -> 1.29 us
  other arithmetic: 13 us -> 2.1 us
  local copies, waits for them, and re-layouts: 17.7 us -> 14.7 us
    reduce_scatter x2 -> x0, waiting for transfers between devices: 70.4 us -> none  [the longest x1 38.1 us: per_device(): lax.psum_scatter(grad_up.astype(jnp.bfloat16), 'dp', scatter_dimension=1,...]
    psum x2 -> x0, waiting for transfers between devices: 57.8 us -> none  [per_device(): lax.psum(part_latent.astype(jnp.bfloat16), 'tensor').astype(jnp.float32)]
    dot_general x12 -> x0, matrix products: 25.9 us -> none  [the longest x2 8.19 us: per_device(): jnp.einsum('snd,snr->sdr', scaled[1], latent_step, preferred_element_type...]
    psum x2 -> x0, blocking collectives: 24 us -> none  [per_device(): lax.psum(part_squares.astype(jnp.bfloat16), 'tensor').astype(jnp.float32)]
    ppermute x4 -> x23, starting transfers between devices: 6.04 us -> 28.8 us  [the longest x12 18.9 us: around(): lax.ppermute(arrays[k], 'tensor', [(i, i ^ k) for i in range(parts)])]
    pallas_call x0 -> x7, Pallas kernels: none -> 21.4 us  [the longest x1 4.9 us: last_results(): pl.pallas_call(functools.partial(last_results_body, parts, chunk, rank),...]
    ppermute x4 -> x23, waiting for transfers between devices: 29.1 us -> 11.9 us  [the longest x12 8.58 us: around(): lax.ppermute(arrays[k], 'tensor', [(i, i ^ k) for i in range(parts)])]
    convert_element_type x6 -> x1, other arithmetic: 4.57 us -> 0.11 us  [per_device(): scaled = (kept.astype(F32) * gain[None]).astype(BF16)]
  transfers between devices with their start and end apart: 8 -> 23, of which waited for: 6 -> 9; matrix products, arithmetic and copies ran while one was open for 5% -> 11% of each run, Pallas kernels for 0% -> 13%
where the time goes in v1:
time: 81.3 us; the launch traced here: 80.1 us
  starting transfers between devices  28.8 us (35%)
  Pallas kernels  21.4 us (26%)
  local copies, waits for them, and re-layouts  14.7 us (18%)
  waiting for transfers between devices  11.9 us (15%)
  other arithmetic  2.1 us (3%)
  between operations  1.29 us (2%)
    ppermute x12, starting transfers between devices, around(): lax.ppermute(arrays[k], 'tensor', [(i, i ^ k) for i in range(parts)])  18.9 us
    ppermute x12, waiting for transfers between devices, around(): lax.ppermute(arrays[k], 'tensor', [(i, i ^ k) for i in range(parts)])  8.58 us
    unnamed x75, local copies, waits for them, and re-layouts  7.26 us
    ppermute x6, starting transfers between devices, relayed(): out.append(lax.ppermute(far(k), ('pipe', 'dp'), pairs))  7.08 us
    pallas_call x1, Pallas kernels, last_results(): pl.pallas_call(functools.partial(last_results_body, parts, chunk, rank),...  4.9 us
    pallas_call x1, Pallas kernels, first_partials(): pl.pallas_call(functools.partial(first_partials_body, parts, chunk), grid...  4.74 us
    pallas_call x1, Pallas kernels, middle_results(): pl.pallas_call(functools.partial(middle_results_body, parts, chunk, rank)...  4.17 us
    pallas_call x1, Pallas kernels, later_partials(): pl.pallas_call(functools.partial(later_partials_body, parts, chunk), grid...  4.09 us
  transfers between devices with their start and end apart: 23, of which 9 were waited for; matrix products, arithmetic and copies ran while one was open for 11% of the time, Pallas kernels for 13%

profile of v1, /device:TPU:0, one launch (start us, length us, event | category | flops | bytes accessed | tf_op | source)
XLA Modules:
  0.0 80.1 jit_solution(11001328327159663588)
XLA Ops:
  1.5 1.7 %copy-done = bf16[1,4,1280,256]{3,2,1,0:T(8,128)(2,1)S(1)} copy-done((bf16[1,4,1280,256]{3,2,1,0:T(8,128)(2,1)S(1)}, bf16[1,4,1280,256]{3,2,1,0:T(8,128)(2,1)}, u32[]{:S(2)}) %copy-start) | copy-done | bytes 2621464
  3.2 1.1 %copy-done.2 = bf16[2,1,4,32,1280]{4,3,2,1,0:T(8,128)(2,1)S(1)} copy-done((bf16[2,1,4,32,1280]{4,3,2,1,0:T(8,128)(2,1)S(1)}, bf16[2,1,4,32,1280]{4,3,2,1,0:T(8,128)(2,1)}, u32[]{:S(2)}) %copy-start.2) | copy-done | bytes 655384
  4.3 1.0 %copy-done.4 = bf16[1,4,32,1280]{3,2,1,0:T(8,128)(2,1)S(1)} copy-done((bf16[1,4,32,1280]{3,2,1,0:T(8,128)(2,1)S(1)}, bf16[1,4,32,1280]{3,2,1,0:T(8,128)(2,1)}, u32[]{:S(2)}) %copy-start.4) | copy-done | bytes 327704
  5.3 1.0 %copy-done.7 = bf16[1,4,32,1280]{3,2,1,0:T(8,128)(2,1)S(1)} copy-done((bf16[1,4,32,1280]{3,2,1,0:T(8,128)(2,1)S(1)}, bf16[1,4,32,1280]{3,2,1,0:T(8,128)(2,1)}, u32[]{:S(2)}) %copy-start.7) | copy-done | bytes 327704
  6.3 4.7 %first_partials.1 = (bf16[32,1152]{1,0:T(8,128)(2,1)S(1)}, bf16[32,1152]{1,0:T(8,128)(2,1)}, bf16[32,1152]{1,0:T(8,128)(2,1)}, bf16[32,1152]{1,0:T(8,128)(2,1)}) custom-call(s32[3]{0:T(128)S(1)} %pad_add_fusion.info, bf16[4,32,1280]{2,1,0:T(8,128)(2,1)S(1)} %bitcast.111, bf16[2,4,32,1280]{3,2,1,0:T(8,128)(2,1)S(1)} %bitcast.106, ...), custom_call_target="tpu_custom_call" | custom-call | tf_op jit(solution)/shard_map/first_partials/pallas_call | solution.py:81
  11.0 3.0 %collective-permute-start = (bf16[32,1152]{1,0:T(8,128)(2,1)}, bf16[32,1152]{1,0:T(8,128)(2,1)}, u32[]{:S(2)}, u32[]{:S(2)}) collective-permute-start(bf16[32,1152]{1,0:T(8,128)(2,1)} %get-tuple-element.26), channel_id=1, source_target_pairs={{0,2},{2,0},{4,6},{6,4},{1,3},{3,1},{5,7},{7,5},{8,10},{10,8},{12,... | collective-permute-start | bytes 221192 | tf_op jit(solution)/shard_map/ppermute | solution.py:470
  14.0 2.6 %collective-permute-start.1 = (bf16[32,1152]{1,0:T(8,128)(2,1)}, bf16[32,1152]{1,0:T(8,128)(2,1)}, u32[]{:S(2)}, u32[]{:S(2)}) collective-permute-start(bf16[32,1152]{1,0:T(8,128)(2,1)} %get-tuple-element.27), channel_id=1, source_target_pairs={{0,4},{2,6},{4,0},{6,2},{1,5},{3,7},{5,1},{7,3},{8,12},{10,14},{12... | collective-permute-start | bytes 221192 | tf_op jit(solution)/shard_map/ppermute | solution.py:470
  19.2 1.3 %collective-permute-start.20 = (bf16[256,640]{1,0:T(8,128)(2,1)}, bf16[256,640]{1,0:T(8,128)(2,1)}, u32[]{:S(2)}, u32[]{:S(2)}) collective-permute-start(bf16[256,640]{1,0:T(8,128)(2,1)} %get-tuple-element.115), channel_id=1, source_target_pairs={{0,25},{1,24},{8,17},{9,16},{16,9},{17,8},{24,1},{25,0},{2,27},{3,... | collective-permute-start | bytes 983048 | tf_op jit(solution)/shard_map/ppermute | solution.py:484
  20.5 1.6 %collective-permute-start.17 = (bf16[256,640]{1,0:T(8,128)(2,1)}, bf16[256,640]{1,0:T(8,128)(2,1)}, u32[]{:S(2)}, u32[]{:S(2)}) collective-permute-start(bf16[256,640]{1,0:T(8,128)(2,1)} %get-tuple-element.116), channel_id=1, source_target_pairs={{0,24},{1,25},{8,16},{9,17},{16,8},{17,9},{24,0},{25,1},{2,26},{3,... | collective-permute-start | bytes 983048 | tf_op jit(solution)/shard_map/ppermute | solution.py:484
  22.1 1.0 %constant_dynamic-slice_fusion.5 = (bf16[2,2,32,640]{3,2,1,0:T(8,128)(2,1)S(1)}, bf16[2,2,32,640]{3,2,1,0:T(8,128)(2,1)S(1)}) fusion(bf16[2,2,32,1280]{3,2,1,0:T(8,128)(2,1)} %get-tuple-element.47, s32[]{:T(128)S(6)} %select_n.26, s32[]{:T(128)S(6)} %select_n.24), kind=kLoop, calls=%fused_computation.88 | loop fusion | bytes 655368 | tf_op jit(solution)/shard_map/dynamic_slice | solution.py:429
  23.2 1.2 %first_latents.1 = (bf16[32,1152]{1,0:T(8,128)(2,1)S(1)}, f32[32,384]{1,0:T(8,128)S(1)}) custom-call(bf16[32,1152]{1,0:T(8,128)(2,1)S(1)} %get-tuple-element.25.refs_0_, bf16[32,1152]{1,0:T(8,128)(2,1)} %collective-permute-done.refs_1_, bf16[32,1152]{1,0:T(8,128)(2,1)} %collective-permute-done.1.refs_2_, bf16[32,1152]{1,0:T(8,128)(2,1)} %collective-permute-done.2.refs_3_), custom_call_target="tpu_custom_call" | custom-call | tf_op jit(solution)/shard_map/first_latents/pallas_call | solution.py:149
  24.4 3.6 %collective-permute-start.5 = (bf16[32,1152]{1,0:T(8,128)(2,1)S(1)}, bf16[32,1152]{1,0:T(8,128)(2,1)S(1)}, u32[]{:S(2)}, u32[]{:S(2)}) collective-permute-start(bf16[32,1152]{1,0:T(8,128)(2,1)S(1)} %get-tuple-element.29.refs_0_), channel_id=1, source_target_pairs={{0,6},{2,4},{4,2},{6,0},{1,7},{3,5},{5,3},{7,1},{8,14},{10,12},{12... | collective-permute-start | bytes 221192 | tf_op jit(solution)/shard_map/ppermute | solution.py:470
  29.8 1.5 %collective-permute-done.5.refs_3_ = bf16[32,1152]{1,0:T(8,128)(2,1)S(1)} collective-permute-done((bf16[32,1152]{1,0:T(8,128)(2,1)S(1)}, bf16[32,1152]{1,0:T(8,128)(2,1)S(1)}, u32[]{:S(2)}, u32[]{:S(2)}) %collective-permute-start.5) | collective-permute-done | bytes 73760 | tf_op jit(solution)/shard_map/ppermute | solution.py:470
  32.2 1.9 %collective-permute-done.4.refs_2_ = bf16[32,1152]{1,0:T(8,128)(2,1)S(1)} collective-permute-done((bf16[32,1152]{1,0:T(8,128)(2,1)S(1)}, bf16[32,1152]{1,0:T(8,128)(2,1)S(1)}, u32[]{:S(2)}, u32[]{:S(2)}) %collective-permute-start.4) | collective-permute-done | bytes 73760 | tf_op jit(solution)/shard_map/ppermute | solution.py:470
  35.0 1.0 %copy-done.8 = bf16[1,4,32,1280]{3,2,1,0:T(8,128)(2,1)S(1)} copy-done((bf16[1,4,32,1280]{3,2,1,0:T(8,128)(2,1)S(1)}, bf16[1,4,32,1280]{3,2,1,0:T(8,128)(2,1)}, u32[]{:S(2)}) %copy-start.8) | copy-done | bytes 327704
  36.0 4.2 %middle_results.1 = (bf16[4,32,1280]{2,1,0:T(8,128)(2,1)S(1)}, bf16[4,32,1280]{2,1,0:T(8,128)(2,1)S(1)}, bf16[4,32,256]{2,1,0:T(8,128)(2,1)S(1)}, bf16[2,4,32,256]{3,2,1,0:T(8,128)(2,1)S(1)}) custom-call(s32[3]{0:T(128)S(1)} %pad_add_fusion.info, bf16[32,1152]{1,0:T(8,128)(2,1)S(1)} %get-tuple-element.29.refs_0_, ...), custom_call_target="tpu_custom_call" | custom-call | tf_op jit(solution)/shard_map/middle_results/pallas_call | solution.py:233
  42.2 1.0 %fusion.3 = (bf16[64,640]{1,0:T(8,128)(2,1)S(1)}, bf16[64,640]{1,0:T(8,128)(2,1)S(1)}) fusion(bf16[256,640]{1,0:T(8,128)(2,1)} %collective-permute-done.17), kind=kLoop, calls=%fused_computation.95 | loop fusion | bytes 327680 | tf_op jit(solution)/shard_map/slice | solution.py:447
  45.2 4.1 %later_partials.1 = (bf16[32,640]{1,0:T(8,128)(2,1)S(1)}, bf16[32,640]{1,0:T(8,128)(2,1)S(1)}, bf16[32,640]{1,0:T(8,128)(2,1)S(1)}, bf16[32,640]{1,0:T(8,128)(2,...) custom-call(s32[3]{0:T(128)S(1)} %pad_add_fusion.info, ...), custom_call_target="tpu_custom_call" | custom-call | tf_op jit(solution)/shard_map/later_partials/pallas_call | solution.py:301
  49.4 1.3 %collective-permute-start.8 = (bf16[32,640]{1,0:T(8,128)(2,1)S(1)}, bf16[32,640]{1,0:T(8,128)(2,1)S(1)}, u32[]{:S(2)}, u32[]{:S(2)}) collective-permute-start(bf16[32,640]{1,0:T(8,128)(2,1)S(1)} %get-tuple-element.33), channel_id=1, source_target_pairs={{0,2},{2,0},{4,6},{6,4},{1,3},{3,1},{5,7},{7,5},{8,10},{10,8},{12,... | collective-permute-start | bytes 122888 | tf_op jit(solution)/shard_map/ppermute | solution.py:470
  50.7 1.8 %collective-permute-start.9 = (bf16[32,640]{1,0:T(8,128)(2,1)S(1)}, bf16[32,640]{1,0:T(8,128)(2,1)S(1)}, u32[]{:S(2)}, u32[]{:S(2)}) collective-permute-start(bf16[32,640]{1,0:T(8,128)(2,1)S(1)} %get-tuple-element.34), channel_id=1, source_target_pairs={{0,4},{2,6},{4,0},{6,2},{1,5},{3,7},{5,1},{7,3},{8,12},{10,14},{12... | collective-permute-start | bytes 122888 | tf_op jit(solution)/shard_map/ppermute | solution.py:470
  52.5 1.3 %collective-permute-start.10 = (bf16[32,640]{1,0:T(8,128)(2,1)S(1)}, bf16[32,640]{1,0:T(8,128)(2,1)S(1)}, u32[]{:S(2)}, u32[]{:S(2)}) collective-permute-start(bf16[32,640]{1,0:T(8,128)(2,1)S(1)} %get-tuple-element.35), channel_id=1, source_target_pairs={{0,6},{2,4},{4,2},{6,0},{1,7},{3,5},{5,3},{7,1},{8,14},{10,12},{12... | collective-permute-start | bytes 122888 | tf_op jit(solution)/shard_map/ppermute | solution.py:470
  55.0 1.0 %collective-permute-done.9.refs_2_ = bf16[32,640]{1,0:T(8,128)(2,1)S(1)} collective-permute-done((bf16[32,640]{1,0:T(8,128)(2,1)S(1)}, bf16[32,640]{1,0:T(8,128)(2,1)S(1)}, u32[]{:S(2)}, u32[]{:S(2)}) %collective-permute-start.9) | collective-permute-done | bytes 40992 | tf_op jit(solution)/shard_map/ppermute | solution.py:470
  56.0 2.5 %collective-permute-done.10.refs_3_ = bf16[32,640]{1,0:T(8,128)(2,1)S(1)} collective-permute-done((bf16[32,640]{1,0:T(8,128)(2,1)S(1)}, bf16[32,640]{1,0:T(8,128)(2,1)S(1)}, u32[]{:S(2)}, u32[]{:S(2)}) %collective-permute-start.10) | collective-permute-done | bytes 40992 | tf_op jit(solution)/shard_map/ppermute | solution.py:470
  58.7 1.6 %collective-permute-start.13 = (bf16[32,640]{1,0:T(8,128)(2,1)S(1)}, bf16[32,640]{1,0:T(8,128)(2,1)S(1)}, u32[]{:S(2)}, u32[]{:S(2)}) collective-permute-start(bf16[32,640]{1,0:T(8,128)(2,1)S(1)} %later_latents.1.refs_0_), channel_id=1, source_target_pairs={{0,6},{2,4},{4,2},{6,0},{1,7},{3,5},{5,3},{7,1},{8,14},{10,12},{12... | collective-permute-start | bytes 122888 | tf_op jit(solution)/shard_map/ppermute | solution.py:470
  60.4 2.8 %collective-permute-start.11 = (bf16[32,640]{1,0:T(8,128)(2,1)S(1)}, bf16[32,640]{1,0:T(8,128)(2,1)S(1)}, u32[]{:S(2)}, u32[]{:S(2)}) collective-permute-start(bf16[32,640]{1,0:T(8,128)(2,1)S(1)} %later_latents.1.refs_0_), channel_id=1, source_target_pairs={{0,2},{2,0},{4,6},{6,4},{1,3},{3,1},{5,7},{7,5},{8,10},{10,8},{12,... | collective-permute-start | bytes 122888 | tf_op jit(solution)/shard_map/ppermute | solution.py:470
  63.2 1.3 %collective-permute-done.13.refs_3_ = bf16[32,640]{1,0:T(8,128)(2,1)S(1)} collective-permute-done((bf16[32,640]{1,0:T(8,128)(2,1)S(1)}, bf16[32,640]{1,0:T(8,128)(2,1)S(1)}, u32[]{:S(2)}, u32[]{:S(2)}) %collective-permute-start.13) | collective-permute-done | bytes 40992 | tf_op jit(solution)/shard_map/ppermute | solution.py:470
  64.5 1.2 %collective-permute-start.18 = (bf16[896,128]{1,0:T(8,128)(2,1)S(1)}, bf16[896,128]{1,0:T(8,128)(2,1)S(1)}, u32[]{:S(2)}, u32[]{:S(2)}) collective-permute-start(bf16[896,128]{1,0:T(8,128)(2,1)S(1)} %get-tuple-element.134), channel_id=1, source_target_pairs={{0,24},{1,25},{8,16},{9,17},{16,8},{17,9},{24,0},{25,1},{2,26},{3,... | collective-permute-start | bytes 688136 | tf_op jit(solution)/shard_map/ppermute | solution.py:484
  66.0 4.9 %last_results.1 = (bf16[4,32,1280]{2,1,0:T(8,128)(2,1)}, bf16[4,32,1280]{2,1,0:T(8,128)(2,1)}, bf16[4,32,256]{2,1,0:T(8,128)(2,1)S(1)}) custom-call(s32[3]{0:T(128)S(1)} %pad_add_fusion.info, bf16[32,640]{1,0:T(8,128)(2,1)S(1)} %later_latents.1.refs_0_, bf16[32,640]{1,0:T(8,128)(2,1)S(1)} %collective-permute-done.11.refs_1_, ...), custom_call_target="tpu_custom_call" | custom-call | tf_op jit(solution)/shard_map/last_results/pallas_call | solution.py:349
  70.9 1.2 %collective-permute-start.22 = (bf16[2,32,256]{2,1,0:T(8,128)(2,1)S(1)}, bf16[2,32,256]{2,1,0:T(8,128)(2,1)S(1)}, u32[]{:S(2)}, u32[]{:S(2)}) collective-permute-start(bf16[2,32,256]{2,1,0:T(8,128)(2,1)S(1)} %get-tuple-element.125), channel_id=1, source_target_pairs={{0,25},{1,24},{8,17},{9,16},{16,9},{17,8},{24,1},{25,0},{2,27},{3,... | collective-permute-start | bytes 98312 | tf_op jit(solution)/shard_map/ppermute | solution.py:484
  72.1 1.8 %collective-permute-start.19 = (bf16[2,32,256]{2,1,0:T(8,128)(2,1)S(1)}, bf16[2,32,256]{2,1,0:T(8,128)(2,1)S(1)}, u32[]{:S(2)}, u32[]{:S(2)}) collective-permute-start(bf16[2,32,256]{2,1,0:T(8,128)(2,1)S(1)} %get-tuple-element.125), channel_id=1, source_target_pairs={{0,24},{1,25},{8,16},{9,17},{16,8},{17,9},{24,0},{25,1},{2,26},{3,... | collective-permute-start | bytes 98312 | tf_op jit(solution)/shard_map/ppermute | solution.py:484
  74.3 2.9 %collective-permute-done.18 = bf16[896,128]{1,0:T(8,128)(2,1)S(1)} collective-permute-done((bf16[896,128]{1,0:T(8,128)(2,1)S(1)}, bf16[896,128]{1,0:T(8,128)(2,1)S(1)}, u32[]{:S(2)}, u32[]{:S(2)}) %collective-permute-start.18) | collective-permute-done | bytes 229408 | tf_op jit(solution)/shard_map/ppermute | solution.py:484
  78.1 2.0 %weight_grads.1 = (f32[2,640,256]{2,1,0:T(8,128)}, f32[2,128,1280]{2,1,0:T(8,128)}) custom-call(bf16[2,2,32,640]{3,2,1,0:T(8,128)(2,1)S(1)} %get-tuple-element.78.refs_0_, bf16[2,32,1280]{2,1,0:T(8,128)(2,1)S(1)} %get-tuple-element.74.refs_1_, bf16[2,2,32,128]{3,2,1,0:T(8,128)(2,1)S(1)} %get-tuple-element.132.refs_2_, ...), custom_call_target="tpu_custom_call" | custom-call | tf_op jit(solution)/shard_map/weight_grads/pallas_call | solution.py:410
  (138 shorter events, 13.7 us)
Async XLA Ops:
  1.5 1.7 %copy-start = (bf16[1,4,1280,256]{3,2,1,0:T(8,128)(2,1)S(1)}, bf16[1,4,1280,256]{3,2,1,0:T(8,128)(2,1)}, u32[]{:S(2)}) copy-start(bf16[1,4,1280,256]{3,2,1,0:T(8,128)(2,1)} %param.8) | copy-start | bytes 7864324
  3.2 1.1 %copy-start.2 = (bf16[2,1,4,32,1280]{4,3,2,1,0:T(8,128)(2,1)S(1)}, bf16[2,1,4,32,1280]{4,3,2,1,0:T(8,128)(2,1)}, u32[]{:S(2)}) copy-start(bf16[2,1,4,32,1280]{4,3,2,1,0:T(8,128)(2,1)} %param.12) | copy-start | bytes 1966084
  6.3 10.4 %copy-start.5 = (bf16[1,4,32,1280]{3,2,1,0:T(8,128)(2,1)S(1)}, bf16[1,4,32,1280]{3,2,1,0:T(8,128)(2,1)}, u32[]{:S(2)}) copy-start(bf16[1,4,32,1280]{3,2,1,0:T(8,128)(2,1)} %param.13) | copy-start | bytes 983044
  6.3 10.4 %copy-start.3 = (bf16[2,1,4,32,1280]{4,3,2,1,0:T(8,128)(2,1)S(1)}, bf16[2,1,4,32,1280]{4,3,2,1,0:T(8,128)(2,1)}, u32[]{:S(2)}) copy-start(bf16[2,1,4,32,1280]{4,3,2,1,0:T(8,128)(2,1)} %param.12) | copy-start | bytes 1966084
  6.3 10.4 %copy-start.11 = (f32[1,4,1280]{2,1,0:T(4,128)S(1)}, f32[1,4,1280]{2,1,0:T(4,128)}, u32[]{:S(2)}) copy-start(f32[1,4,1280]{2,1,0:T(4,128)} %param.10) | copy-start | bytes 61444
  11.0 12.1 %collective-permute-start = (bf16[32,1152]{1,0:T(8,128)(2,1)}, bf16[32,1152]{1,0:T(8,128)(2,1)}, u32[]{:S(2)}, u32[]{:S(2)}) collective-permute-start(bf16[32,1152]{1,0:T(8,128)(2,1)} %get-tuple-element.26), channel_id=1, source_target_pairs={{0,2},{2,0},{4,6},{6,4},{1,3},{3,1},{5,7},{7,5},{8,10},{10,8},{12,... | collective-permute-start | bytes 221192 | tf_op jit(solution)/shard_map/ppermute | solution.py:470
  14.0 9.1 %collective-permute-start.1 = (bf16[32,1152]{1,0:T(8,128)(2,1)}, bf16[32,1152]{1,0:T(8,128)(2,1)}, u32[]{:S(2)}, u32[]{:S(2)}) collective-permute-start(bf16[32,1152]{1,0:T(8,128)(2,1)} %get-tuple-element.27), channel_id=1, source_target_pairs={{0,4},{2,6},{4,0},{6,2},{1,5},{3,7},{5,1},{7,3},{8,12},{10,14},{12... | collective-permute-start | bytes 221192 | tf_op jit(solution)/shard_map/ppermute | solution.py:470
  16.6 6.6 %collective-permute-start.2 = (bf16[32,1152]{1,0:T(8,128)(2,1)}, bf16[32,1152]{1,0:T(8,128)(2,1)}, u32[]{:S(2)}, u32[]{:S(2)}) collective-permute-start(bf16[32,1152]{1,0:T(8,128)(2,1)} %get-tuple-element.28), channel_id=1, source_target_pairs={{0,6},{2,4},{4,2},{6,0},{1,7},{3,5},{5,3},{7,1},{8,14},{10,12},{12... | collective-permute-start | bytes 221192 | tf_op jit(solution)/shard_map/ppermute | solution.py:470
  18.3 15.8 %copy-start.1 = (bf16[1,4,1280,256]{3,2,1,0:T(8,128)(2,1)S(1)}, bf16[1,4,1280,256]{3,2,1,0:T(8,128)(2,1)}, u32[]{:S(2)}) copy-start(bf16[1,4,1280,256]{3,2,1,0:T(8,128)(2,1)} %param.8) | copy-start | bytes 7864324
  19.2 22.0 %collective-permute-start.20 = (bf16[256,640]{1,0:T(8,128)(2,1)}, bf16[256,640]{1,0:T(8,128)(2,1)}, u32[]{:S(2)}, u32[]{:S(2)}) collective-permute-start(bf16[256,640]{1,0:T(8,128)(2,1)} %get-tuple-element.115), channel_id=1, source_target_pairs={{0,25},{1,24},{8,17},{9,16},{16,9},{17,8},{24,1},{25,0},{2,27},{3,... | collective-permute-start | bytes 983048 | tf_op jit(solution)/shard_map/ppermute | solution.py:484
  20.5 21.7 %collective-permute-start.17 = (bf16[256,640]{1,0:T(8,128)(2,1)}, bf16[256,640]{1,0:T(8,128)(2,1)}, u32[]{:S(2)}, u32[]{:S(2)}) collective-permute-start(bf16[256,640]{1,0:T(8,128)(2,1)} %get-tuple-element.116), channel_id=1, source_target_pairs={{0,24},{1,25},{8,16},{9,17},{16,8},{17,9},{24,0},{25,1},{2,26},{3,... | collective-permute-start | bytes 983048 | tf_op jit(solution)/shard_map/ppermute | solution.py:484
  24.4 6.9 %collective-permute-start.5 = (bf16[32,1152]{1,0:T(8,128)(2,1)S(1)}, bf16[32,1152]{1,0:T(8,128)(2,1)S(1)}, u32[]{:S(2)}, u32[]{:S(2)}) collective-permute-start(bf16[32,1152]{1,0:T(8,128)(2,1)S(1)} %get-tuple-element.29.refs_0_), channel_id=1, source_target_pairs={{0,6},{2,4},{4,2},{6,0},{1,7},{3,5},{5,3},{7,1},{8,14},{10,12},{12... | collective-permute-start | bytes 221192 | tf_op jit(solution)/shard_map/ppermute | solution.py:470
  28.0 6.1 %collective-permute-start.4 = (bf16[32,1152]{1,0:T(8,128)(2,1)S(1)}, bf16[32,1152]{1,0:T(8,128)(2,1)S(1)}, u32[]{:S(2)}, u32[]{:S(2)}) collective-permute-start(bf16[32,1152]{1,0:T(8,128)(2,1)S(1)} %get-tuple-element.29.refs_0_), channel_id=1, source_target_pairs={{0,4},{2,6},{4,0},{6,2},{1,5},{3,7},{5,1},{7,3},{8,12},{10,14},{12... | collective-permute-start | bytes 221192 | tf_op jit(solution)/shard_map/ppermute | solution.py:470
  28.0 6.1 %collective-permute-start.3 = (bf16[32,1152]{1,0:T(8,128)(2,1)S(1)}, bf16[32,1152]{1,0:T(8,128)(2,1)S(1)}, u32[]{:S(2)}, u32[]{:S(2)}) collective-permute-start(bf16[32,1152]{1,0:T(8,128)(2,1)S(1)} %get-tuple-element.29.refs_0_), channel_id=1, source_target_pairs={{0,2},{2,0},{4,6},{6,4},{1,3},{3,1},{5,7},{7,5},{8,10},{10,8},{12,... | collective-permute-start | bytes 221192 | tf_op jit(solution)/shard_map/ppermute | solution.py:470
  31.3 11.9 %collective-permute-start.14 = (bf16[256,640]{1,0:T(8,128)(2,1)S(1)}, bf16[256,640]{1,0:T(8,128)(2,1)S(1)}, u32[]{:S(2)}, u32[]{:S(2)}) collective-permute-start(bf16[256,640]{1,0:T(8,128)(2,1)S(1)} %pad_maximum_fusion.4), channel_id=1, source_target_pairs={{0,1},{1,0},{2,3},{3,2},{4,5},{5,4},{6,7},{7,6},{8,9},{9,8},{10,11... | collective-permute-start | bytes 983048 | tf_op jit(solution)/shard_map/ppermute | solution.py:477
  34.1 1.0 %copy-start.6 = (bf16[1,4,32,1280]{3,2,1,0:T(8,128)(2,1)S(1)}, bf16[1,4,32,1280]{3,2,1,0:T(8,128)(2,1)}, u32[]{:S(2)}) copy-start(bf16[1,4,32,1280]{3,2,1,0:T(8,128)(2,1)} %param.13) | copy-start | bytes 983044
  40.3 4.9 %collective-permute-start.6 = (bf16[4,32,1280]{2,1,0:T(8,128)(2,1)S(1)}, bf16[4,32,1280]{2,1,0:T(8,128)(2,1)S(1)}, u32[]{:S(2)}, u32[]{:S(2)}) collective-permute-start(bf16[4,32,1280]{2,1,0:T(8,128)(2,1)S(1)} %get-tuple-element.30), channel_id=1, source_target_pairs={{0,8},{8,0},{16,24},{24,16},{1,9},{9,1},{17,25},{25,17},{2,10},{10... | collective-permute-start | bytes 983048 | tf_op jit(solution)/shard_map/ppermute | solution.py:507
  40.4 4.8 %collective-permute-start.7 = (bf16[4,32,1280]{2,1,0:T(8,128)(2,1)S(1)}, bf16[4,32,1280]{2,1,0:T(8,128)(2,1)S(1)}, u32[]{:S(2)}, u32[]{:S(2)}) collective-permute-start(bf16[4,32,1280]{2,1,0:T(8,128)(2,1)S(1)} %get-tuple-element.31.refs_4_.refs_5_), channel_id=1, source_target_pairs={{8,16},{16,8},{9,17},{17,9},{10,18},{18,10},{11,19},{19,11},{12,20... | collective-permute-start | bytes 983048 | tf_op jit(solution)/shard_map/ppermute | solution.py:508
  42.1 3.1 %copy-start.9 = (bf16[1,2,32,1280]{3,2,1,0:T(8,128)(2,1)S(1)}, bf16[1,2,32,1280]{3,2,1,0:T(8,128)(2,1)}, u32[]{:S(2)}) copy-start(bf16[1,2,32,1280]{3,2,1,0:T(8,128)(2,1)} %param.14) | copy-start | bytes 491524
  42.1 3.1 %copy-start.10 = (bf16[1,2,32,1280]{3,2,1,0:T(8,128)(2,1)S(1)}, bf16[1,2,32,1280]{3,2,1,0:T(8,128)(2,1)}, u32[]{:S(2)}) copy-start(bf16[1,2,32,1280]{3,2,1,0:T(8,128)(2,1)} %param.15) | copy-start | bytes 491524
  49.4 5.5 %collective-permute-start.8 = (bf16[32,640]{1,0:T(8,128)(2,1)S(1)}, bf16[32,640]{1,0:T(8,128)(2,1)S(1)}, u32[]{:S(2)}, u32[]{:S(2)}) collective-permute-start(bf16[32,640]{1,0:T(8,128)(2,1)S(1)} %get-tuple-element.33), channel_id=1, source_target_pairs={{0,2},{2,0},{4,6},{6,4},{1,3},{3,1},{5,7},{7,5},{8,10},{10,8},{12,... | collective-permute-start | bytes 122888 | tf_op jit(solution)/shard_map/ppermute | solution.py:470
  50.7 5.3 %collective-permute-start.9 = (bf16[32,640]{1,0:T(8,128)(2,1)S(1)}, bf16[32,640]{1,0:T(8,128)(2,1)S(1)}, u32[]{:S(2)}, u32[]{:S(2)}) collective-permute-start(bf16[32,640]{1,0:T(8,128)(2,1)S(1)} %get-tuple-element.34), channel_id=1, source_target_pairs={{0,4},{2,6},{4,0},{6,2},{1,5},{3,7},{5,1},{7,3},{8,12},{10,14},{12... | collective-permute-start | bytes 122888 | tf_op jit(solution)/shard_map/ppermute | solution.py:470
  52.5 6.0 %collective-permute-start.10 = (bf16[32,640]{1,0:T(8,128)(2,1)S(1)}, bf16[32,640]{1,0:T(8,128)(2,1)S(1)}, u32[]{:S(2)}, u32[]{:S(2)}) collective-permute-start(bf16[32,640]{1,0:T(8,128)(2,1)S(1)} %get-tuple-element.35), channel_id=1, source_target_pairs={{0,6},{2,4},{4,2},{6,0},{1,7},{3,5},{5,3},{7,1},{8,14},{10,12},{12... | collective-permute-start | bytes 122888 | tf_op jit(solution)/shard_map/ppermute | solution.py:470
  54.0 19.9 %collective-permute-start.15 = (bf16[896,128]{1,0:T(8,128)(2,1)S(1)}, bf16[896,128]{1,0:T(8,128)(2,1)S(1)}, u32[]{:S(2)}, u32[]{:S(2)}) collective-permute-start(bf16[896,128]{1,0:T(8,128)(2,1)S(1)} %constant_dynamic-update-slice_fusion), channel_id=1, source_target_pairs={{0,1},{1,0},{2,3},{3,2},{4,5},{5,4},{6,7},{7,6},{8,9},{9,8},{10,11... | collective-permute-start | bytes 688136 | tf_op jit(solution)/shard_map/ppermute | solution.py:477
  58.7 5.8 %collective-permute-start.13 = (bf16[32,640]{1,0:T(8,128)(2,1)S(1)}, bf16[32,640]{1,0:T(8,128)(2,1)S(1)}, u32[]{:S(2)}, u32[]{:S(2)}) collective-permute-start(bf16[32,640]{1,0:T(8,128)(2,1)S(1)} %later_latents.1.refs_0_), channel_id=1, source_target_pairs={{0,6},{2,4},{4,2},{6,0},{1,7},{3,5},{5,3},{7,1},{8,14},{10,12},{12... | collective-permute-start | bytes 122888 | tf_op jit(solution)/shard_map/ppermute | solution.py:470
  60.4 5.3 %collective-permute-start.12 = (bf16[32,640]{1,0:T(8,128)(2,1)S(1)}, bf16[32,640]{1,0:T(8,128)(2,1)S(1)}, u32[]{:S(2)}, u32[]{:S(2)}) collective-permute-start(bf16[32,640]{1,0:T(8,128)(2,1)S(1)} %later_latents.1.refs_0_), channel_id=1, source_target_pairs={{0,4},{2,6},{4,0},{6,2},{1,5},{3,7},{5,1},{7,3},{8,12},{10,14},{12... | collective-permute-start | bytes 122888 | tf_op jit(solution)/shard_map/ppermute | solution.py:470
  60.4 5.6 %collective-permute-start.11 = (bf16[32,640]{1,0:T(8,128)(2,1)S(1)}, bf16[32,640]{1,0:T(8,128)(2,1)S(1)}, u32[]{:S(2)}, u32[]{:S(2)}) collective-permute-start(bf16[32,640]{1,0:T(8,128)(2,1)S(1)} %later_latents.1.refs_0_), channel_id=1, source_target_pairs={{0,2},{2,0},{4,6},{6,4},{1,3},{3,1},{5,7},{7,5},{8,10},{10,8},{12,... | collective-permute-start | bytes 122888 | tf_op jit(solution)/shard_map/ppermute | solution.py:470
  63.2 11.1 %collective-permute-start.21 = (bf16[896,128]{1,0:T(8,128)(2,1)S(1)}, bf16[896,128]{1,0:T(8,128)(2,1)S(1)}, u32[]{:S(2)}, u32[]{:S(2)}) collective-permute-start(bf16[896,128]{1,0:T(8,128)(2,1)S(1)} %get-tuple-element.133), channel_id=1, source_target_pairs={{0,25},{1,24},{8,17},{9,16},{16,9},{17,8},{24,1},{25,0},{2,27},{3,... | collective-permute-start | bytes 688136 | tf_op jit(solution)/shard_map/ppermute | solution.py:484
  64.5 12.7 %collective-permute-start.18 = (bf16[896,128]{1,0:T(8,128)(2,1)S(1)}, bf16[896,128]{1,0:T(8,128)(2,1)S(1)}, u32[]{:S(2)}, u32[]{:S(2)}) collective-permute-start(bf16[896,128]{1,0:T(8,128)(2,1)S(1)} %get-tuple-element.134), channel_id=1, source_target_pairs={{0,24},{1,25},{8,16},{9,17},{16,8},{17,9},{24,0},{25,1},{2,26},{3,... | collective-permute-start | bytes 688136 | tf_op jit(solution)/shard_map/ppermute | solution.py:484
  70.9 6.8 %collective-permute-start.22 = (bf16[2,32,256]{2,1,0:T(8,128)(2,1)S(1)}, bf16[2,32,256]{2,1,0:T(8,128)(2,1)S(1)}, u32[]{:S(2)}, u32[]{:S(2)}) collective-permute-start(bf16[2,32,256]{2,1,0:T(8,128)(2,1)S(1)} %get-tuple-element.125), channel_id=1, source_target_pairs={{0,25},{1,24},{8,17},{9,16},{16,9},{17,8},{24,1},{25,0},{2,27},{3,... | collective-permute-start | bytes 98312 | tf_op jit(solution)/shard_map/ppermute | solution.py:484
  72.1 5.6 %collective-permute-start.19 = (bf16[2,32,256]{2,1,0:T(8,128)(2,1)S(1)}, bf16[2,32,256]{2,1,0:T(8,128)(2,1)S(1)}, u32[]{:S(2)}, u32[]{:S(2)}) collective-permute-start(bf16[2,32,256]{2,1,0:T(8,128)(2,1)S(1)} %get-tuple-element.125), channel_id=1, source_target_pairs={{0,24},{1,25},{8,16},{9,17},{16,8},{17,9},{24,0},{25,1},{2,26},{3,... | collective-permute-start | bytes 98312 | tf_op jit(solution)/shard_map/ppermute | solution.py:484
  73.9 4.2 %collective-permute-start.16 = (bf16[2,32,256]{2,1,0:T(8,128)(2,1)S(1)}, bf16[2,32,256]{2,1,0:T(8,128)(2,1)S(1)}, u32[]{:S(2)}, u32[]{:S(2)}) collective-permute-start(bf16[2,32,256]{2,1,0:T(8,128)(2,1)S(1)} %get-tuple-element.126.refs_5_), channel_id=1, source_target_pairs={{0,1},{1,0},{2,3},{3,2},{4,5},{5,4},{6,7},{7,6},{8,9},{9,8},{10,11... | collective-permute-start | bytes 98312 | tf_op jit(solution)/shard_map/ppermute | solution.py:477
  (3 other events, 2.9 us)

commit v2 on v0

v2 whole, which is shorter than its diff:
```python
import functools

import jax
import jax.numpy as jnp
from jax import lax
from jax.experimental import pallas as pl
from jax.experimental.pallas import tpu as pltpu
from jax.sharding import PartitionSpec as P

D = 5120
EPS = 1e-06
LANES = 128
F32 = jnp.float32
BF16 = jnp.bfloat16

COSTS = {
    "first_partials": 5.0,
    "early_factors": 0.3,
    "held_weights": 0.5,
    "marker": 1.5,
    "first_latents": 0.3,
    "second_results": 0.8,
    "first_results": 0.8,
    "later_partials": 1.3,
    "middle_factors": 0.1,
    "early_share": 0.3,
    "middle_share": 0.2,
    "late_share": 0.1,
    "later_latents": 0.3,
    "late_factors": 0.2,
    "last_results": 0.7,
    "up_grads": 0.4,
    "down_grads": 1.5
}
FLOPS_PER_US = 1.1e9

NN = (((1,), (0,)), ((), ()))
NT = (((1,), (1,)), ((), ()))
TN = (((0,), (0,)), ((), ()))


def dot(a, b, dims=NN):
    return lax.dot_general(a, b, dims, preferred_element_type=F32)


def call(body, operands, outs, name, scratch=(), limit=24, after=(), raw=0):
    count = len(operands)

    def run(*refs):
        body(*refs[:count], *refs[count + len(after) :])

    return pl.pallas_call(
        run,
        in_specs=[pl.BlockSpec(memory_space=pl.ANY)] * raw
        + [pl.BlockSpec(memory_space=pltpu.VMEM)] * (count - raw)
        + [pl.BlockSpec(memory_space=pl.ANY)] * len(after),
        out_specs=[pl.BlockSpec(memory_space=pltpu.VMEM)] * len(outs),
        out_shape=[jax.ShapeDtypeStruct(shape, dtype) for shape, dtype in outs],
        scratch_shapes=list(scratch),
        compiler_params=pltpu.CompilerParams(vmem_limit_bytes=limit * 2**20),
        cost_estimate=pl.CostEstimate(
            flops=round(COSTS[name] * FLOPS_PER_US), bytes_accessed=0, transcendentals=0
        ),
        name=name,
    )(*operands, *after)


def place():
    return lax.axis_index("tensor")


def group():
    return lax.axis_index("dp")


def odd():
    return lax.rem(lax.axis_index("pipe"), 2) == 1


def even():
    return jnp.logical_not(odd())


def edge():
    position = lax.axis_index("pipe")
    return jnp.logical_or(position == 0, position == lax.axis_size("pipe") - 1)


def on_lanes(columns, rows):
    lane = lax.broadcasted_iota(jnp.int32, (rows, LANES), 1)
    out = jnp.zeros((rows, LANES), F32)
    for index, column in enumerate(columns):
        out = jnp.where(lane == index, column, out)
    return out


def squares_of(rows):
    return jnp.sum(rows * rows, axis=-1, keepdims=True)


def lane_part(value, index, count):
    size = value.shape[-1] // count
    out = value[:, :size]
    for i in range(1, count):
        out = jnp.where(index == i, value[:, i * size : (i + 1) * size], out)
    return out


def deal(table, outs):
    here, chunk = place(), outs[0].shape[0]
    for k, out in enumerate(outs):
        start = pl.multiple_of((here ^ k) * chunk, chunk)
        out[...] = table[pl.ds(start, chunk), :]


def collect(ins, table):
    here, chunk = place(), ins[0].shape[0]
    for k, ref in enumerate(ins):
        start = pl.multiple_of((here ^ k) * chunk, chunk)
        table[pl.ds(start, chunk), :] = ref[...]


def first_partials(parts, w_down, w_up, gains, entry, kept, upstream, after):
    _, slots, rows, feats = entry.shape
    ticks, rank = kept.shape[0], w_down.shape[-1]
    width = (ticks + 2) * rank + LANES

    def body(down_ref, up_ref, gain_ref, x_ref, kept_ref, dy_ref, *rest):
        outs, table = rest[:parts], rest[parts]
        for s in range(slots):
            gain = gain_ref[0, s : s + 1, :]
            here = slice(s * rows, (s + 1) * rows)
            streams = [x_ref[0, s].astype(F32)]
            streams += [kept_ref[t, 0, s].astype(F32) for t in range(ticks)]
            scaled = jnp.concatenate([(v * gain).astype(BF16) for v in streams], axis=0)
            latent = dot(scaled, down_ref[0, s]).astype(BF16)
            for i in range(ticks + 1):
                table[here, i * rank : (i + 1) * rank] = latent[i * rows : (i + 1) * rows]
            base = (ticks + 1) * rank
            table[here, base : base + rank] = dot(dy_ref[0, s], up_ref[0, s], NT).astype(BF16)
            squares = on_lanes([squares_of(v) for v in streams], rows)
            table[here, base + rank :] = squares.astype(BF16)
        deal(table, outs)

    return call(
        body,
        [w_down, w_up, gains, entry, kept, upstream],
        [((slots * rows // parts, width), BF16)] * parts,
        "first_partials",
        [pltpu.VMEM((slots * rows, width), BF16)],
        limit=62,
        after=after,
    )


def early_factors(gains, kept, upstream, own, after):
    ticks, _, slots, rows, feats = kept.shape
    half = slots // 2

    def body(gain_ref, kept_ref, dy_ref, own_ref, near, far, own_out):
        own_out[...] = own_ref[...]
        for s in range(slots):
            gain = gain_ref[0, s : s + 1, :]
            out = near if s < half else far
            for t in range(ticks):
                hg = kept_ref[t, 0, s].astype(F32) * gain
                out[s % half, :, t * feats : (t + 1) * feats] = hg.astype(BF16)
            out[s % half, :, ticks * feats :] = dy_ref[0, s]

    return call(
        body,
        [gains, kept, upstream, own],
        [((half, rows, (ticks + 1) * feats), BF16)] * 2 + [(own.shape, own.dtype)],
        "early_factors",
        after=after,
    )


def shared(name, groups, cut, near, far, after=()):
    half, rows, width = near.shape
    count = sum(size for _, size in cut)
    kept = width - count + count // groups

    def body(near_ref, far_ref, *outs):
        mine = group()
        for j in range(2 * half):
            ref = near_ref if j < half else far_ref
            for k, out in enumerate(outs):
                source, target = 0, 0
                for start, size in [*cut, (width, 0)]:
                    plain = start - source
                    if plain:
                        out[j, :, target : target + plain] = ref[j % half, :, source:start]
                    source, target = start, target + plain
                    if size:
                        run = ref[j % half, :, start : start + size].astype(F32)
                        part = lane_part(run, mine ^ k, groups).astype(BF16)
                        out[j, :, target : target + size // groups] = part
                        source, target = start + size, target + size // groups

    return call(
        body, [near, far], [((2 * half, rows, kept), BF16)] * groups, name, after=after
    )


def held_weights(w_down, w_up, after):
    def body(down_ref, up_ref, down_out, up_out, sems):
        copies = [
            pltpu.make_async_copy(down_ref, down_out, sems.at[0]),
            pltpu.make_async_copy(up_ref, up_out, sems.at[1]),
        ]
        for copy in copies:
            copy.start()
        for copy in copies:
            copy.wait()

    return call(
        body,
        [w_down, w_up],
        [(w_down.shape, w_down.dtype), (w_up.shape, w_up.dtype)],
        "held_weights",
        [pltpu.SemaphoreType.DMA((2,))],
        after=after,
        raw=2,
    )


def marker(after):
    def body(out):
        out[...] = jnp.zeros(out.shape, out.dtype)

    return call(body, [], [((8, LANES), F32)], "marker", after=after)


def total(refs):
    value = refs[0][...].astype(F32)
    for ref in refs[1:]:
        value = value + ref[...].astype(F32)
    return value


def scale_of(squares):
    return 1.0 / jnp.sqrt(squares / D + EPS)


def logistic(z):
    return 1.0 / (1.0 + jnp.exp(-z))


def latent_grads(da, u, r):
    z = u * r
    gate = logistic(z)
    dz = da * gate * (1.0 + z * (1.0 - gate))
    dss = (-0.5 / D) * r * r * r * jnp.sum(dz * u, axis=-1, keepdims=True)
    return dz * r, dss


def first_latents(ticks, rank, received, after):
    parts, chunk = len(received), received[0].shape[0]

    def body(*refs):
        ins, (out, held) = refs[:parts], refs[parts:]
        value = total(ins)
        base = (ticks + 2) * rank
        streams = []
        for i in range(ticks + 1):
            u = value[:, i * rank : (i + 1) * rank]
            streams.append((u, scale_of(value[:, base + i : base + i + 1])))
        du, dss = latent_grads(value[:, base - rank : base], *streams[1])
        active = [u * r * logistic(u * r) for u, r in streams]
        out[:, :rank] = active[0].astype(BF16)
        out[:, rank : 2 * rank] = du.astype(BF16)
        out[:, 2 * rank : 2 * rank + LANES] = on_lanes([dss], chunk).astype(BF16)
        for t in range(ticks):
            start = 2 * rank + LANES + t * rank
            out[:, start : start + rank] = active[t + 1].astype(BF16)
        u, r = streams[2]
        held[:, :rank] = u
        held[:, rank:] = on_lanes([r], chunk)

    return call(
        body,
        received,
        [((chunk, (ticks + 2) * rank + LANES), BF16), ((chunk, rank + LANES), F32)],
        "first_latents",
        after=after,
    )


def later_latents(rank, received, held, after):
    parts, chunk = len(received), received[0].shape[0]

    def body(*refs):
        ins, held, out = refs[:parts], refs[parts], refs[parts + 1]
        value = total(ins)
        z = value[:, :rank] * scale_of(value[:, 2 * rank : 2 * rank + 1])
        grads = value[:, rank : 2 * rank]
        du, dss = latent_grads(grads, held[:, :rank], held[:, rank : rank + 1])
        out[:, :rank] = (z * logistic(z)).astype(BF16)
        out[:, rank : 2 * rank] = du.astype(BF16)
        out[:, 2 * rank :] = on_lanes([dss], chunk).astype(BF16)

    outs = [((chunk, 2 * rank + LANES), BF16)]
    return call(body, [*received, held], outs, "later_latents", after=after)[0]


def slot_results(own, x, kept, dy, gain, w_down, w_up):
    rank = w_down.shape[-1]
    y = x.astype(F32) + dot(own[:, :rank], w_up)
    dss = own[:, 2 * rank : 2 * rank + 1].astype(F32)
    dh = dot(own[:, rank : 2 * rank], w_down, NT) * gain
    dh = dh + 2.0 * kept.astype(F32) * dss + dy.astype(F32)
    return y.astype(BF16), dh.astype(BF16)


def middle_results(
    name, mine, received, w_down, w_up, gains, entry, kept, upstream, factors=False, after=()
):
    parts = len(received)
    _, slots, rows, feats = entry.shape
    ticks, rank = kept.shape[0], w_down.shape[-1]
    width = received[0].shape[-1]

    def body(*refs):
        ins, refs = refs[:parts], refs[parts:]
        down_ref, up_ref, gain_ref, x_ref, kept_ref, dy_ref = refs[:6]
        out, table = refs[6], refs[-1]
        collect(ins, table)
        upward = mine()
        for i in range(slots // 2):
            outer, inner = (0, 3)[i], (1, 2)[i]
            s = jnp.where(upward, outer, inner)
            own = table[pl.ds(pl.multiple_of(s * rows, rows), rows), :rank]
            y = x_ref[0, s].astype(F32) + dot(own, up_ref[0, s])
            out[i] = y.astype(BF16)
            s = jnp.where(upward, inner, outer)
            own = table[pl.ds(pl.multiple_of(s * rows, rows), rows), rank : 2 * rank + LANES]
            dh = dot(own[:, :rank], down_ref[0, s], NT) * gain_ref[0, pl.ds(s, 1), :]
            dss = own[:, rank : rank + 1].astype(F32)
            dh = dh + 2.0 * kept_ref[0, 0, s].astype(F32) * dss + dy_ref[0, s].astype(F32)
            out[2 + i] = dh.astype(BF16)
        if factors:
            for s in range(slots):
                own = table[s * rows : (s + 1) * rows, :]
                refs[7][s, :, :rank] = own[:, rank : 2 * rank]
                refs[7][s, :, rank:] = own[:, 2 * rank + LANES :]

    outs = [((slots, rows, feats), BF16)]
    if factors:
        outs.append(((slots, rows, (ticks + 1) * rank), BF16))
    return call(
        body,
        [*received, w_down, w_up, gains, entry, kept, upstream],
        outs,
        name,
        [pltpu.VMEM((slots * rows, width), BF16)],
        after=after,
    )


def later_partials(
    parts, first, second, own, fresh, arriving, w_down, w_up, gains, after
):
    slots, rows, feats = first.shape
    rank = w_down.shape[-1]
    width = 2 * rank + LANES

    def body(*refs):
        a_ref, b_ref, own_ref, fresh_ref, arriving_ref, down_ref, up_ref, gain_ref = refs[:8]
        outs, (x_out, g_out, table) = refs[8 : 8 + parts], refs[8 + parts :]
        odd_one, at_edge = odd(), edge()
        for s in range(slots):
            i, j = s // 2, 2 + s // 2
            ends = (fresh_ref[0, i], own_ref[j]) if s % 2 == 0 else (own_ref[i], arriving_ref[0, i])
            second_x = jnp.where(at_edge, ends[0], b_ref[i])
            second_g = jnp.where(at_edge, ends[1], b_ref[j])
            outer = odd_one if s in (0, 3) else jnp.logical_not(odd_one)
            x = jnp.where(outer, a_ref[i], second_x)
            g = jnp.where(outer, second_g, a_ref[j])
            x_out[s] = x
            g_out[s] = g
            here = slice(s * rows, (s + 1) * rows)
            wide = x.astype(F32)
            scaled = (wide * gain_ref[0, s : s + 1, :]).astype(BF16)
            table[here, :rank] = dot(scaled, down_ref[0, s]).astype(BF16)
            table[here, rank : 2 * rank] = dot(g, up_ref[0, s], NT).astype(BF16)
            table[here, 2 * rank :] = on_lanes([squares_of(wide)], rows).astype(BF16)
        deal(table, outs)

    results = call(
        body,
        [first, second, own, fresh, arriving, w_down, w_up, gains],
        [((slots * rows // parts, width), BF16)] * parts
        + [((slots, rows, feats), BF16)] * 2,
        "later_partials",
        [pltpu.VMEM((slots * rows, width), BF16)],
        after=after,
    )
    return results[:parts], *results[parts:]


def middle_factors(groups, ticks, factors, g, after=()):
    slots, rows, feats = g.shape
    rank = factors.shape[-1] // (ticks + 1)
    some, half = rank // groups, slots // 2

    def body(factor_ref, g_ref, *outs):
        mine = group()
        for s in range(slots):
            for k, out in enumerate(outs[s // half * groups : (s // half + 1) * groups]):
                out[s % half, :, :feats] = g_ref[s]
                out[s % half, :, feats : feats + rank] = factor_ref[s, :, :rank]
                for t in range(ticks):
                    active = factor_ref[s, :, (t + 1) * rank : (t + 2) * rank].astype(F32)
                    part = lane_part(active, mine ^ k, groups).astype(BF16)
                    start = feats + rank + t * some
                    out[s % half, :, start : start + some] = part

    outs = call(
        body,
        [factors, g],
        [((half, rows, feats + rank + ticks * some), BF16)] * (2 * groups),
        "middle_factors",
        after=after,
    )
    return outs[:groups], outs[groups:]


def late_factors(slots, rows, rank, received, after):
    parts, (chunk, width) = len(received), received[0].shape

    def body(*refs):
        ins, (near, far, table) = refs[:parts], refs[parts:]
        here = place()
        for k, ref in enumerate(ins):
            start = pl.multiple_of((here ^ k) * chunk, chunk)
            table[pl.ds(start, chunk), :] = ref[:, rank : 2 * rank]
        for s in range(slots):
            out = near if s < slots // 2 else far
            out[s % (slots // 2)] = table[s * rows : (s + 1) * rows, :]

    return call(
        body,
        received,
        [((slots // 2, rows, rank), BF16)] * 2,
        "late_factors",
        [pltpu.VMEM((slots * rows, rank), BF16)],
        after=after,
    )


def late_share(near, far, after):
    half, rows, rank = near.shape

    def body(near_ref, far_ref, out):
        out[:half] = near_ref[...]
        out[half:] = far_ref[...]

    return call(body, [near, far], [((2 * half, rows, rank), BF16)], "late_share", after=after)[0]


def last_results(received, w_down, w_up, gains, x, kept, g):
    parts = len(received)
    slots, rows, feats = x.shape
    ticks = kept.shape[0]
    width = received[0].shape[-1]

    def body(*refs):
        ins, refs = refs[:parts], refs[parts:]
        down_ref, up_ref, gain_ref, x_ref, kept_ref, g_ref, y_out, dh_out, table = refs
        collect(ins, table)
        for s in range(slots):
            y, dh = slot_results(
                table[s * rows : (s + 1) * rows, :],
                x_ref[s],
                kept_ref[ticks - 1, 0, s],
                g_ref[s],
                gain_ref[0, s : s + 1, :],
                down_ref[0, s],
                up_ref[0, s],
            )
            y_out[0, s] = y
            dh_out[0, s] = dh

    return call(
        body,
        [*received, w_down, w_up, gains, x, kept, g],
        [((1, slots, rows, feats), BF16)] * 2,
        "last_results",
        [pltpu.VMEM((slots * rows, width), BF16)],
    )


def up_grads(groups, ticks, rank, early, mid):
    count, (slots, rows, _) = len(early), early[0].shape
    half, some = slots // 2, rank // groups
    feats = mid[0].shape[-1] - rank - ticks * some

    def body(*refs):
        early, mid, (out, token) = refs[:count], refs[count : 3 * count], refs[-2:]
        token[...] = jnp.zeros(token.shape, token.dtype)
        for j in range(half):
            act, dy = [], []
            for k, e in enumerate(early):
                for i, m in ((j, mid[k]), (half + j, mid[count + k])):
                    start = feats + rank
                    for t in range(ticks):
                        act.append(m[j, :, start + t * some : start + (t + 1) * some])
                    dy += [e[i, :, e.shape[-1] - feats :], m[j, :, :feats]]
            out[0, j] = dot(jnp.concatenate(act, axis=0), jnp.concatenate(dy, axis=0), TN)

    outs = [((1, half, some, feats), F32), ((8, LANES), F32)]
    return call(body, [*early, *mid], outs, "up_grads")


def down_grads(groups, ticks, feats, early, mid, late):
    count, (slots, rows, rank) = len(early), late[0].shape
    half, wide = slots // 2, feats // groups

    def body(*refs):
        early, mid, late = refs[:count], refs[count : 3 * count], refs[3 * count : 4 * count]
        out = refs[-1]
        for j in range(half):
            hg, du = [], []
            for k, (e, l) in enumerate(zip(early, late)):
                for i, m in ((j, mid[k]), (half + j, mid[count + k])):
                    hg += [e[i, :, t * wide : (t + 1) * wide] for t in range(ticks)]
                    du += [m[j, :, feats : feats + rank], l[i]]
            out[0, j] = dot(jnp.concatenate(hg, axis=0), jnp.concatenate(du, axis=0), TN)

    return call(
        body, [*early, *mid, *late], [((1, half, wide, rank), F32)], "down_grads"
    )[0]


def per_device(w_down, w_up, gains, entry, kept, upstream, fresh, arriving):
    holders, parts, groups = (lax.axis_size(a) for a in ("pipe", "tensor", "dp"))
    _, slots, rows, feats = entry.shape
    ticks, rank = kept.shape[0], w_down.shape[-1]

    def around(arrays):
        return [arrays[0]] + [
            lax.ppermute(arrays[k], "tensor", [(i, i ^ k) for i in range(parts)])
            for k in range(1, parts)
        ]

    def mirrored(far, k=0):
        pairs = [
            (d * groups + i, (holders - 1 - d) * groups + (i ^ k))
            for d in range(holders)
            for i in range(groups)
        ]
        return lax.ppermute(far, ("pipe", "dp"), pairs)

    def across(arrays):
        return [arrays[0]] + [
            lax.ppermute(arrays[k], "dp", [(i, i ^ k) for i in range(groups)])
            for k in range(1, groups)
        ]

    dealt = first_partials(parts, w_down, w_up, gains, entry, kept, upstream, after=[])
    received = around(dealt)

    near, far, own = early_factors(gains, kept, upstream, dealt[0], after=dealt[1:2])
    far = mirrored(far)

    weights = held_weights(w_down, w_up, after=dealt[1:2])
    message, held = first_latents(ticks, rank, [own] + received[1:], after=[near, weights[0]])
    received = around([message] * parts)

    tick = (received, *weights, gains, entry, kept, upstream)
    (second,) = middle_results("second_results", odd, *tick)
    swap = [(i, i ^ 1) for i in range(holders)]
    cross = []
    for d in range(holders):
        to = d if d in (0, holders - 1) else d + 1 if d % 2 else d - 1
        for i in range(parts):
            peer = i if to != d else i ^ (parts > 1)
            cross.append((d * parts + i, to * parts + peer))
    from_second = lax.ppermute(second, ("pipe", "tensor"), cross)
    first, factors = middle_results(
        "first_results", even, *tick, factors=True, after=[second] + []
    )
    from_first = lax.ppermute(first, "pipe", swap)

    early = across(
        shared("early_share", groups, [(t * feats, feats) for t in range(ticks)], near, far, [])
    )
    ready = marker(early[1:])

    dealt, x, g = later_partials(
        parts, from_first, from_second, second, fresh, arriving, *weights, gains, after=[]
    )
    received = around(dealt)
    near, far = middle_factors(groups, ticks, factors, g, after=[])
    mid = across(near) + [mirrored(far[k], k) for k in range(groups)]
    message = later_latents(rank, received, held, after=ready)
    received = around([message] * parts)
    grad_up, token = up_grads(groups, ticks, rank, early, mid)
    near, far = late_factors(slots, rows, rank, received, after=[])
    late = across([late_share(near, mirrored(far), after=[token])] * groups)
    y, dh = last_results(received, *weights, gains, x, kept, g)
    grad_down = down_grads(groups, ticks, feats, early, mid, late)
    return y, dh, grad_down, grad_up


def solution(mesh):
    return jax.shard_map(
        per_device,
        mesh=mesh,
        in_specs=(
            P("pipe", None, "tensor", None),
            P("pipe", None, None, "tensor"),
            P("pipe", None, "tensor"),
            P("pipe", None, "dp", "tensor"),
            P(None, "pipe", None, "dp", "tensor"),
            P("pipe", None, "dp", "tensor"),
            P(None, None, "dp", "tensor"),
            P(None, None, "dp", "tensor"),
        ),
        out_specs=(
            P("pipe", None, "dp", "tensor"),
            P("pipe", None, "dp", "tensor"),
            P("pipe", None, ("tensor", "dp"), None),
            P("pipe", None, "dp", "tensor"),
        ),
        check_vma=False,
    )
```

time: 259 us -> 68.7 us (0.27)
  waiting for transfers between devices: 157 us -> 22 us
  matrix products: 25.9 us -> 0 us
  blocking collectives: 24 us -> 0 us
  starting transfers between devices: 6.2 us -> 27.3 us
  Pallas kernels: 0 us -> 13.9 us
  between operations: 14.2 us -> 0.83 us
  local copies, waits for them, and re-layouts: 17.7 us -> 4.39 us
  other arithmetic: 13 us -> 0 us
    reduce_scatter x2 -> x0, waiting for transfers between devices: 70.4 us -> none  [the longest x1 38.1 us: per_device(): lax.psum_scatter(grad_up.astype(jnp.bfloat16), 'dp', scatter_dimension=1,...]
    psum x2 -> x0, waiting for transfers between devices: 57.8 us -> none  [per_device(): lax.psum(part_latent.astype(jnp.bfloat16), 'tensor').astype(jnp.float32)]
    dot_general x12 -> x0, matrix products: 25.9 us -> none  [the longest x2 8.19 us: per_device(): jnp.einsum('snd,snr->sdr', scaled[1], latent_step, preferred_element_type...]
    psum x2 -> x0, blocking collectives: 24 us -> none  [per_device(): lax.psum(part_squares.astype(jnp.bfloat16), 'tensor').astype(jnp.float32)]
    ppermute x4 -> x21, starting transfers between devices: 6.04 us -> 27.3 us  [the longest x12 17.1 us: around(): lax.ppermute(arrays[k], 'tensor', [(i, i ^ k) for i in range(parts)])]
    pallas_call x0 -> x16, Pallas kernels: none -> 13.9 us  [call(): pl.pallas_call(run, in_specs=[pl.BlockSpec(memory_space=pl.ANY)] * raw +...]
    slice x10 -> x0, local copies, waits for them, and re-layouts: 9.89 us -> none  [the longest x2 4.16 us: per_device(): mirrored_up = flattened[count_down:].reshape(far_up.shape)]
    ppermute x4 -> x21, waiting for transfers between devices: 29.1 us -> 22 us  [the longest x12 13.5 us: around(): lax.ppermute(arrays[k], 'tensor', [(i, i ^ k) for i in range(parts)])]
  transfers between devices with their start and end apart: 8 -> 21, of which waited for: 6 -> 9; matrix products, arithmetic and copies ran while one was open for 5% -> 0% of each run, Pallas kernels for 0% -> 11%
where the time goes in v2:
time: 68.7 us; the launch traced here: 68.4 us
  starting transfers between devices  27.3 us (40%)
  waiting for transfers between devices  22 us (32%)
  Pallas kernels  13.9 us (20%)
  local copies, waits for them, and re-layouts  4.39 us (6%)
  between operations  0.83 us (1%)
    ppermute x12, starting transfers between devices, around(): lax.ppermute(arrays[k], 'tensor', [(i, i ^ k) for i in range(parts)])  17.1 us
    pallas_call x16, Pallas kernels, call(): pl.pallas_call(run, in_specs=[pl.BlockSpec(memory_space=pl.ANY)] * raw +...  13.9 us
    ppermute x12, waiting for transfers between devices, around(): lax.ppermute(arrays[k], 'tensor', [(i, i ^ k) for i in range(parts)])  13.5 us
    ppermute x1, waiting for transfers between devices, per_device(): from_second = lax.ppermute(second, ('pipe', 'tensor'), cross)  5.52 us
    ppermute x3, starting transfers between devices, across(): lax.ppermute(arrays[k], 'dp', [(i, i ^ k) for i in range(groups)])  4.44 us
    unnamed x18, local copies, waits for them, and re-layouts  4.39 us
    ppermute x4, starting transfers between devices, mirrored(): return lax.ppermute(far, ('pipe', 'dp'), pairs)  4.29 us
    ppermute x4, waiting for transfers between devices, mirrored(): return lax.ppermute(far, ('pipe', 'dp'), pairs)  1.87 us
  transfers between devices with their start and end apart: 21, of which 9 were waited for; matrix products, arithmetic and copies ran while one was open for 0% of the time, Pallas kernels for 11%

profile of v2, /device:TPU:0, one launch (start us, length us, event | category | flops | bytes accessed | tf_op | source)
XLA Modules:
  0.0 68.4 jit_solution(8915458586153654551)
XLA Ops:
  0.7 4.9 %first_partials.1 = (bf16[32,1152]{1,0:T(8,128)(2,1)}, bf16[32,1152]{1,0:T(8,128)(2,1)}, bf16[32,1152]{1,0:T(8,128)(2,1)}, bf16[32,1152]{1,0:T(8,128)(2,1)}) custom-call(bf16[1,4,1280,256]{3,2,1,0:T(8,128)(2,1)} %refs_0_.5, bf16[1,4,256,1280]{3,2,1,0:T(8,128)(2,1)} %refs_1_.5, f32[1,4,1280]{2,1,0:T(4,128)} %refs_6_.5, bf16[1,4,32,1280]{3,2,1,0:T(8,128)(2,1)} %refs_7_.4, ...), custom_call_target="tpu_custom_call" | custom-call | flops 5500000256 | tf_op jit(solution)/shard_map/first_partials/pallas_call | solution.py:52
  5.6 0.9 %copy-done.8 = bf16[32,1152]{1,0:T(8,128)(2,1)S(1)} copy-done((bf16[32,1152]{1,0:T(8,128)(2,1)S(1)}, bf16[32,1152]{1,0:T(8,128)(2,1)}, u32[]{:S(2)}) %copy-start.8) | copy-done | bytes 73752
  6.6 2.5 %collective-permute-start.11 = (bf16[2,32,3840]{2,1,0:T(8,128)(2,1)S(1)}, bf16[2,32,3840]{2,1,0:T(8,128)(2,1)S(1)}, u32[]{:S(2)}, u32[]{:S(2)}) collective-permute-start(bf16[2,32,3840]{2,1,0:T(8,128)(2,1)S(1)} %get-tuple-element.50), channel_id=1, source_target_pairs={{0,24},{1,25},{8,16},{9,17},{16,8},{17,9},{24,0},{25,1},{2,26},{3,... | collective-permute-start | bytes 1474568 | tf_op jit(solution)/shard_map/ppermute | solution.py:553
  9.1 1.6 %collective-permute-start = (bf16[32,1152]{1,0:T(8,128)(2,1)}, bf16[32,1152]{1,0:T(8,128)(2,1)S(1)}, u32[]{:S(2)}, u32[]{:S(2)}) collective-permute-start(bf16[32,1152]{1,0:T(8,128)(2,1)} %get-tuple-element.36.refs_4_.refs_2_), channel_id=1, source_target_pairs={{0,2},{2,0},{4,6},{6,4},{1,3},{3,1},{5,7},{7,5},{8,10},{10,8},{12,... | collective-permute-start | bytes 221192 | tf_op jit(solution)/shard_map/ppermute | solution.py:543
  10.7 2.6 %collective-permute-start.1 = (bf16[32,1152]{1,0:T(8,128)(2,1)}, bf16[32,1152]{1,0:T(8,128)(2,1)S(1)}, u32[]{:S(2)}, u32[]{:S(2)}) collective-permute-start(bf16[32,1152]{1,0:T(8,128)(2,1)} %get-tuple-element.38), channel_id=1, source_target_pairs={{0,4},{2,6},{4,0},{6,2},{1,5},{3,7},{5,1},{7,3},{8,12},{10,14},{12... | collective-permute-start | bytes 221192 | tf_op jit(solution)/shard_map/ppermute | solution.py:543
  13.5 1.7 %copy-done.1 = bf16[1,4,1280,256]{3,2,1,0:T(8,128)(2,1)S(1)} copy-done((bf16[1,4,1280,256]{3,2,1,0:T(8,128)(2,1)S(1)}, bf16[1,4,1280,256]{3,2,1,0:T(8,128)(2,1)}, u32[]{:S(2)}) %copy-start.1) | copy-done | bytes 2621464
  15.2 1.7 %copy-done.2 = bf16[1,4,256,1280]{3,2,1,0:T(8,128)(2,1)S(1)} copy-done((bf16[1,4,256,1280]{3,2,1,0:T(8,128)(2,1)S(1)}, bf16[1,4,256,1280]{3,2,1,0:T(8,128)(2,1)}, u32[]{:S(2)}) %copy-start.2) | copy-done | bytes 2621464
  17.4 2.5 %collective-permute-done.1.refs_2_ = bf16[32,1152]{1,0:T(8,128)(2,1)S(1)} collective-permute-done((bf16[32,1152]{1,0:T(8,128)(2,1)}, bf16[32,1152]{1,0:T(8,128)(2,1)S(1)}, u32[]{:S(2)}, u32[]{:S(2)}) %collective-permute-start.1) | collective-permute-done | bytes 73760 | tf_op jit(solution)/shard_map/ppermute | solution.py:543
  20.2 1.8 %collective-permute-start.3 = (bf16[32,1152]{1,0:T(8,128)(2,1)S(1)}, bf16[32,1152]{1,0:T(8,128)(2,1)S(1)}, u32[]{:S(2)}, u32[]{:S(2)}) collective-permute-start(bf16[32,1152]{1,0:T(8,128)(2,1)S(1)} %get-tuple-element.42.refs_0_), channel_id=1, source_target_pairs={{0,2},{2,0},{4,6},{6,4},{1,3},{3,1},{5,7},{7,5},{8,10},{10,8},{12,... | collective-permute-start | bytes 221192 | tf_op jit(solution)/shard_map/ppermute | solution.py:543
  21.9 1.5 %collective-permute-start.4 = (bf16[32,1152]{1,0:T(8,128)(2,1)S(1)}, bf16[32,1152]{1,0:T(8,128)(2,1)S(1)}, u32[]{:S(2)}, u32[]{:S(2)}) collective-permute-start(bf16[32,1152]{1,0:T(8,128)(2,1)S(1)} %get-tuple-element.42.refs_0_), channel_id=1, source_target_pairs={{0,4},{2,6},{4,0},{6,2},{1,5},{3,7},{5,1},{7,3},{8,12},{10,14},{12... | collective-permute-start | bytes 221192 | tf_op jit(solution)/shard_map/ppermute | solution.py:543
  23.4 1.2 %collective-permute-start.5 = (bf16[32,1152]{1,0:T(8,128)(2,1)S(1)}, bf16[32,1152]{1,0:T(8,128)(2,1)S(1)}, u32[]{:S(2)}, u32[]{:S(2)}) collective-permute-start(bf16[32,1152]{1,0:T(8,128)(2,1)S(1)} %get-tuple-element.42.refs_0_), channel_id=1, source_target_pairs={{0,6},{2,4},{4,2},{6,0},{1,7},{3,5},{5,3},{7,1},{8,14},{10,12},{12... | collective-permute-start | bytes 221192 | tf_op jit(solution)/shard_map/ppermute | solution.py:543
  24.8 1.6 %collective-permute-start.12 = (bf16[4,32,2560]{2,1,0:T(8,128)(2,1)S(1)}, bf16[4,32,2560]{2,1,0:T(8,128)(2,1)S(1)}, u32[]{:S(2)}, u32[]{:S(2)}) collective-permute-start(bf16[4,32,2560]{2,1,0:T(8,128)(2,1)S(1)} %get-tuple-element.51), channel_id=1, source_target_pairs={{0,1},{1,0},{2,3},{3,2},{4,5},{5,4},{6,7},{7,6},{8,9},{9,8},{10,11... | collective-permute-start | bytes 1966088 | tf_op jit(solution)/shard_map/ppermute | solution.py:557
  26.3 4.1 %collective-permute-done.4.refs_2_ = bf16[32,1152]{1,0:T(8,128)(2,1)S(1)} collective-permute-done((bf16[32,1152]{1,0:T(8,128)(2,1)S(1)}, bf16[32,1152]{1,0:T(8,128)(2,1)S(1)}, u32[]{:S(2)}, u32[]{:S(2)}) %collective-permute-start.4) | collective-permute-done | bytes 73760 | tf_op jit(solution)/shard_map/ppermute | solution.py:543
  32.0 1.4 %collective-permute-start.7 = (bf16[4,32,1280]{2,1,0:T(8,128)(2,1)S(1)}, bf16[4,32,1280]{2,1,0:T(8,128)(2,1)S(1)}, u32[]{:S(2)}, u32[]{:S(2)}) collective-permute-start(bf16[4,32,1280]{2,1,0:T(8,128)(2,1)S(1)} %second_results.1.refs_10_.refs_2_), channel_id=1, source_target_pairs={{0,2},{2,0},{4,6},{6,4},{8,16},{10,18},{12,20},{14,22},{16,8},{18,... | collective-permute-start | bytes 983048 | tf_op jit(solution)/shard_map/ppermute | solution.py:580
  33.6 5.5 %collective-permute-done.7.refs_1_ = bf16[4,32,1280]{2,1,0:T(8,128)(2,1)S(1)} collective-permute-done((bf16[4,32,1280]{2,1,0:T(8,128)(2,1)S(1)}, bf16[4,32,1280]{2,1,0:T(8,128)(2,1)S(1)}, u32[]{:S(2)}, u32[]{:S(2)}) %collective-permute-start.7) | collective-permute-done | bytes 327712 | tf_op jit(solution)/shard_map/ppermute | solution.py:580
  39.1 1.3 %later_partials.1 = (bf16[32,640]{1,0:T(8,128)(2,1)S(1)}, bf16[32,640]{1,0:T(8,128)(2,1)S(1)}, bf16[32,640]{1,0:T(8,128)(2,1)S(1)}, bf16[32,640]{1,0:T(8,128)(2,...) custom-call(bf16[4,32,1280]{2,1,0:T(8,128)(2,1)S(1)} %collective-permute-done.6.refs_0_, ...), custom_call_target="tpu_custom_call" | custom-call | flops 1430000000 | tf_op jit(solution)/shard_map/later_partials/pallas_call | solution.py:52
  40.5 1.4 %collective-permute-start.8 = (bf16[32,640]{1,0:T(8,128)(2,1)S(1)}, bf16[32,640]{1,0:T(8,128)(2,1)S(1)}, u32[]{:S(2)}, u32[]{:S(2)}) collective-permute-start(bf16[32,640]{1,0:T(8,128)(2,1)S(1)} %get-tuple-element.46), channel_id=1, source_target_pairs={{0,2},{2,0},{4,6},{6,4},{1,3},{3,1},{5,7},{7,5},{8,10},{10,8},{12,... | collective-permute-start | bytes 122888 | tf_op jit(solution)/shard_map/ppermute | solution.py:543
  41.9 1.5 %collective-permute-start.9 = (bf16[32,640]{1,0:T(8,128)(2,1)S(1)}, bf16[32,640]{1,0:T(8,128)(2,1)S(1)}, u32[]{:S(2)}, u32[]{:S(2)}) collective-permute-start(bf16[32,640]{1,0:T(8,128)(2,1)S(1)} %get-tuple-element.47), channel_id=1, source_target_pairs={{0,4},{2,6},{4,0},{6,2},{1,5},{3,7},{5,1},{7,3},{8,12},{10,14},{12... | collective-permute-start | bytes 122888 | tf_op jit(solution)/shard_map/ppermute | solution.py:543
  43.4 1.5 %collective-permute-start.10 = (bf16[32,640]{1,0:T(8,128)(2,1)S(1)}, bf16[32,640]{1,0:T(8,128)(2,1)S(1)}, u32[]{:S(2)}, u32[]{:S(2)}) collective-permute-start(bf16[32,640]{1,0:T(8,128)(2,1)S(1)} %get-tuple-element.48), channel_id=1, source_target_pairs={{0,6},{2,4},{4,2},{6,0},{1,7},{3,5},{5,3},{7,1},{8,14},{10,12},{12... | collective-permute-start | bytes 122888 | tf_op jit(solution)/shard_map/ppermute | solution.py:543
  45.0 1.5 %collective-permute-start.16 = (bf16[2,32,1792]{2,1,0:T(8,128)(2,1)S(1)}, bf16[2,32,1792]{2,1,0:T(8,128)(2,1)S(1)}, u32[]{:S(2)}, u32[]{:S(2)}) collective-permute-start(bf16[2,32,1792]{2,1,0:T(8,128)(2,1)S(1)} %get-tuple-element.59), channel_id=1, source_target_pairs={{0,1},{1,0},{2,3},{3,2},{4,5},{5,4},{6,7},{7,6},{8,9},{9,8},{10,11... | collective-permute-start | bytes 688136 | tf_op jit(solution)/shard_map/ppermute | solution.py:557
  46.5 1.7 %collective-permute-start.18 = (bf16[2,32,1792]{2,1,0:T(8,128)(2,1)S(1)}, bf16[2,32,1792]{2,1,0:T(8,128)(2,1)S(1)}, u32[]{:S(2)}, u32[]{:S(2)}) collective-permute-start(bf16[2,32,1792]{2,1,0:T(8,128)(2,1)S(1)} %get-tuple-element.61), channel_id=1, source_target_pairs={{0,25},{1,24},{8,17},{9,16},{16,9},{17,8},{24,1},{25,0},{2,27},{3,... | collective-permute-start | bytes 688136 | tf_op jit(solution)/shard_map/ppermute | solution.py:553
  48.3 0.9 %collective-permute-done.10.refs_3_ = bf16[32,640]{1,0:T(8,128)(2,1)S(1)} collective-permute-done((bf16[32,640]{1,0:T(8,128)(2,1)S(1)}, bf16[32,640]{1,0:T(8,128)(2,1)S(1)}, u32[]{:S(2)}, u32[]{:S(2)}) %collective-permute-start.10) | collective-permute-done | bytes 40992 | tf_op jit(solution)/shard_map/ppermute | solution.py:543
  49.5 2.2 %collective-permute-start.14 = (bf16[32,640]{1,0:T(8,128)(2,1)S(1)}, bf16[32,640]{1,0:T(8,128)(2,1)S(1)}, u32[]{:S(2)}, u32[]{:S(2)}) collective-permute-start(bf16[32,640]{1,0:T(8,128)(2,1)S(1)} %later_latents.1.refs_0_), channel_id=1, source_target_pairs={{0,4},{2,6},{4,0},{6,2},{1,5},{3,7},{5,1},{7,3},{8,12},{10,14},{12... | collective-permute-start | bytes 122888 | tf_op jit(solution)/shard_map/ppermute | solution.py:543
  51.7 1.8 %collective-permute-done.13.refs_1_ = bf16[32,640]{1,0:T(8,128)(2,1)S(1)} collective-permute-done((bf16[32,640]{1,0:T(8,128)(2,1)S(1)}, bf16[32,640]{1,0:T(8,128)(2,1)S(1)}, u32[]{:S(2)}, u32[]{:S(2)}) %collective-permute-start.13) | collective-permute-done | bytes 40992 | tf_op jit(solution)/shard_map/ppermute | solution.py:543
  53.5 1.6 %collective-permute-start.15 = (bf16[32,640]{1,0:T(8,128)(2,1)S(1)}, bf16[32,640]{1,0:T(8,128)(2,1)S(1)}, u32[]{:S(2)}, u32[]{:S(2)}) collective-permute-start(bf16[32,640]{1,0:T(8,128)(2,1)S(1)} %later_latents.1.refs_0_), channel_id=1, source_target_pairs={{0,6},{2,4},{4,2},{6,0},{1,7},{3,5},{5,3},{7,1},{8,14},{10,12},{12... | collective-permute-start | bytes 122888 | tf_op jit(solution)/shard_map/ppermute | solution.py:543
  55.1 4.2 %collective-permute-done.15.refs_3_ = bf16[32,640]{1,0:T(8,128)(2,1)S(1)} collective-permute-done((bf16[32,640]{1,0:T(8,128)(2,1)S(1)}, bf16[32,640]{1,0:T(8,128)(2,1)S(1)}, u32[]{:S(2)}, u32[]{:S(2)}) %collective-permute-start.15) | collective-permute-done | bytes 40992 | tf_op jit(solution)/shard_map/ppermute | solution.py:543
  59.4 1.4 %up_grads.1 = (f32[1,2,128,1280]{3,2,1,0:T(8,128)}, f32[8,128]{1,0:T(8,128)S(1)}) custom-call(bf16[4,32,2560]{2,1,0:T(8,128)(2,1)S(1)} %get-tuple-element.56.refs_0_, bf16[4,32,2560]{2,1,0:T(8,128)(2,1)S(1)} %collective-permute-done.12.refs_0_.refs_1_, bf16[2,32,1792]{2,1,0:T(8,128)(2,1)S(1)} %get-tuple-element.58.refs_2_, ...), custom_call_target="tpu_custom_call" | custom-call | flops 440000000 | tf_op jit(solution)/shard_map/up_grads/pallas_call | solution.py:52
  60.9 1.9 %collective-permute-done.19.refs_1_ = bf16[2,32,256]{2,1,0:T(8,128)(2,1)S(1)} collective-permute-done((bf16[2,32,256]{2,1,0:T(8,128)(2,1)S(1)}, bf16[2,32,256]{2,1,0:T(8,128)(2,1)S(1)}, u32[]{:S(2)}, u32[]{:S(2)}) %collective-permute-start.19) | collective-permute-done | bytes 32800 | tf_op jit(solution)/shard_map/ppermute | solution.py:553
  62.7 1.3 %collective-permute-start.20 = (bf16[4,32,256]{2,1,0:T(8,128)(2,1)S(1)}, bf16[4,32,256]{2,1,0:T(8,128)(2,1)S(1)}, u32[]{:S(2)}, u32[]{:S(2)}) collective-permute-start(bf16[4,32,256]{2,1,0:T(8,128)(2,1)S(1)} %late_share.1.refs_6_), channel_id=1, source_target_pairs={{0,1},{1,0},{2,3},{3,2},{4,5},{5,4},{6,7},{7,6},{8,9},{9,8},{10,11... | collective-permute-start | bytes 196616 | tf_op jit(solution)/shard_map/ppermute | solution.py:557
  64.1 2.1 %last_results.1 = (bf16[1,4,32,1280]{3,2,1,0:T(8,128)(2,1)}, bf16[1,4,32,1280]{3,2,1,0:T(8,128)(2,1)}) custom-call(bf16[32,640]{1,0:T(8,128)(2,1)S(1)} %later_latents.1.refs_0_, bf16[32,640]{1,0:T(8,128)(2,1)S(1)} %collective-permute-done.13.refs_1_, bf16[32,640]{1,0:T(8,128)(2,1)S(1)} %collective-permute-done.14.refs_2_, ...), custom_call_target="tpu_custom_call" | custom-call | flops 770000000 | tf_op jit(solution)/shard_map/last_results/pallas_call | solution.py:52
  66.1 0.9 %collective-permute-done.20.refs_7_ = bf16[4,32,256]{2,1,0:T(8,128)(2,1)S(1)} collective-permute-done((bf16[4,32,256]{2,1,0:T(8,128)(2,1)S(1)}, bf16[4,32,256]{2,1,0:T(8,128)(2,1)S(1)}, u32[]{:S(2)}, u32[]{:S(2)}) %collective-permute-start.20) | collective-permute-done | bytes 65568 | tf_op jit(solution)/shard_map/ppermute | solution.py:557
  67.0 1.4 %down_grads.1 = f32[1,2,640,256]{3,2,1,0:T(8,128)} custom-call(bf16[4,32,2560]{2,1,0:T(8,128)(2,1)S(1)} %get-tuple-element.56.refs_0_, bf16[4,32,2560]{2,1,0:T(8,128)(2,1)S(1)} %collective-permute-done.12.refs_0_.refs_1_, bf16[2,32,1792]{2,1,0:T(8,128)(2,1)S(1)} %get-tuple-element.58.refs_2_, bf16[2,32,1792]{2,1,0:T(8,128)(2,1)S(1)} %collective-permute-done.16.refs_3_, ...), custom_call_target="tpu_custom_call" | custom-call | flops 1650000000 | tf_op jit(solution)/shard_map/down_grads/pallas_call | solution.py:52
  (44 shorter events, 3.4 us)
Async XLA Ops:
  0.6 5.0 %copy-start.5 = (f32[1,4,1280]{2,1,0:T(4,128)S(1)}, f32[1,4,1280]{2,1,0:T(4,128)}, u32[]{:S(2)}) copy-start(f32[1,4,1280]{2,1,0:T(4,128)} %refs_6_.5) | copy-start | bytes 61444
  0.6 5.0 %copy-start = (bf16[2,1,4,32,1280]{4,3,2,1,0:T(8,128)(2,1)S(1)}, bf16[2,1,4,32,1280]{4,3,2,1,0:T(8,128)(2,1)}, u32[]{:S(2)}) copy-start(bf16[2,1,4,32,1280]{4,3,2,1,0:T(8,128)(2,1)} %refs_8_.5) | copy-start | bytes 1966084
  0.7 4.9 %copy-start.3 = (bf16[1,4,32,1280]{3,2,1,0:T(8,128)(2,1)S(1)}, bf16[1,4,32,1280]{3,2,1,0:T(8,128)(2,1)}, u32[]{:S(2)}) copy-start(bf16[1,4,32,1280]{3,2,1,0:T(8,128)(2,1)} %refs_9_.3) | copy-start | bytes 983044
  5.6 0.9 %copy-start.8 = (bf16[32,1152]{1,0:T(8,128)(2,1)S(1)}, bf16[32,1152]{1,0:T(8,128)(2,1)}, u32[]{:S(2)}) copy-start(bf16[32,1152]{1,0:T(8,128)(2,1)} %get-tuple-element.35.refs_3_) | copy-start | bytes 221188
  6.6 18.0 %collective-permute-start.11 = (bf16[2,32,3840]{2,1,0:T(8,128)(2,1)S(1)}, bf16[2,32,3840]{2,1,0:T(8,128)(2,1)S(1)}, u32[]{:S(2)}, u32[]{:S(2)}) collective-permute-start(bf16[2,32,3840]{2,1,0:T(8,128)(2,1)S(1)} %get-tuple-element.50), channel_id=1, source_target_pairs={{0,24},{1,25},{8,16},{9,17},{16,8},{17,9},{24,0},{25,1},{2,26},{3,... | collective-permute-start | bytes 1474568 | tf_op jit(solution)/shard_map/ppermute | solution.py:553
  9.1 8.3 %collective-permute-start = (bf16[32,1152]{1,0:T(8,128)(2,1)}, bf16[32,1152]{1,0:T(8,128)(2,1)S(1)}, u32[]{:S(2)}, u32[]{:S(2)}) collective-permute-start(bf16[32,1152]{1,0:T(8,128)(2,1)} %get-tuple-element.36.refs_4_.refs_2_), channel_id=1, source_target_pairs={{0,2},{2,0},{4,6},{6,4},{1,3},{3,1},{5,7},{7,5},{8,10},{10,8},{12,... | collective-permute-start | bytes 221192 | tf_op jit(solution)/shard_map/ppermute | solution.py:543
  10.7 9.2 %collective-permute-start.1 = (bf16[32,1152]{1,0:T(8,128)(2,1)}, bf16[32,1152]{1,0:T(8,128)(2,1)S(1)}, u32[]{:S(2)}, u32[]{:S(2)}) collective-permute-start(bf16[32,1152]{1,0:T(8,128)(2,1)} %get-tuple-element.38), channel_id=1, source_target_pairs={{0,4},{2,6},{4,0},{6,2},{1,5},{3,7},{5,1},{7,3},{8,12},{10,14},{12... | collective-permute-start | bytes 221192 | tf_op jit(solution)/shard_map/ppermute | solution.py:543
  13.3 6.6 %collective-permute-start.2 = (bf16[32,1152]{1,0:T(8,128)(2,1)}, bf16[32,1152]{1,0:T(8,128)(2,1)S(1)}, u32[]{:S(2)}, u32[]{:S(2)}) collective-permute-start(bf16[32,1152]{1,0:T(8,128)(2,1)} %get-tuple-element.39), channel_id=1, source_target_pairs={{0,6},{2,4},{4,2},{6,0},{1,7},{3,5},{5,3},{7,1},{8,14},{10,12},{12... | collective-permute-start | bytes 221192 | tf_op jit(solution)/shard_map/ppermute | solution.py:543
  13.5 1.7 %copy-start.1 = (bf16[1,4,1280,256]{3,2,1,0:T(8,128)(2,1)S(1)}, bf16[1,4,1280,256]{3,2,1,0:T(8,128)(2,1)}, u32[]{:S(2)}) copy-start(bf16[1,4,1280,256]{3,2,1,0:T(8,128)(2,1)} %refs_0_.5) | copy-start | bytes 7864324
  15.2 1.7 %copy-start.2 = (bf16[1,4,256,1280]{3,2,1,0:T(8,128)(2,1)S(1)}, bf16[1,4,256,1280]{3,2,1,0:T(8,128)(2,1)}, u32[]{:S(2)}) copy-start(bf16[1,4,256,1280]{3,2,1,0:T(8,128)(2,1)} %refs_1_.5) | copy-start | bytes 7864324
  17.4 13.1 %copy-start.4 = (bf16[1,4,32,1280]{3,2,1,0:T(8,128)(2,1)S(1)}, bf16[1,4,32,1280]{3,2,1,0:T(8,128)(2,1)}, u32[]{:S(2)}) copy-start(bf16[1,4,32,1280]{3,2,1,0:T(8,128)(2,1)} %refs_7_.4) | copy-start | bytes 983044
  20.2 6.2 %collective-permute-start.3 = (bf16[32,1152]{1,0:T(8,128)(2,1)S(1)}, bf16[32,1152]{1,0:T(8,128)(2,1)S(1)}, u32[]{:S(2)}, u32[]{:S(2)}) collective-permute-start(bf16[32,1152]{1,0:T(8,128)(2,1)S(1)} %get-tuple-element.42.refs_0_), channel_id=1, source_target_pairs={{0,2},{2,0},{4,6},{6,4},{1,3},{3,1},{5,7},{7,5},{8,10},{10,8},{12,... | collective-permute-start | bytes 221192 | tf_op jit(solution)/shard_map/ppermute | solution.py:543
  21.9 8.5 %collective-permute-start.4 = (bf16[32,1152]{1,0:T(8,128)(2,1)S(1)}, bf16[32,1152]{1,0:T(8,128)(2,1)S(1)}, u32[]{:S(2)}, u32[]{:S(2)}) collective-permute-start(bf16[32,1152]{1,0:T(8,128)(2,1)S(1)} %get-tuple-element.42.refs_0_), channel_id=1, source_target_pairs={{0,4},{2,6},{4,0},{6,2},{1,5},{3,7},{5,1},{7,3},{8,12},{10,14},{12... | collective-permute-start | bytes 221192 | tf_op jit(solution)/shard_map/ppermute | solution.py:543
  23.4 7.0 %collective-permute-start.5 = (bf16[32,1152]{1,0:T(8,128)(2,1)S(1)}, bf16[32,1152]{1,0:T(8,128)(2,1)S(1)}, u32[]{:S(2)}, u32[]{:S(2)}) collective-permute-start(bf16[32,1152]{1,0:T(8,128)(2,1)S(1)} %get-tuple-element.42.refs_0_), channel_id=1, source_target_pairs={{0,6},{2,4},{4,2},{6,0},{1,7},{3,5},{5,3},{7,1},{8,14},{10,12},{12... | collective-permute-start | bytes 221192 | tf_op jit(solution)/shard_map/ppermute | solution.py:543
  24.8 21.8 %collective-permute-start.12 = (bf16[4,32,2560]{2,1,0:T(8,128)(2,1)S(1)}, bf16[4,32,2560]{2,1,0:T(8,128)(2,1)S(1)}, u32[]{:S(2)}, u32[]{:S(2)}) collective-permute-start(bf16[4,32,2560]{2,1,0:T(8,128)(2,1)S(1)} %get-tuple-element.51), channel_id=1, source_target_pairs={{0,1},{1,0},{2,3},{3,2},{4,5},{5,4},{6,7},{7,6},{8,9},{9,8},{10,11... | collective-permute-start | bytes 1966088 | tf_op jit(solution)/shard_map/ppermute | solution.py:557
  31.2 8.0 %copy-start.6 = (bf16[1,2,32,1280]{3,2,1,0:T(8,128)(2,1)S(1)}, bf16[1,2,32,1280]{3,2,1,0:T(8,128)(2,1)}, u32[]{:S(2)}) copy-start(bf16[1,2,32,1280]{3,2,1,0:T(8,128)(2,1)} %refs_3_.3) | copy-start | bytes 491524
  31.2 8.0 %copy-start.7 = (bf16[1,2,32,1280]{3,2,1,0:T(8,128)(2,1)S(1)}, bf16[1,2,32,1280]{3,2,1,0:T(8,128)(2,1)}, u32[]{:S(2)}) copy-start(bf16[1,2,32,1280]{3,2,1,0:T(8,128)(2,1)} %refs_4_.3) | copy-start | bytes 491524
  31.9 1.7 %collective-permute-start.6 = (bf16[4,32,1280]{2,1,0:T(8,128)(2,1)S(1)}, bf16[4,32,1280]{2,1,0:T(8,128)(2,1)S(1)}, u32[]{:S(2)}, u32[]{:S(2)}) collective-permute-start(bf16[4,32,1280]{2,1,0:T(8,128)(2,1)S(1)} %get-tuple-element.44), channel_id=1, source_target_pairs={{0,8},{8,0},{16,24},{24,16},{1,9},{9,1},{17,25},{25,17},{2,10},{10... | collective-permute-start | bytes 983048 | tf_op jit(solution)/shard_map/ppermute | solution.py:584
  32.0 7.1 %collective-permute-start.7 = (bf16[4,32,1280]{2,1,0:T(8,128)(2,1)S(1)}, bf16[4,32,1280]{2,1,0:T(8,128)(2,1)S(1)}, u32[]{:S(2)}, u32[]{:S(2)}) collective-permute-start(bf16[4,32,1280]{2,1,0:T(8,128)(2,1)S(1)} %second_results.1.refs_10_.refs_2_), channel_id=1, source_target_pairs={{0,2},{2,0},{4,6},{6,4},{8,16},{10,18},{12,20},{14,22},{16,8},{18,... | collective-permute-start | bytes 983048 | tf_op jit(solution)/shard_map/ppermute | solution.py:580
  40.5 6.1 %collective-permute-start.8 = (bf16[32,640]{1,0:T(8,128)(2,1)S(1)}, bf16[32,640]{1,0:T(8,128)(2,1)S(1)}, u32[]{:S(2)}, u32[]{:S(2)}) collective-permute-start(bf16[32,640]{1,0:T(8,128)(2,1)S(1)} %get-tuple-element.46), channel_id=1, source_target_pairs={{0,2},{2,0},{4,6},{6,4},{1,3},{3,1},{5,7},{7,5},{8,10},{10,8},{12,... | collective-permute-start | bytes 122888 | tf_op jit(solution)/shard_map/ppermute | solution.py:543
  41.9 6.4 %collective-permute-start.9 = (bf16[32,640]{1,0:T(8,128)(2,1)S(1)}, bf16[32,640]{1,0:T(8,128)(2,1)S(1)}, u32[]{:S(2)}, u32[]{:S(2)}) collective-permute-start(bf16[32,640]{1,0:T(8,128)(2,1)S(1)} %get-tuple-element.47), channel_id=1, source_target_pairs={{0,4},{2,6},{4,0},{6,2},{1,5},{3,7},{5,1},{7,3},{8,12},{10,14},{12... | collective-permute-start | bytes 122888 | tf_op jit(solution)/shard_map/ppermute | solution.py:543
  43.4 5.8 %collective-permute-start.10 = (bf16[32,640]{1,0:T(8,128)(2,1)S(1)}, bf16[32,640]{1,0:T(8,128)(2,1)S(1)}, u32[]{:S(2)}, u32[]{:S(2)}) collective-permute-start(bf16[32,640]{1,0:T(8,128)(2,1)S(1)} %get-tuple-element.48), channel_id=1, source_target_pairs={{0,6},{2,4},{4,2},{6,0},{1,7},{3,5},{5,3},{7,1},{8,14},{10,12},{12... | collective-permute-start | bytes 122888 | tf_op jit(solution)/shard_map/ppermute | solution.py:543
  45.0 14.4 %collective-permute-start.16 = (bf16[2,32,1792]{2,1,0:T(8,128)(2,1)S(1)}, bf16[2,32,1792]{2,1,0:T(8,128)(2,1)S(1)}, u32[]{:S(2)}, u32[]{:S(2)}) collective-permute-start(bf16[2,32,1792]{2,1,0:T(8,128)(2,1)S(1)} %get-tuple-element.59), channel_id=1, source_target_pairs={{0,1},{1,0},{2,3},{3,2},{4,5},{5,4},{6,7},{7,6},{8,9},{9,8},{10,11... | collective-permute-start | bytes 688136 | tf_op jit(solution)/shard_map/ppermute | solution.py:557
  46.5 12.9 %collective-permute-start.17 = (bf16[2,32,1792]{2,1,0:T(8,128)(2,1)S(1)}, bf16[2,32,1792]{2,1,0:T(8,128)(2,1)S(1)}, u32[]{:S(2)}, u32[]{:S(2)}) collective-permute-start(bf16[2,32,1792]{2,1,0:T(8,128)(2,1)S(1)} %get-tuple-element.60), channel_id=1, source_target_pairs={{0,24},{1,25},{8,16},{9,17},{16,8},{17,9},{24,0},{25,1},{2,26},{3,... | collective-permute-start | bytes 688136 | tf_op jit(solution)/shard_map/ppermute | solution.py:553
  46.5 12.9 %collective-permute-start.18 = (bf16[2,32,1792]{2,1,0:T(8,128)(2,1)S(1)}, bf16[2,32,1792]{2,1,0:T(8,128)(2,1)S(1)}, u32[]{:S(2)}, u32[]{:S(2)}) collective-permute-start(bf16[2,32,1792]{2,1,0:T(8,128)(2,1)S(1)} %get-tuple-element.61), channel_id=1, source_target_pairs={{0,25},{1,24},{8,17},{9,16},{16,9},{17,8},{24,1},{25,0},{2,27},{3,... | collective-permute-start | bytes 688136 | tf_op jit(solution)/shard_map/ppermute | solution.py:553
  49.4 4.1 %collective-permute-start.13 = (bf16[32,640]{1,0:T(8,128)(2,1)S(1)}, bf16[32,640]{1,0:T(8,128)(2,1)S(1)}, u32[]{:S(2)}, u32[]{:S(2)}) collective-permute-start(bf16[32,640]{1,0:T(8,128)(2,1)S(1)} %later_latents.1.refs_0_), channel_id=1, source_target_pairs={{0,2},{2,0},{4,6},{6,4},{1,3},{3,1},{5,7},{7,5},{8,10},{10,8},{12,... | collective-permute-start | bytes 122888 | tf_op jit(solution)/shard_map/ppermute | solution.py:543
  49.5 5.6 %collective-permute-start.14 = (bf16[32,640]{1,0:T(8,128)(2,1)S(1)}, bf16[32,640]{1,0:T(8,128)(2,1)S(1)}, u32[]{:S(2)}, u32[]{:S(2)}) collective-permute-start(bf16[32,640]{1,0:T(8,128)(2,1)S(1)} %later_latents.1.refs_0_), channel_id=1, source_target_pairs={{0,4},{2,6},{4,0},{6,2},{1,5},{3,7},{5,1},{7,3},{8,12},{10,14},{12... | collective-permute-start | bytes 122888 | tf_op jit(solution)/shard_map/ppermute | solution.py:543
  53.5 5.8 %collective-permute-start.15 = (bf16[32,640]{1,0:T(8,128)(2,1)S(1)}, bf16[32,640]{1,0:T(8,128)(2,1)S(1)}, u32[]{:S(2)}, u32[]{:S(2)}) collective-permute-start(bf16[32,640]{1,0:T(8,128)(2,1)S(1)} %later_latents.1.refs_0_), channel_id=1, source_target_pairs={{0,6},{2,4},{4,2},{6,0},{1,7},{3,5},{5,3},{7,1},{8,14},{10,12},{12... | collective-permute-start | bytes 122888 | tf_op jit(solution)/shard_map/ppermute | solution.py:543
  59.3 3.4 %collective-permute-start.19 = (bf16[2,32,256]{2,1,0:T(8,128)(2,1)S(1)}, bf16[2,32,256]{2,1,0:T(8,128)(2,1)S(1)}, u32[]{:S(2)}, u32[]{:S(2)}) collective-permute-start(bf16[2,32,256]{2,1,0:T(8,128)(2,1)S(1)} %get-tuple-element.63), channel_id=1, source_target_pairs={{0,24},{1,25},{8,16},{9,17},{16,8},{17,9},{24,0},{25,1},{2,26},{3,... | collective-permute-start | bytes 98312 | tf_op jit(solution)/shard_map/ppermute | solution.py:553
  62.7 4.3 %collective-permute-start.20 = (bf16[4,32,256]{2,1,0:T(8,128)(2,1)S(1)}, bf16[4,32,256]{2,1,0:T(8,128)(2,1)S(1)}, u32[]{:S(2)}, u32[]{:S(2)}) collective-permute-start(bf16[4,32,256]{2,1,0:T(8,128)(2,1)S(1)} %late_share.1.refs_6_), channel_id=1, source_target_pairs={{0,1},{1,0},{2,3},{3,2},{4,5},{5,4},{6,7},{7,6},{8,9},{9,8},{10,11... | collective-permute-start | bytes 196616 | tf_op jit(solution)/shard_map/ppermute | solution.py:557

commit v3 on v2

--- a/solution.py
+++ b/solution.py
@@ -26,9 +26,9 @@
     "early_share": 0.3,
     "middle_share": 0.2,
     "late_share": 0.1,
-    "later_latents": 0.3,
+    "later_latents": 3,
     "late_factors": 0.2,
-    "last_results": 0.7,
+    "last_results": 0.2,
     "up_grads": 0.4,
     "down_grads": 1.5
 }
@@ -43,7 +43,7 @@
     return lax.dot_general(a, b, dims, preferred_element_type=F32)
 
 
-def call(body, operands, outs, name, scratch=(), limit=24, after=(), raw=0):
+def call(body, operands, outs, name, scratch=(), limit=24, after=(), raw=0, sent=0):
     count = len(operands)
 
     def run(*refs):
@@ -54,7 +54,8 @@
         in_specs=[pl.BlockSpec(memory_space=pl.ANY)] * raw
         + [pl.BlockSpec(memory_space=pltpu.VMEM)] * (count - raw)
         + [pl.BlockSpec(memory_space=pl.ANY)] * len(after),
-        out_specs=[pl.BlockSpec(memory_space=pltpu.VMEM)] * len(outs),
+        out_specs=[pl.BlockSpec(memory_space=pl.ANY)] * sent
+        + [pl.BlockSpec(memory_space=pltpu.VMEM)] * (len(outs) - sent),
         out_shape=[jax.ShapeDtypeStruct(shape, dtype) for shape, dtype in outs],
         scratch_shapes=list(scratch),
         compiler_params=pltpu.CompilerParams(vmem_limit_bytes=limit * 2**20),
@@ -449,25 +450,43 @@
     )
 
 
-def late_share(near, far, after):
-    half, rows, rank = near.shape
-
-    def body(near_ref, far_ref, out):
-        out[:half] = near_ref[...]
-        out[half:] = far_ref[...]
-
-    return call(body, [near, far], [((2 * half, rows, rank), BF16)], "late_share", after=after)[0]
-
-
-def last_results(received, w_down, w_up, gains, x, kept, g):
-    parts = len(received)
+def sender(sems):
+    copies = []
+
+    def send(source, target):
+        copies.append(pltpu.make_async_copy(source, target, sems.at[len(copies)]))
+        copies[-1].start()
+
+    def finish():
+        for copy in copies:
+            copy.wait()
+
+    return send, finish
+
+
+def last_results(groups, received, w_down, w_up, gains, x, kept, g, early, mid):
+    parts, count = len(received), len(early)
     slots, rows, feats = x.shape
-    ticks = kept.shape[0]
+    ticks, rank = kept.shape[0], w_down.shape[-1]
     width = received[0].shape[-1]
+    half, some = slots // 2, rank // groups
 
     def body(*refs):
         ins, refs = refs[:parts], refs[parts:]
-        down_ref, up_ref, gain_ref, x_ref, kept_ref, g_ref, y_out, dh_out, table = refs
+        down_ref, up_ref, gain_ref, x_ref, kept_ref, g_ref = refs[:6]
+        early, mid, refs = refs[6 : 6 + count], refs[6 + count : 6 + 3 * count], refs[6 + 3 * count :]
+        y_hbm, dh_hbm, grad_hbm, table, y_out, dh_out, grad_out, sems = refs
+        send, finish = sender(sems)
+        for j in range(half):
+            act, dy = [], []
+            for k, e in enumerate(early):
+                for i, m in ((j, mid[k]), (half + j, mid[count + k])):
+                    start = feats + rank
+                    for t in range(ticks):
+                        act.append(m[j, :, start + t * some : start + (t + 1) * some])
+                    dy += [e[i, :, e.shape[-1] - feats :], m[j, :, :feats]]
+            grad_out[j] = dot(jnp.concatenate(act, axis=0), jnp.concatenate(dy, axis=0), TN)
+            send(grad_out.at[j], grad_hbm.at[0, j])
         collect(ins, table)
         for s in range(slots):
             y, dh = slot_results(
@@ -479,57 +498,53 @@
                 down_ref[0, s],
                 up_ref[0, s],
             )
-            y_out[0, s] = y
-            dh_out[0, s] = dh
-
-    return call(
-        body,
-        [*received, w_down, w_up, gains, x, kept, g],
-        [((1, slots, rows, feats), BF16)] * 2,
+            y_out[s] = y
+            dh_out[s] = dh
+            send(y_out.at[s], y_hbm.at[0, s])
+            send(dh_out.at[s], dh_hbm.at[0, s])
+        finish()
+
+    return call(
+        body,
+        [*received, w_down, w_up, gains, x, kept, g, *early, *mid],
+        [((1, slots, rows, feats), BF16)] * 2 + [((1, half, some, feats), F32)],
         "last_results",
-        [pltpu.VMEM((slots * rows, width), BF16)],
-    )
-
-
-def up_grads(groups, ticks, rank, early, mid):
-    count, (slots, rows, _) = len(early), early[0].shape
-    half, some = slots // 2, rank // groups
-    feats = mid[0].shape[-1] - rank - ticks * some
+        [
+            pltpu.VMEM((slots * rows, width), BF16),
+            pltpu.VMEM((slots, rows, feats), BF16),
+            pltpu.VMEM((slots, rows, feats), BF16),
+            pltpu.VMEM((half, some, feats), F32),
+            pltpu.SemaphoreType.DMA((half + 2 * slots,)),
+        ],
+        sent=3,
+    )
+
+
+def down_grads(groups, ticks, feats, early, mid, late):
+    count, (half, rows, rank) = len(early), late[0].shape
+    wide = feats // groups
 
     def body(*refs):
-        early, mid, (out, token) = refs[:count], refs[count : 3 * count], refs[-2:]
-        token[...] = jnp.zeros(token.shape, token.dtype)
-        for j in range(half):
-            act, dy = [], []
-            for k, e in enumerate(early):
-                for i, m in ((j, mid[k]), (half + j, mid[count + k])):
-                    start = feats + rank
-                    for t in range(ticks):
-                        act.append(m[j, :, start + t * some : start + (t + 1) * some])
-                    dy += [e[i, :, e.shape[-1] - feats :], m[j, :, :feats]]
-            out[0, j] = dot(jnp.concatenate(act, axis=0), jnp.concatenate(dy, axis=0), TN)
-
-    outs = [((1, half, some, feats), F32), ((8, LANES), F32)]
-    return call(body, [*early, *mid], outs, "up_grads")
-
-
-def down_grads(groups, ticks, feats, early, mid, late):
-    count, (slots, rows, rank) = len(early), late[0].shape
-    half, wide = slots // 2, feats // groups
-
-    def body(*refs):
-        early, mid, late = refs[:count], refs[count : 3 * count], refs[3 * count : 4 * count]
-        out = refs[-1]
+        early, mid, late = refs[:count], refs[count : 3 * count], refs[3 * count : 5 * count]
+        grad_hbm, grad_out, sems = refs[5 * count :]
+        send, finish = sender(sems)
         for j in range(half):
             hg, du = [], []
-            for k, (e, l) in enumerate(zip(early, late)):
-                for i, m in ((j, mid[k]), (half + j, mid[count + k])):
+            for k, e in enumerate(early):
+                for i, n in ((j, k), (half + j, count + k)):
                     hg += [e[i, :, t * wide : (t + 1) * wide] for t in range(ticks)]
-                    du += [m[j, :, feats : feats + rank], l[i]]
-            out[0, j] = dot(jnp.concatenate(hg, axis=0), jnp.concatenate(du, axis=0), TN)
-
-    return call(
-        body, [*early, *mid, *late], [((1, half, wide, rank), F32)], "down_grads"
+                    du += [mid[n][j, :, feats : feats + rank], late[n][j]]
+            grad_out[j] = dot(jnp.concatenate(hg, axis=0), jnp.concatenate(du, axis=0), TN)
+            send(grad_out.at[j], grad_hbm.at[0, j])
+        finish()
+
+    return call(
+        body,
+        [*early, *mid, *late],
+        [((1, half, wide, rank), F32)],
+        "down_grads",
+        [pltpu.VMEM((half, wide, rank), F32), pltpu.SemaphoreType.DMA((half,))],
+        sent=1,
     )[0]
 
 
@@ -596,10 +611,11 @@
     mid = across(near) + [mirrored(far[k], k) for k in range(groups)]
     message = later_latents(rank, received, held, after=ready)
     received = around([message] * parts)
-    grad_up, token = up_grads(groups, ticks, rank, early, mid)
     near, far = late_factors(slots, rows, rank, received, after=[])
-    late = across([late_share(near, mirrored(far), after=[token])] * groups)
-    y, dh = last_results(received, *weights, gains, x, kept, g)
+    late = across([near] * groups) + [mirrored(far, k) for k in range(groups)]
+    y, dh, grad_up = last_results(
+        groups, received, *weights, gains, x, kept, g, early, mid
+    )
     grad_down = down_grads(groups, ticks, feats, early, mid, late)
     return y, dh, grad_down, grad_up
 

time: 68.7 us -> 66.6 us (0.969)
  waiting for transfers between devices: 22 us -> 19.3 us
  starting transfers between devices: 27.3 us -> 29.2 us
  Pallas kernels: 13.9 us -> 12.6 us
    ppermute x4 -> x5, waiting for transfers between devices: 1.87 us -> 0.07 us  [mirrored(): return lax.ppermute(far, ('pipe', 'dp'), pairs)]
    ppermute x4 -> x5, starting transfers between devices: 4.29 us -> 6.08 us  [mirrored(): return lax.ppermute(far, ('pipe', 'dp'), pairs)]
    pallas_call x16 -> x14, Pallas kernels: 13.9 us -> 12.6 us  [call(): pl.pallas_call(run, in_specs=[pl.BlockSpec(memory_space=pl.ANY)] * raw +...]
    ppermute x3, waiting for transfers between devices: 0.88 us -> 0.01 us  [across(): lax.ppermute(arrays[k], 'dp', [(i, i ^ k) for i in range(groups)])]
  transfers between devices with their start and end apart: 21 -> 22, of which waited for: 9 -> 8; matrix products, arithmetic and copies ran while one was open for 0% -> 0% of each run, Pallas kernels for 11% -> 9%
where the time goes in v3:
time: 66.6 us; the launch traced here: 66.4 us
  starting transfers between devices  29.2 us (44%)
  waiting for transfers between devices  19.3 us (29%)
  Pallas kernels  12.6 us (19%)
  local copies, waits for them, and re-layouts  4.39 us (7%)
  between operations  0.83 us (1%)
    ppermute x12, starting transfers between devices, around(): lax.ppermute(arrays[k], 'tensor', [(i, i ^ k) for i in range(parts)])  17.1 us
    ppermute x12, waiting for transfers between devices, around(): lax.ppermute(arrays[k], 'tensor', [(i, i ^ k) for i in range(parts)])  13.5 us
    pallas_call x14, Pallas kernels, call(): pl.pallas_call(run, in_specs=[pl.BlockSpec(memory_space=pl.ANY)] * raw +...  12.6 us
    ppermute x5, starting transfers between devices, mirrored(): return lax.ppermute(far, ('pipe', 'dp'), pairs)  6.08 us
    ppermute x1, waiting for transfers between devices, per_device(): from_second = lax.ppermute(second, ('pipe', 'tensor'), cross)  5.52 us
    ppermute x3, starting transfers between devices, across(): lax.ppermute(arrays[k], 'dp', [(i, i ^ k) for i in range(groups)])  4.51 us
    unnamed x18, local copies, waits for them, and re-layouts  4.39 us
    ppermute x1, starting transfers between devices, per_device(): from_second = lax.ppermute(second, ('pipe', 'tensor'), cross)  1.41 us
  transfers between devices with their start and end apart: 22, of which 8 were waited for; matrix products, arithmetic and copies ran while one was open for 0% of the time, Pallas kernels for 9%

profile of v3, /device:TPU:0, one launch (start us, length us, event | category | flops | bytes accessed | tf_op | source)
XLA Modules:
  0.0 66.4 jit_solution(12925607721974414301)
XLA Ops:
  0.7 4.9 %first_partials.1 = (bf16[32,1152]{1,0:T(8,128)(2,1)}, bf16[32,1152]{1,0:T(8,128)(2,1)}, bf16[32,1152]{1,0:T(8,128)(2,1)}, bf16[32,1152]{1,0:T(8,128)(2,1)}) custom-call(bf16[1,4,1280,256]{3,2,1,0:T(8,128)(2,1)} %refs_0_.5, bf16[1,4,256,1280]{3,2,1,0:T(8,128)(2,1)} %refs_1_.5, f32[1,4,1280]{2,1,0:T(4,128)} %refs_6_.5, bf16[1,4,32,1280]{3,2,1,0:T(8,128)(2,1)} %refs_7_.4, ...), custom_call_target="tpu_custom_call" | custom-call | flops 5500000256 | tf_op jit(solution)/shard_map/first_partials/pallas_call | solution.py:52
  5.6 0.9 %copy-done.8 = bf16[32,1152]{1,0:T(8,128)(2,1)S(1)} copy-done((bf16[32,1152]{1,0:T(8,128)(2,1)S(1)}, bf16[32,1152]{1,0:T(8,128)(2,1)}, u32[]{:S(2)}) %copy-start.8) | copy-done | bytes 73752
  6.6 2.5 %collective-permute-start.11 = (bf16[2,32,3840]{2,1,0:T(8,128)(2,1)S(1)}, bf16[2,32,3840]{2,1,0:T(8,128)(2,1)S(1)}, u32[]{:S(2)}, u32[]{:S(2)}) collective-permute-start(bf16[2,32,3840]{2,1,0:T(8,128)(2,1)S(1)} %get-tuple-element.49), channel_id=1, source_target_pairs={{0,24},{1,25},{8,16},{9,17},{16,8},{17,9},{24,0},{25,1},{2,26},{3,... | collective-permute-start | bytes 1474568 | tf_op jit(solution)/shard_map/ppermute | solution.py:568
  9.1 1.6 %collective-permute-start = (bf16[32,1152]{1,0:T(8,128)(2,1)}, bf16[32,1152]{1,0:T(8,128)(2,1)S(1)}, u32[]{:S(2)}, u32[]{:S(2)}) collective-permute-start(bf16[32,1152]{1,0:T(8,128)(2,1)} %get-tuple-element.35.refs_4_.refs_2_), channel_id=1, source_target_pairs={{0,2},{2,0},{4,6},{6,4},{1,3},{3,1},{5,7},{7,5},{8,10},{10,8},{12,... | collective-permute-start | bytes 221192 | tf_op jit(solution)/shard_map/ppermute | solution.py:558
  10.7 2.6 %collective-permute-start.1 = (bf16[32,1152]{1,0:T(8,128)(2,1)}, bf16[32,1152]{1,0:T(8,128)(2,1)S(1)}, u32[]{:S(2)}, u32[]{:S(2)}) collective-permute-start(bf16[32,1152]{1,0:T(8,128)(2,1)} %get-tuple-element.37), channel_id=1, source_target_pairs={{0,4},{2,6},{4,0},{6,2},{1,5},{3,7},{5,1},{7,3},{8,12},{10,14},{12... | collective-permute-start | bytes 221192 | tf_op jit(solution)/shard_map/ppermute | solution.py:558
  13.5 1.7 %copy-done.1 = bf16[1,4,1280,256]{3,2,1,0:T(8,128)(2,1)S(1)} copy-done((bf16[1,4,1280,256]{3,2,1,0:T(8,128)(2,1)S(1)}, bf16[1,4,1280,256]{3,2,1,0:T(8,128)(2,1)}, u32[]{:S(2)}) %copy-start.1) | copy-done | bytes 2621464
  15.2 1.7 %copy-done.2 = bf16[1,4,256,1280]{3,2,1,0:T(8,128)(2,1)S(1)} copy-done((bf16[1,4,256,1280]{3,2,1,0:T(8,128)(2,1)S(1)}, bf16[1,4,256,1280]{3,2,1,0:T(8,128)(2,1)}, u32[]{:S(2)}) %copy-start.2) | copy-done | bytes 2621464
  17.4 2.5 %collective-permute-done.1.refs_2_ = bf16[32,1152]{1,0:T(8,128)(2,1)S(1)} collective-permute-done((bf16[32,1152]{1,0:T(8,128)(2,1)}, bf16[32,1152]{1,0:T(8,128)(2,1)S(1)}, u32[]{:S(2)}, u32[]{:S(2)}) %collective-permute-start.1) | collective-permute-done | bytes 73760 | tf_op jit(solution)/shard_map/ppermute | solution.py:558
  20.2 1.8 %collective-permute-start.3 = (bf16[32,1152]{1,0:T(8,128)(2,1)S(1)}, bf16[32,1152]{1,0:T(8,128)(2,1)S(1)}, u32[]{:S(2)}, u32[]{:S(2)}) collective-permute-start(bf16[32,1152]{1,0:T(8,128)(2,1)S(1)} %get-tuple-element.41.refs_0_), channel_id=1, source_target_pairs={{0,2},{2,0},{4,6},{6,4},{1,3},{3,1},{5,7},{7,5},{8,10},{10,8},{12,... | collective-permute-start | bytes 221192 | tf_op jit(solution)/shard_map/ppermute | solution.py:558
  21.9 1.5 %collective-permute-start.4 = (bf16[32,1152]{1,0:T(8,128)(2,1)S(1)}, bf16[32,1152]{1,0:T(8,128)(2,1)S(1)}, u32[]{:S(2)}, u32[]{:S(2)}) collective-permute-start(bf16[32,1152]{1,0:T(8,128)(2,1)S(1)} %get-tuple-element.41.refs_0_), channel_id=1, source_target_pairs={{0,4},{2,6},{4,0},{6,2},{1,5},{3,7},{5,1},{7,3},{8,12},{10,14},{12... | collective-permute-start | bytes 221192 | tf_op jit(solution)/shard_map/ppermute | solution.py:558
  23.4 1.2 %collective-permute-start.5 = (bf16[32,1152]{1,0:T(8,128)(2,1)S(1)}, bf16[32,1152]{1,0:T(8,128)(2,1)S(1)}, u32[]{:S(2)}, u32[]{:S(2)}) collective-permute-start(bf16[32,1152]{1,0:T(8,128)(2,1)S(1)} %get-tuple-element.41.refs_0_), channel_id=1, source_target_pairs={{0,6},{2,4},{4,2},{6,0},{1,7},{3,5},{5,3},{7,1},{8,14},{10,12},{12... | collective-permute-start | bytes 221192 | tf_op jit(solution)/shard_map/ppermute | solution.py:558
  24.8 1.6 %collective-permute-start.12 = (bf16[4,32,2560]{2,1,0:T(8,128)(2,1)S(1)}, bf16[4,32,2560]{2,1,0:T(8,128)(2,1)S(1)}, u32[]{:S(2)}, u32[]{:S(2)}) collective-permute-start(bf16[4,32,2560]{2,1,0:T(8,128)(2,1)S(1)} %get-tuple-element.50), channel_id=1, source_target_pairs={{0,1},{1,0},{2,3},{3,2},{4,5},{5,4},{6,7},{7,6},{8,9},{9,8},{10,11... | collective-permute-start | bytes 1966088 | tf_op jit(solution)/shard_map/ppermute | solution.py:572
  26.3 4.1 %collective-permute-done.4.refs_2_ = bf16[32,1152]{1,0:T(8,128)(2,1)S(1)} collective-permute-done((bf16[32,1152]{1,0:T(8,128)(2,1)S(1)}, bf16[32,1152]{1,0:T(8,128)(2,1)S(1)}, u32[]{:S(2)}, u32[]{:S(2)}) %collective-permute-start.4) | collective-permute-done | bytes 73760 | tf_op jit(solution)/shard_map/ppermute | solution.py:558
  30.4 0.7 %second_results.1.refs_10_.refs_2_ = bf16[4,32,1280]{2,1,0:T(8,128)(2,1)S(1)} custom-call(bf16[32,1152]{1,0:T(8,128)(2,1)S(1)} %get-tuple-element.41.refs_0_, bf16[32,1152]{1,0:T(8,128)(2,1)S(1)} %collective-permute-done.3.refs_1_, bf16[32,1152]{1,0:T(8,128)(2,1)S(1)} %collective-permute-done.4.refs_2_, bf16[32,1152]{1,0:T(8,128)(2,1)S(1)} %collective-permute-done.5.refs_3_, ...), custom_call_target="tpu_custom_call" | custom-call | flops 880000000 | tf_op jit(solution)/shard_map/second_results/pallas_call | solution.py:52
  31.2 0.7 %first_results.1 = (bf16[4,32,1280]{2,1,0:T(8,128)(2,1)S(1)}, bf16[4,32,768]{2,1,0:T(8,128)(2,1)S(1)}) custom-call(bf16[32,1152]{1,0:T(8,128)(2,1)S(1)} %get-tuple-element.41.refs_0_, bf16[32,1152]{1,0:T(8,128)(2,1)S(1)} %collective-permute-done.3.refs_1_, bf16[32,1152]{1,0:T(8,128)(2,1)S(1)} %collective-permute-done.4.refs_2_, ...), custom_call_target="tpu_custom_call" | custom-call | flops 880000000 | tf_op jit(solution)/shard_map/first_results/pallas_call | solution.py:52
  32.0 1.4 %collective-permute-start.7 = (bf16[4,32,1280]{2,1,0:T(8,128)(2,1)S(1)}, bf16[4,32,1280]{2,1,0:T(8,128)(2,1)S(1)}, u32[]{:S(2)}, u32[]{:S(2)}) collective-permute-start(bf16[4,32,1280]{2,1,0:T(8,128)(2,1)S(1)} %second_results.1.refs_10_.refs_2_), channel_id=1, source_target_pairs={{0,2},{2,0},{4,6},{6,4},{8,16},{10,18},{12,20},{14,22},{16,8},{18,... | collective-permute-start | bytes 983048 | tf_op jit(solution)/shard_map/ppermute | solution.py:595
  33.6 5.5 %collective-permute-done.7.refs_1_ = bf16[4,32,1280]{2,1,0:T(8,128)(2,1)S(1)} collective-permute-done((bf16[4,32,1280]{2,1,0:T(8,128)(2,1)S(1)}, bf16[4,32,1280]{2,1,0:T(8,128)(2,1)S(1)}, u32[]{:S(2)}, u32[]{:S(2)}) %collective-permute-start.7) | collective-permute-done | bytes 327712 | tf_op jit(solution)/shard_map/ppermute | solution.py:595
  39.1 1.3 %later_partials.1 = (bf16[32,640]{1,0:T(8,128)(2,1)S(1)}, bf16[32,640]{1,0:T(8,128)(2,1)S(1)}, bf16[32,640]{1,0:T(8,128)(2,1)S(1)}, bf16[32,640]{1,0:T(8,128)(2,...) custom-call(bf16[4,32,1280]{2,1,0:T(8,128)(2,1)S(1)} %collective-permute-done.6.refs_0_, ...), custom_call_target="tpu_custom_call" | custom-call | flops 1430000000 | tf_op jit(solution)/shard_map/later_partials/pallas_call | solution.py:52
  40.5 1.4 %collective-permute-start.8 = (bf16[32,640]{1,0:T(8,128)(2,1)S(1)}, bf16[32,640]{1,0:T(8,128)(2,1)S(1)}, u32[]{:S(2)}, u32[]{:S(2)}) collective-permute-start(bf16[32,640]{1,0:T(8,128)(2,1)S(1)} %get-tuple-element.45), channel_id=1, source_target_pairs={{0,2},{2,0},{4,6},{6,4},{1,3},{3,1},{5,7},{7,5},{8,10},{10,8},{12,... | collective-permute-start | bytes 122888 | tf_op jit(solution)/shard_map/ppermute | solution.py:558
  41.9 1.5 %collective-permute-start.9 = (bf16[32,640]{1,0:T(8,128)(2,1)S(1)}, bf16[32,640]{1,0:T(8,128)(2,1)S(1)}, u32[]{:S(2)}, u32[]{:S(2)}) collective-permute-start(bf16[32,640]{1,0:T(8,128)(2,1)S(1)} %get-tuple-element.46), channel_id=1, source_target_pairs={{0,4},{2,6},{4,0},{6,2},{1,5},{3,7},{5,1},{7,3},{8,12},{10,14},{12... | collective-permute-start | bytes 122888 | tf_op jit(solution)/shard_map/ppermute | solution.py:558
  43.4 1.5 %collective-permute-start.10 = (bf16[32,640]{1,0:T(8,128)(2,1)S(1)}, bf16[32,640]{1,0:T(8,128)(2,1)S(1)}, u32[]{:S(2)}, u32[]{:S(2)}) collective-permute-start(bf16[32,640]{1,0:T(8,128)(2,1)S(1)} %get-tuple-element.47), channel_id=1, source_target_pairs={{0,6},{2,4},{4,2},{6,0},{1,7},{3,5},{5,3},{7,1},{8,14},{10,12},{12... | collective-permute-start | bytes 122888 | tf_op jit(solution)/shard_map/ppermute | solution.py:558
  45.0 1.5 %collective-permute-start.16 = (bf16[2,32,1792]{2,1,0:T(8,128)(2,1)S(1)}, bf16[2,32,1792]{2,1,0:T(8,128)(2,1)S(1)}, u32[]{:S(2)}, u32[]{:S(2)}) collective-permute-start(bf16[2,32,1792]{2,1,0:T(8,128)(2,1)S(1)} %get-tuple-element.56), channel_id=1, source_target_pairs={{0,1},{1,0},{2,3},{3,2},{4,5},{5,4},{6,7},{7,6},{8,9},{9,8},{10,11... | collective-permute-start | bytes 688136 | tf_op jit(solution)/shard_map/ppermute | solution.py:572
  46.5 1.7 %collective-permute-start.18 = (bf16[2,32,1792]{2,1,0:T(8,128)(2,1)S(1)}, bf16[2,32,1792]{2,1,0:T(8,128)(2,1)S(1)}, u32[]{:S(2)}, u32[]{:S(2)}) collective-permute-start(bf16[2,32,1792]{2,1,0:T(8,128)(2,1)S(1)} %get-tuple-element.58), channel_id=1, source_target_pairs={{0,25},{1,24},{8,17},{9,16},{16,9},{17,8},{24,1},{25,0},{2,27},{3,... | collective-permute-start | bytes 688136 | tf_op jit(solution)/shard_map/ppermute | solution.py:568
  48.3 0.9 %collective-permute-done.10.refs_3_ = bf16[32,640]{1,0:T(8,128)(2,1)S(1)} collective-permute-done((bf16[32,640]{1,0:T(8,128)(2,1)S(1)}, bf16[32,640]{1,0:T(8,128)(2,1)S(1)}, u32[]{:S(2)}, u32[]{:S(2)}) %collective-permute-start.10) | collective-permute-done | bytes 40992 | tf_op jit(solution)/shard_map/ppermute | solution.py:558
  49.5 2.2 %collective-permute-start.14 = (bf16[32,640]{1,0:T(8,128)(2,1)S(1)}, bf16[32,640]{1,0:T(8,128)(2,1)S(1)}, u32[]{:S(2)}, u32[]{:S(2)}) collective-permute-start(bf16[32,640]{1,0:T(8,128)(2,1)S(1)} %later_latents.1.refs_0_), channel_id=1, source_target_pairs={{0,4},{2,6},{4,0},{6,2},{1,5},{3,7},{5,1},{7,3},{8,12},{10,14},{12... | collective-permute-start | bytes 122888 | tf_op jit(solution)/shard_map/ppermute | solution.py:558
  51.7 1.8 %collective-permute-done.13.refs_1_ = bf16[32,640]{1,0:T(8,128)(2,1)S(1)} collective-permute-done((bf16[32,640]{1,0:T(8,128)(2,1)S(1)}, bf16[32,640]{1,0:T(8,128)(2,1)S(1)}, u32[]{:S(2)}, u32[]{:S(2)}) %collective-permute-start.13) | collective-permute-done | bytes 40992 | tf_op jit(solution)/shard_map/ppermute | solution.py:558
  53.5 1.6 %collective-permute-start.15 = (bf16[32,640]{1,0:T(8,128)(2,1)S(1)}, bf16[32,640]{1,0:T(8,128)(2,1)S(1)}, u32[]{:S(2)}, u32[]{:S(2)}) collective-permute-start(bf16[32,640]{1,0:T(8,128)(2,1)S(1)} %later_latents.1.refs_0_), channel_id=1, source_target_pairs={{0,6},{2,4},{4,2},{6,0},{1,7},{3,5},{5,3},{7,1},{8,14},{10,12},{12... | collective-permute-start | bytes 122888 | tf_op jit(solution)/shard_map/ppermute | solution.py:558
  55.1 4.2 %collective-permute-done.15.refs_3_ = bf16[32,640]{1,0:T(8,128)(2,1)S(1)} collective-permute-done((bf16[32,640]{1,0:T(8,128)(2,1)S(1)}, bf16[32,640]{1,0:T(8,128)(2,1)S(1)}, u32[]{:S(2)}, u32[]{:S(2)}) %collective-permute-start.15) | collective-permute-done | bytes 40992 | tf_op jit(solution)/shard_map/ppermute | solution.py:558
  59.3 1.4 %collective-permute-start.19 = (bf16[2,32,256]{2,1,0:T(8,128)(2,1)S(1)}, bf16[2,32,256]{2,1,0:T(8,128)(2,1)S(1)}, u32[]{:S(2)}, u32[]{:S(2)}) collective-permute-start(bf16[2,32,256]{2,1,0:T(8,128)(2,1)S(1)} %get-tuple-element.61.refs_6_), channel_id=1, source_target_pairs={{0,1},{1,0},{2,3},{3,2},{4,5},{5,4},{6,7},{7,6},{8,9},{9,8},{10,11... | collective-permute-start | bytes 98312 | tf_op jit(solution)/shard_map/ppermute | solution.py:572
  60.7 1.9 %collective-permute-start.21 = (bf16[2,32,256]{2,1,0:T(8,128)(2,1)S(1)}, bf16[2,32,256]{2,1,0:T(8,128)(2,1)S(1)}, u32[]{:S(2)}, u32[]{:S(2)}) collective-permute-start(bf16[2,32,256]{2,1,0:T(8,128)(2,1)S(1)} %get-tuple-element.62), channel_id=1, source_target_pairs={{0,25},{1,24},{8,17},{9,16},{16,9},{17,8},{24,1},{25,0},{2,27},{3,... | collective-permute-start | bytes 98312 | tf_op jit(solution)/shard_map/ppermute | solution.py:568
  62.6 2.3 %last_results.1 = (bf16[1,4,32,1280]{3,2,1,0:T(8,128)(2,1)}, bf16[1,4,32,1280]{3,2,1,0:T(8,128)(2,1)}, f32[1,2,128,1280]{3,2,1,0:T(8,128)}) custom-call(bf16[32,640]{1,0:T(8,128)(2,1)S(1)} %later_latents.1.refs_0_, bf16[32,640]{1,0:T(8,128)(2,1)S(1)} %collective-permute-done.13.refs_1_, bf16[32,640]{1,0:T(8,128)(2,1)S(1)} %collective-permute-done.14.refs_2_, ...), custom_call_target="tpu_custom_call" | custom-call | flops 220000000 | tf_op jit(solution)/shard_map/last_results/pallas_call | solution.py:52
  65.0 1.4 %down_grads.1 = f32[1,2,640,256]{3,2,1,0:T(8,128)} custom-call(bf16[4,32,2560]{2,1,0:T(8,128)(2,1)S(1)} %get-tuple-element.53.refs_10_.refs_0_, bf16[4,32,2560]{2,1,0:T(8,128)(2,1)S(1)} %collective-permute-done.12.refs_0_.refs_11_.refs_1_, bf16[2,32,1792]{2,1,0:T(8,128)(2,1)S(1)} %get-tuple-element.55.refs_12_.refs_2_, ...), custom_call_target="tpu_custom_call" | custom-call | flops 1650000000 | tf_op jit(solution)/shard_map/down_grads/pallas_call | solution.py:52
  (44 shorter events, 1.9 us)
Async XLA Ops:
  0.6 5.0 %copy-start.5 = (f32[1,4,1280]{2,1,0:T(4,128)S(1)}, f32[1,4,1280]{2,1,0:T(4,128)}, u32[]{:S(2)}) copy-start(f32[1,4,1280]{2,1,0:T(4,128)} %refs_6_.5) | copy-start | bytes 61444
  0.6 5.0 %copy-start = (bf16[2,1,4,32,1280]{4,3,2,1,0:T(8,128)(2,1)S(1)}, bf16[2,1,4,32,1280]{4,3,2,1,0:T(8,128)(2,1)}, u32[]{:S(2)}) copy-start(bf16[2,1,4,32,1280]{4,3,2,1,0:T(8,128)(2,1)} %refs_8_.5) | copy-start | bytes 1966084
  0.7 4.9 %copy-start.3 = (bf16[1,4,32,1280]{3,2,1,0:T(8,128)(2,1)S(1)}, bf16[1,4,32,1280]{3,2,1,0:T(8,128)(2,1)}, u32[]{:S(2)}) copy-start(bf16[1,4,32,1280]{3,2,1,0:T(8,128)(2,1)} %refs_9_.3) | copy-start | bytes 983044
  5.6 0.9 %copy-start.8 = (bf16[32,1152]{1,0:T(8,128)(2,1)S(1)}, bf16[32,1152]{1,0:T(8,128)(2,1)}, u32[]{:S(2)}) copy-start(bf16[32,1152]{1,0:T(8,128)(2,1)} %get-tuple-element.34.refs_3_) | copy-start | bytes 221188
  6.6 18.0 %collective-permute-start.11 = (bf16[2,32,3840]{2,1,0:T(8,128)(2,1)S(1)}, bf16[2,32,3840]{2,1,0:T(8,128)(2,1)S(1)}, u32[]{:S(2)}, u32[]{:S(2)}) collective-permute-start(bf16[2,32,3840]{2,1,0:T(8,128)(2,1)S(1)} %get-tuple-element.49), channel_id=1, source_target_pairs={{0,24},{1,25},{8,16},{9,17},{16,8},{17,9},{24,0},{25,1},{2,26},{3,... | collective-permute-start | bytes 1474568 | tf_op jit(solution)/shard_map/ppermute | solution.py:568
  9.1 8.3 %collective-permute-start = (bf16[32,1152]{1,0:T(8,128)(2,1)}, bf16[32,1152]{1,0:T(8,128)(2,1)S(1)}, u32[]{:S(2)}, u32[]{:S(2)}) collective-permute-start(bf16[32,1152]{1,0:T(8,128)(2,1)} %get-tuple-element.35.refs_4_.refs_2_), channel_id=1, source_target_pairs={{0,2},{2,0},{4,6},{6,4},{1,3},{3,1},{5,7},{7,5},{8,10},{10,8},{12,... | collective-permute-start | bytes 221192 | tf_op jit(solution)/shard_map/ppermute | solution.py:558
  10.7 9.2 %collective-permute-start.1 = (bf16[32,1152]{1,0:T(8,128)(2,1)}, bf16[32,1152]{1,0:T(8,128)(2,1)S(1)}, u32[]{:S(2)}, u32[]{:S(2)}) collective-permute-start(bf16[32,1152]{1,0:T(8,128)(2,1)} %get-tuple-element.37), channel_id=1, source_target_pairs={{0,4},{2,6},{4,0},{6,2},{1,5},{3,7},{5,1},{7,3},{8,12},{10,14},{12... | collective-permute-start | bytes 221192 | tf_op jit(solution)/shard_map/ppermute | solution.py:558
  13.3 6.6 %collective-permute-start.2 = (bf16[32,1152]{1,0:T(8,128)(2,1)}, bf16[32,1152]{1,0:T(8,128)(2,1)S(1)}, u32[]{:S(2)}, u32[]{:S(2)}) collective-permute-start(bf16[32,1152]{1,0:T(8,128)(2,1)} %get-tuple-element.38), channel_id=1, source_target_pairs={{0,6},{2,4},{4,2},{6,0},{1,7},{3,5},{5,3},{7,1},{8,14},{10,12},{12... | collective-permute-start | bytes 221192 | tf_op jit(solution)/shard_map/ppermute | solution.py:558
  13.5 1.7 %copy-start.1 = (bf16[1,4,1280,256]{3,2,1,0:T(8,128)(2,1)S(1)}, bf16[1,4,1280,256]{3,2,1,0:T(8,128)(2,1)}, u32[]{:S(2)}) copy-start(bf16[1,4,1280,256]{3,2,1,0:T(8,128)(2,1)} %refs_0_.5) | copy-start | bytes 7864324
  15.2 1.7 %copy-start.2 = (bf16[1,4,256,1280]{3,2,1,0:T(8,128)(2,1)S(1)}, bf16[1,4,256,1280]{3,2,1,0:T(8,128)(2,1)}, u32[]{:S(2)}) copy-start(bf16[1,4,256,1280]{3,2,1,0:T(8,128)(2,1)} %refs_1_.5) | copy-start | bytes 7864324
  17.4 13.1 %copy-start.4 = (bf16[1,4,32,1280]{3,2,1,0:T(8,128)(2,1)S(1)}, bf16[1,4,32,1280]{3,2,1,0:T(8,128)(2,1)}, u32[]{:S(2)}) copy-start(bf16[1,4,32,1280]{3,2,1,0:T(8,128)(2,1)} %refs_7_.4) | copy-start | bytes 983044
  20.2 6.2 %collective-permute-start.3 = (bf16[32,1152]{1,0:T(8,128)(2,1)S(1)}, bf16[32,1152]{1,0:T(8,128)(2,1)S(1)}, u32[]{:S(2)}, u32[]{:S(2)}) collective-permute-start(bf16[32,1152]{1,0:T(8,128)(2,1)S(1)} %get-tuple-element.41.refs_0_), channel_id=1, source_target_pairs={{0,2},{2,0},{4,6},{6,4},{1,3},{3,1},{5,7},{7,5},{8,10},{10,8},{12,... | collective-permute-start | bytes 221192 | tf_op jit(solution)/shard_map/ppermute | solution.py:558
  21.9 8.5 %collective-permute-start.4 = (bf16[32,1152]{1,0:T(8,128)(2,1)S(1)}, bf16[32,1152]{1,0:T(8,128)(2,1)S(1)}, u32[]{:S(2)}, u32[]{:S(2)}) collective-permute-start(bf16[32,1152]{1,0:T(8,128)(2,1)S(1)} %get-tuple-element.41.refs_0_), channel_id=1, source_target_pairs={{0,4},{2,6},{4,0},{6,2},{1,5},{3,7},{5,1},{7,3},{8,12},{10,14},{12... | collective-permute-start | bytes 221192 | tf_op jit(solution)/shard_map/ppermute | solution.py:558
  23.4 7.0 %collective-permute-start.5 = (bf16[32,1152]{1,0:T(8,128)(2,1)S(1)}, bf16[32,1152]{1,0:T(8,128)(2,1)S(1)}, u32[]{:S(2)}, u32[]{:S(2)}) collective-permute-start(bf16[32,1152]{1,0:T(8,128)(2,1)S(1)} %get-tuple-element.41.refs_0_), channel_id=1, source_target_pairs={{0,6},{2,4},{4,2},{6,0},{1,7},{3,5},{5,3},{7,1},{8,14},{10,12},{12... | collective-permute-start | bytes 221192 | tf_op jit(solution)/shard_map/ppermute | solution.py:558
  24.8 21.8 %collective-permute-start.12 = (bf16[4,32,2560]{2,1,0:T(8,128)(2,1)S(1)}, bf16[4,32,2560]{2,1,0:T(8,128)(2,1)S(1)}, u32[]{:S(2)}, u32[]{:S(2)}) collective-permute-start(bf16[4,32,2560]{2,1,0:T(8,128)(2,1)S(1)} %get-tuple-element.50), channel_id=1, source_target_pairs={{0,1},{1,0},{2,3},{3,2},{4,5},{5,4},{6,7},{7,6},{8,9},{9,8},{10,11... | collective-permute-start | bytes 1966088 | tf_op jit(solution)/shard_map/ppermute | solution.py:572
  31.2 8.0 %copy-start.6 = (bf16[1,2,32,1280]{3,2,1,0:T(8,128)(2,1)S(1)}, bf16[1,2,32,1280]{3,2,1,0:T(8,128)(2,1)}, u32[]{:S(2)}) copy-start(bf16[1,2,32,1280]{3,2,1,0:T(8,128)(2,1)} %refs_3_.3) | copy-start | bytes 491524
  31.2 8.0 %copy-start.7 = (bf16[1,2,32,1280]{3,2,1,0:T(8,128)(2,1)S(1)}, bf16[1,2,32,1280]{3,2,1,0:T(8,128)(2,1)}, u32[]{:S(2)}) copy-start(bf16[1,2,32,1280]{3,2,1,0:T(8,128)(2,1)} %refs_4_.3) | copy-start | bytes 491524
  31.9 1.7 %collective-permute-start.6 = (bf16[4,32,1280]{2,1,0:T(8,128)(2,1)S(1)}, bf16[4,32,1280]{2,1,0:T(8,128)(2,1)S(1)}, u32[]{:S(2)}, u32[]{:S(2)}) collective-permute-start(bf16[4,32,1280]{2,1,0:T(8,128)(2,1)S(1)} %get-tuple-element.43), channel_id=1, source_target_pairs={{0,8},{8,0},{16,24},{24,16},{1,9},{9,1},{17,25},{25,17},{2,10},{10... | collective-permute-start | bytes 983048 | tf_op jit(solution)/shard_map/ppermute | solution.py:599
  32.0 7.1 %collective-permute-start.7 = (bf16[4,32,1280]{2,1,0:T(8,128)(2,1)S(1)}, bf16[4,32,1280]{2,1,0:T(8,128)(2,1)S(1)}, u32[]{:S(2)}, u32[]{:S(2)}) collective-permute-start(bf16[4,32,1280]{2,1,0:T(8,128)(2,1)S(1)} %second_results.1.refs_10_.refs_2_), channel_id=1, source_target_pairs={{0,2},{2,0},{4,6},{6,4},{8,16},{10,18},{12,20},{14,22},{16,8},{18,... | collective-permute-start | bytes 983048 | tf_op jit(solution)/shard_map/ppermute | solution.py:595
  40.5 6.1 %collective-permute-start.8 = (bf16[32,640]{1,0:T(8,128)(2,1)S(1)}, bf16[32,640]{1,0:T(8,128)(2,1)S(1)}, u32[]{:S(2)}, u32[]{:S(2)}) collective-permute-start(bf16[32,640]{1,0:T(8,128)(2,1)S(1)} %get-tuple-element.45), channel_id=1, source_target_pairs={{0,2},{2,0},{4,6},{6,4},{1,3},{3,1},{5,7},{7,5},{8,10},{10,8},{12,... | collective-permute-start | bytes 122888 | tf_op jit(solution)/shard_map/ppermute | solution.py:558
  41.9 6.4 %collective-permute-start.9 = (bf16[32,640]{1,0:T(8,128)(2,1)S(1)}, bf16[32,640]{1,0:T(8,128)(2,1)S(1)}, u32[]{:S(2)}, u32[]{:S(2)}) collective-permute-start(bf16[32,640]{1,0:T(8,128)(2,1)S(1)} %get-tuple-element.46), channel_id=1, source_target_pairs={{0,4},{2,6},{4,0},{6,2},{1,5},{3,7},{5,1},{7,3},{8,12},{10,14},{12... | collective-permute-start | bytes 122888 | tf_op jit(solution)/shard_map/ppermute | solution.py:558
  43.4 5.8 %collective-permute-start.10 = (bf16[32,640]{1,0:T(8,128)(2,1)S(1)}, bf16[32,640]{1,0:T(8,128)(2,1)S(1)}, u32[]{:S(2)}, u32[]{:S(2)}) collective-permute-start(bf16[32,640]{1,0:T(8,128)(2,1)S(1)} %get-tuple-element.47), channel_id=1, source_target_pairs={{0,6},{2,4},{4,2},{6,0},{1,7},{3,5},{5,3},{7,1},{8,14},{10,12},{12... | collective-permute-start | bytes 122888 | tf_op jit(solution)/shard_map/ppermute | solution.py:558
  45.0 15.7 %collective-permute-start.16 = (bf16[2,32,1792]{2,1,0:T(8,128)(2,1)S(1)}, bf16[2,32,1792]{2,1,0:T(8,128)(2,1)S(1)}, u32[]{:S(2)}, u32[]{:S(2)}) collective-permute-start(bf16[2,32,1792]{2,1,0:T(8,128)(2,1)S(1)} %get-tuple-element.56), channel_id=1, source_target_pairs={{0,1},{1,0},{2,3},{3,2},{4,5},{5,4},{6,7},{7,6},{8,9},{9,8},{10,11... | collective-permute-start | bytes 688136 | tf_op jit(solution)/shard_map/ppermute | solution.py:572
  46.5 16.1 %collective-permute-start.17 = (bf16[2,32,1792]{2,1,0:T(8,128)(2,1)S(1)}, bf16[2,32,1792]{2,1,0:T(8,128)(2,1)S(1)}, u32[]{:S(2)}, u32[]{:S(2)}) collective-permute-start(bf16[2,32,1792]{2,1,0:T(8,128)(2,1)S(1)} %get-tuple-element.57), channel_id=1, source_target_pairs={{0,24},{1,25},{8,16},{9,17},{16,8},{17,9},{24,0},{25,1},{2,26},{3,... | collective-permute-start | bytes 688136 | tf_op jit(solution)/shard_map/ppermute | solution.py:568
  46.5 16.1 %collective-permute-start.18 = (bf16[2,32,1792]{2,1,0:T(8,128)(2,1)S(1)}, bf16[2,32,1792]{2,1,0:T(8,128)(2,1)S(1)}, u32[]{:S(2)}, u32[]{:S(2)}) collective-permute-start(bf16[2,32,1792]{2,1,0:T(8,128)(2,1)S(1)} %get-tuple-element.58), channel_id=1, source_target_pairs={{0,25},{1,24},{8,17},{9,16},{16,9},{17,8},{24,1},{25,0},{2,27},{3,... | collective-permute-start | bytes 688136 | tf_op jit(solution)/shard_map/ppermute | solution.py:568
  49.4 4.1 %collective-permute-start.13 = (bf16[32,640]{1,0:T(8,128)(2,1)S(1)}, bf16[32,640]{1,0:T(8,128)(2,1)S(1)}, u32[]{:S(2)}, u32[]{:S(2)}) collective-permute-start(bf16[32,640]{1,0:T(8,128)(2,1)S(1)} %later_latents.1.refs_0_), channel_id=1, source_target_pairs={{0,2},{2,0},{4,6},{6,4},{1,3},{3,1},{5,7},{7,5},{8,10},{10,8},{12,... | collective-permute-start | bytes 122888 | tf_op jit(solution)/shard_map/ppermute | solution.py:558
  49.5 5.6 %collective-permute-start.14 = (bf16[32,640]{1,0:T(8,128)(2,1)S(1)}, bf16[32,640]{1,0:T(8,128)(2,1)S(1)}, u32[]{:S(2)}, u32[]{:S(2)}) collective-permute-start(bf16[32,640]{1,0:T(8,128)(2,1)S(1)} %later_latents.1.refs_0_), channel_id=1, source_target_pairs={{0,4},{2,6},{4,0},{6,2},{1,5},{3,7},{5,1},{7,3},{8,12},{10,14},{12... | collective-permute-start | bytes 122888 | tf_op jit(solution)/shard_map/ppermute | solution.py:558
  53.5 5.8 %collective-permute-start.15 = (bf16[32,640]{1,0:T(8,128)(2,1)S(1)}, bf16[32,640]{1,0:T(8,128)(2,1)S(1)}, u32[]{:S(2)}, u32[]{:S(2)}) collective-permute-start(bf16[32,640]{1,0:T(8,128)(2,1)S(1)} %later_latents.1.refs_0_), channel_id=1, source_target_pairs={{0,6},{2,4},{4,2},{6,0},{1,7},{3,5},{5,3},{7,1},{8,14},{10,12},{12... | collective-permute-start | bytes 122888 | tf_op jit(solution)/shard_map/ppermute | solution.py:558
  59.3 5.6 %collective-permute-start.19 = (bf16[2,32,256]{2,1,0:T(8,128)(2,1)S(1)}, bf16[2,32,256]{2,1,0:T(8,128)(2,1)S(1)}, u32[]{:S(2)}, u32[]{:S(2)}) collective-permute-start(bf16[2,32,256]{2,1,0:T(8,128)(2,1)S(1)} %get-tuple-element.61.refs_6_), channel_id=1, source_target_pairs={{0,1},{1,0},{2,3},{3,2},{4,5},{5,4},{6,7},{7,6},{8,9},{9,8},{10,11... | collective-permute-start | bytes 98312 | tf_op jit(solution)/shard_map/ppermute | solution.py:572
  60.7 4.2 %collective-permute-start.20 = (bf16[2,32,256]{2,1,0:T(8,128)(2,1)S(1)}, bf16[2,32,256]{2,1,0:T(8,128)(2,1)S(1)}, u32[]{:S(2)}, u32[]{:S(2)}) collective-permute-start(bf16[2,32,256]{2,1,0:T(8,128)(2,1)S(1)} %get-tuple-element.62), channel_id=1, source_target_pairs={{0,24},{1,25},{8,16},{9,17},{16,8},{17,9},{24,0},{25,1},{2,26},{3,... | collective-permute-start | bytes 98312 | tf_op jit(solution)/shard_map/ppermute | solution.py:568
  60.7 4.2 %collective-permute-start.21 = (bf16[2,32,256]{2,1,0:T(8,128)(2,1)S(1)}, bf16[2,32,256]{2,1,0:T(8,128)(2,1)S(1)}, u32[]{:S(2)}, u32[]{:S(2)}) collective-permute-start(bf16[2,32,256]{2,1,0:T(8,128)(2,1)S(1)} %get-tuple-element.62), channel_id=1, source_target_pairs={{0,25},{1,24},{8,17},{9,16},{16,9},{17,8},{24,1},{25,0},{2,27},{3,... | collective-permute-start | bytes 98312 | tf_op jit(solution)/shard_map/ppermute | solution.py:568

commit v4 on v3

--- a/solution.py
+++ b/solution.py
@@ -18,7 +18,7 @@
     "early_factors": 0.3,
     "held_weights": 0.5,
     "marker": 1.5,
-    "first_latents": 0.3,
+    "first_latents": 4,
     "second_results": 0.8,
     "first_results": 0.8,
     "later_partials": 1.3,
@@ -288,7 +288,7 @@
     )
 
 
-def later_latents(rank, received, held, after):
+def later_latents(rank, received, held):
     parts, chunk = len(received), received[0].shape[0]
 
     def body(*refs):
@@ -302,7 +302,7 @@
         out[:, 2 * rank :] = on_lanes([dss], chunk).astype(BF16)
 
     outs = [((chunk, 2 * rank + LANES), BF16)]
-    return call(body, [*received, held], outs, "later_latents", after=after)[0]
+    return call(body, [*received, held], outs, "later_latents")[0]
 
 
 def slot_results(own, x, kept, dy, gain, w_down, w_up):
@@ -579,9 +579,9 @@
     near, far, own = early_factors(gains, kept, upstream, dealt[0], after=dealt[1:2])
     far = mirrored(far)
 
-    weights = held_weights(w_down, w_up, after=dealt[1:2])
-    message, held = first_latents(ticks, rank, [own] + received[1:], after=[near, weights[0]])
+    message, held = first_latents(ticks, rank, [own] + received[1:], after=[near])
     received = around([message] * parts)
+    weights = held_weights(w_down, w_up, after=[message])
 
     tick = (received, *weights, gains, entry, kept, upstream)
     (second,) = middle_results("second_results", odd, *tick)
@@ -609,9 +609,9 @@
     received = around(dealt)
     near, far = middle_factors(groups, ticks, factors, g, after=[])
     mid = across(near) + [mirrored(far[k], k) for k in range(groups)]
-    message = later_latents(rank, received, held, after=ready)
+    message = later_latents(rank, received, held)
     received = around([message] * parts)
-    near, far = late_factors(slots, rows, rank, received, after=[])
+    near, far = late_factors(slots, rows, rank, received, after=ready)
     late = across([near] * groups) + [mirrored(far, k) for k in range(groups)]
     y, dh, grad_up = last_results(
         groups, received, *weights, gains, x, kept, g, early, mid

time: 66.6 us -> 64.3 us (0.965)
  waiting for transfers between devices: 19.3 us -> 21.9 us
  local copies, waits for them, and re-layouts: 4.39 us -> 1.8 us
  starting transfers between devices: 29.2 us -> 26.8 us
    ppermute x12, waiting for transfers between devices: 13.5 us -> 17.4 us  [around(): lax.ppermute(arrays[k], 'tensor', [(i, i ^ k) for i in range(parts)])]
    unnamed x18 -> x20, local copies, waits for them, and re-layouts: 4.39 us -> 1.8 us
    ppermute x5, starting transfers between devices: 6.08 us -> 4.05 us  [mirrored(): return lax.ppermute(far, ('pipe', 'dp'), pairs)]
    ppermute x1, waiting for transfers between devices: 5.52 us -> 4.39 us  [per_device(): from_second = lax.ppermute(second, ('pipe', 'tensor'), cross)]
  transfers between devices with their start and end apart: 22 -> 22, of which waited for: 8 -> 10; matrix products, arithmetic and copies ran while one was open for 0% -> 0% of each run, Pallas kernels for 9% -> 10%
where the time goes in v4:
time: 64.3 us; the launch traced here: 64 us
  starting transfers between devices  26.8 us (42%)
  waiting for transfers between devices  21.9 us (34%)
  Pallas kernels  12.6 us (20%)
  local copies, waits for them, and re-layouts  1.8 us (3%)
  between operations  0.81 us (1%)
    ppermute x12, waiting for transfers between devices, around(): lax.ppermute(arrays[k], 'tensor', [(i, i ^ k) for i in range(parts)])  17.4 us
    ppermute x12, starting transfers between devices, around(): lax.ppermute(arrays[k], 'tensor', [(i, i ^ k) for i in range(parts)])  17.2 us
    pallas_call x14, Pallas kernels, call(): pl.pallas_call(run, in_specs=[pl.BlockSpec(memory_space=pl.ANY)] * raw +...  12.6 us
    ppermute x3, starting transfers between devices, across(): lax.ppermute(arrays[k], 'dp', [(i, i ^ k) for i in range(groups)])  4.52 us
    ppermute x1, waiting for transfers between devices, per_device(): from_second = lax.ppermute(second, ('pipe', 'tensor'), cross)  4.39 us
    ppermute x5, starting transfers between devices, mirrored(): return lax.ppermute(far, ('pipe', 'dp'), pairs)  4.05 us
    unnamed x20, local copies, waits for them, and re-layouts  1.8 us
  transfers between devices with their start and end apart: 22, of which 10 were waited for; matrix products, arithmetic and copies ran while one was open for 0% of the time, Pallas kernels for 10%

profile of v4, /device:TPU:0, one launch (start us, length us, event | category | flops | bytes accessed | tf_op | source)
XLA Modules:
  0.0 64.0 jit_solution(15825017674539742241)
XLA Ops:
  0.7 4.9 %first_partials.1 = (bf16[32,1152]{1,0:T(8,128)(2,1)}, bf16[32,1152]{1,0:T(8,128)(2,1)}, bf16[32,1152]{1,0:T(8,128)(2,1)}, bf16[32,1152]{1,0:T(8,128)(2,1)}) custom-call(bf16[1,4,1280,256]{3,2,1,0:T(8,128)(2,1)} %refs_0_.5, bf16[1,4,256,1280]{3,2,1,0:T(8,128)(2,1)} %refs_1_.5, f32[1,4,1280]{2,1,0:T(4,128)} %refs_6_.5, bf16[1,4,32,1280]{3,2,1,0:T(8,128)(2,1)} %refs_7_.4, ...), custom_call_target="tpu_custom_call" | custom-call | flops 5500000256 | tf_op jit(solution)/shard_map/first_partials/pallas_call | solution.py:52
  5.6 3.0 %collective-permute-start = (bf16[32,1152]{1,0:T(8,128)(2,1)}, bf16[32,1152]{1,0:T(8,128)(2,1)S(1)}, u32[]{:S(2)}, u32[]{:S(2)}) collective-permute-start(bf16[32,1152]{1,0:T(8,128)(2,1)} %get-tuple-element.35.refs_4_), channel_id=1, source_target_pairs={{0,2},{2,0},{4,6},{6,4},{1,3},{3,1},{5,7},{7,5},{8,10},{10,8},{12,... | collective-permute-start | bytes 221192 | tf_op jit(solution)/shard_map/ppermute | solution.py:558
  8.6 2.6 %collective-permute-start.1 = (bf16[32,1152]{1,0:T(8,128)(2,1)}, bf16[32,1152]{1,0:T(8,128)(2,1)S(1)}, u32[]{:S(2)}, u32[]{:S(2)}) collective-permute-start(bf16[32,1152]{1,0:T(8,128)(2,1)} %get-tuple-element.37), channel_id=1, source_target_pairs={{0,4},{2,6},{4,0},{6,2},{1,5},{3,7},{5,1},{7,3},{8,12},{10,14},{12... | collective-permute-start | bytes 221192 | tf_op jit(solution)/shard_map/ppermute | solution.py:558
  11.2 0.9 %copy-done.8 = bf16[32,1152]{1,0:T(8,128)(2,1)S(1)} copy-done((bf16[32,1152]{1,0:T(8,128)(2,1)S(1)}, bf16[32,1152]{1,0:T(8,128)(2,1)}, u32[]{:S(2)}) %copy-start.8) | copy-done | bytes 73752
  12.1 0.9 %copy-done.9 = bf16[32,1152]{1,0:T(8,128)(2,1)S(1)} copy-done((bf16[32,1152]{1,0:T(8,128)(2,1)S(1)}, bf16[32,1152]{1,0:T(8,128)(2,1)}, u32[]{:S(2)}) %copy-start.9) | copy-done | bytes 73752
  13.6 3.0 %collective-permute-done.1.refs_2_ = bf16[32,1152]{1,0:T(8,128)(2,1)S(1)} collective-permute-done((bf16[32,1152]{1,0:T(8,128)(2,1)}, bf16[32,1152]{1,0:T(8,128)(2,1)S(1)}, u32[]{:S(2)}, u32[]{:S(2)}) %collective-permute-start.1) | collective-permute-done | bytes 73760 | tf_op jit(solution)/shard_map/ppermute | solution.py:558
  16.6 1.1 %collective-permute-done.2.refs_3_ = bf16[32,1152]{1,0:T(8,128)(2,1)S(1)} collective-permute-done((bf16[32,1152]{1,0:T(8,128)(2,1)}, bf16[32,1152]{1,0:T(8,128)(2,1)S(1)}, u32[]{:S(2)}, u32[]{:S(2)}) %collective-permute-start.2) | collective-permute-done | bytes 73760 | tf_op jit(solution)/shard_map/ppermute | solution.py:558
  17.9 1.1 %collective-permute-start.3 = (bf16[32,1152]{1,0:T(8,128)(2,1)S(1)}, bf16[32,1152]{1,0:T(8,128)(2,1)S(1)}, u32[]{:S(2)}, u32[]{:S(2)}) collective-permute-start(bf16[32,1152]{1,0:T(8,128)(2,1)S(1)} %get-tuple-element.40.refs_2_.refs_0_), channel_id=1, source_target_pairs={{0,2},{2,0},{4,6},{6,4},{1,3},{3,1},{5,7},{7,5},{8,10},{10,8},{12,... | collective-permute-start | bytes 221192 | tf_op jit(solution)/shard_map/ppermute | solution.py:558
  19.1 1.7 %collective-permute-start.4 = (bf16[32,1152]{1,0:T(8,128)(2,1)S(1)}, bf16[32,1152]{1,0:T(8,128)(2,1)S(1)}, u32[]{:S(2)}, u32[]{:S(2)}) collective-permute-start(bf16[32,1152]{1,0:T(8,128)(2,1)S(1)} %get-tuple-element.40.refs_2_.refs_0_), channel_id=1, source_target_pairs={{0,4},{2,6},{4,0},{6,2},{1,5},{3,7},{5,1},{7,3},{8,12},{10,14},{12... | collective-permute-start | bytes 221192 | tf_op jit(solution)/shard_map/ppermute | solution.py:558
  20.8 1.6 %collective-permute-start.5 = (bf16[32,1152]{1,0:T(8,128)(2,1)S(1)}, bf16[32,1152]{1,0:T(8,128)(2,1)S(1)}, u32[]{:S(2)}, u32[]{:S(2)}) collective-permute-start(bf16[32,1152]{1,0:T(8,128)(2,1)S(1)} %get-tuple-element.40.refs_2_.refs_0_), channel_id=1, source_target_pairs={{0,6},{2,4},{4,2},{6,0},{1,7},{3,5},{5,3},{7,1},{8,14},{10,12},{12... | collective-permute-start | bytes 221192 | tf_op jit(solution)/shard_map/ppermute | solution.py:558
  22.8 3.0 %collective-permute-done.4.refs_2_ = bf16[32,1152]{1,0:T(8,128)(2,1)S(1)} collective-permute-done((bf16[32,1152]{1,0:T(8,128)(2,1)S(1)}, bf16[32,1152]{1,0:T(8,128)(2,1)S(1)}, u32[]{:S(2)}, u32[]{:S(2)}) %collective-permute-start.4) | collective-permute-done | bytes 73760 | tf_op jit(solution)/shard_map/ppermute | solution.py:558
  25.8 1.2 %collective-permute-done.5.refs_3_ = bf16[32,1152]{1,0:T(8,128)(2,1)S(1)} collective-permute-done((bf16[32,1152]{1,0:T(8,128)(2,1)S(1)}, bf16[32,1152]{1,0:T(8,128)(2,1)S(1)}, u32[]{:S(2)}, u32[]{:S(2)}) %collective-permute-start.5) | collective-permute-done | bytes 73760 | tf_op jit(solution)/shard_map/ppermute | solution.py:558
  27.8 0.7 %first_results.1 = (bf16[4,32,1280]{2,1,0:T(8,128)(2,1)S(1)}, bf16[4,32,768]{2,1,0:T(8,128)(2,1)S(1)}) custom-call(bf16[32,1152]{1,0:T(8,128)(2,1)S(1)} %get-tuple-element.40.refs_2_.refs_0_, bf16[32,1152]{1,0:T(8,128)(2,1)S(1)} %collective-permute-done.3.refs_1_, bf16[32,1152]{1,0:T(8,128)(2,1)S(1)} %collective-permute-done.4.refs_2_, ...), custom_call_target="tpu_custom_call" | custom-call | flops 880000000 | tf_op jit(solution)/shard_map/first_results/pallas_call | solution.py:52
  28.6 1.0 %collective-permute-start.7 = (bf16[4,32,1280]{2,1,0:T(8,128)(2,1)S(1)}, bf16[4,32,1280]{2,1,0:T(8,128)(2,1)S(1)}, u32[]{:S(2)}, u32[]{:S(2)}) collective-permute-start(bf16[4,32,1280]{2,1,0:T(8,128)(2,1)S(1)} %second_results.1.refs_10_.refs_2_), channel_id=1, source_target_pairs={{0,2},{2,0},{4,6},{6,4},{8,16},{10,18},{12,20},{14,22},{16,8},{18,... | collective-permute-start | bytes 983048 | tf_op jit(solution)/shard_map/ppermute | solution.py:595
  29.8 1.6 %collective-permute-start.15 = (bf16[4,32,2560]{2,1,0:T(8,128)(2,1)S(1)}, bf16[4,32,2560]{2,1,0:T(8,128)(2,1)S(1)}, u32[]{:S(2)}, u32[]{:S(2)}) collective-permute-start(bf16[4,32,2560]{2,1,0:T(8,128)(2,1)S(1)} %get-tuple-element.53), channel_id=1, source_target_pairs={{0,1},{1,0},{2,3},{3,2},{4,5},{5,4},{6,7},{7,6},{8,9},{9,8},{10,11... | collective-permute-start | bytes 1966088 | tf_op jit(solution)/shard_map/ppermute | solution.py:572
  31.4 4.4 %collective-permute-done.7.refs_1_ = bf16[4,32,1280]{2,1,0:T(8,128)(2,1)S(1)} collective-permute-done((bf16[4,32,1280]{2,1,0:T(8,128)(2,1)S(1)}, bf16[4,32,1280]{2,1,0:T(8,128)(2,1)S(1)}, u32[]{:S(2)}, u32[]{:S(2)}) %collective-permute-start.7) | collective-permute-done | bytes 327712 | tf_op jit(solution)/shard_map/ppermute | solution.py:595
  35.8 1.3 %later_partials.1 = (bf16[32,640]{1,0:T(8,128)(2,1)S(1)}, bf16[32,640]{1,0:T(8,128)(2,1)S(1)}, bf16[32,640]{1,0:T(8,128)(2,1)S(1)}, bf16[32,640]{1,0:T(8,128)(2,...) custom-call(bf16[4,32,1280]{2,1,0:T(8,128)(2,1)S(1)} %collective-permute-done.6.refs_0_, ...), custom_call_target="tpu_custom_call" | custom-call | flops 1430000000 | tf_op jit(solution)/shard_map/later_partials/pallas_call | solution.py:52
  37.1 1.0 %collective-permute-start.8 = (bf16[32,640]{1,0:T(8,128)(2,1)S(1)}, bf16[32,640]{1,0:T(8,128)(2,1)S(1)}, u32[]{:S(2)}, u32[]{:S(2)}) collective-permute-start(bf16[32,640]{1,0:T(8,128)(2,1)S(1)} %get-tuple-element.45), channel_id=1, source_target_pairs={{0,2},{2,0},{4,6},{6,4},{1,3},{3,1},{5,7},{7,5},{8,10},{10,8},{12,... | collective-permute-start | bytes 122888 | tf_op jit(solution)/shard_map/ppermute | solution.py:558
  38.1 1.8 %collective-permute-start.9 = (bf16[32,640]{1,0:T(8,128)(2,1)S(1)}, bf16[32,640]{1,0:T(8,128)(2,1)S(1)}, u32[]{:S(2)}, u32[]{:S(2)}) collective-permute-start(bf16[32,640]{1,0:T(8,128)(2,1)S(1)} %get-tuple-element.46), channel_id=1, source_target_pairs={{0,4},{2,6},{4,0},{6,2},{1,5},{3,7},{5,1},{7,3},{8,12},{10,14},{12... | collective-permute-start | bytes 122888 | tf_op jit(solution)/shard_map/ppermute | solution.py:558
  39.9 1.6 %collective-permute-start.10 = (bf16[32,640]{1,0:T(8,128)(2,1)S(1)}, bf16[32,640]{1,0:T(8,128)(2,1)S(1)}, u32[]{:S(2)}, u32[]{:S(2)}) collective-permute-start(bf16[32,640]{1,0:T(8,128)(2,1)S(1)} %get-tuple-element.47), channel_id=1, source_target_pairs={{0,6},{2,4},{4,2},{6,0},{1,7},{3,5},{5,3},{7,1},{8,14},{10,12},{12... | collective-permute-start | bytes 122888 | tf_op jit(solution)/shard_map/ppermute | solution.py:558
  41.6 1.6 %collective-permute-start.16 = (bf16[2,32,1792]{2,1,0:T(8,128)(2,1)S(1)}, bf16[2,32,1792]{2,1,0:T(8,128)(2,1)S(1)}, u32[]{:S(2)}, u32[]{:S(2)}) collective-permute-start(bf16[2,32,1792]{2,1,0:T(8,128)(2,1)S(1)} %get-tuple-element.56), channel_id=1, source_target_pairs={{0,1},{1,0},{2,3},{3,2},{4,5},{5,4},{6,7},{7,6},{8,9},{9,8},{10,11... | collective-permute-start | bytes 688136 | tf_op jit(solution)/shard_map/ppermute | solution.py:572
  43.2 1.7 %collective-permute-start.18 = (bf16[2,32,1792]{2,1,0:T(8,128)(2,1)S(1)}, bf16[2,32,1792]{2,1,0:T(8,128)(2,1)S(1)}, u32[]{:S(2)}, u32[]{:S(2)}) collective-permute-start(bf16[2,32,1792]{2,1,0:T(8,128)(2,1)S(1)} %get-tuple-element.58), channel_id=1, source_target_pairs={{0,25},{1,24},{8,17},{9,16},{16,9},{17,8},{24,1},{25,0},{2,27},{3,... | collective-permute-start | bytes 688136 | tf_op jit(solution)/shard_map/ppermute | solution.py:568
  44.9 0.8 %collective-permute-done.10.refs_3_ = bf16[32,640]{1,0:T(8,128)(2,1)S(1)} collective-permute-done((bf16[32,640]{1,0:T(8,128)(2,1)S(1)}, bf16[32,640]{1,0:T(8,128)(2,1)S(1)}, u32[]{:S(2)}, u32[]{:S(2)}) %collective-permute-start.10) | collective-permute-done | bytes 40992 | tf_op jit(solution)/shard_map/ppermute | solution.py:558
  46.0 4.0 %collective-permute-done.11.refs_1_ = bf16[32,640]{1,0:T(8,128)(2,1)S(1)} collective-permute-done((bf16[32,640]{1,0:T(8,128)(2,1)S(1)}, bf16[32,640]{1,0:T(8,128)(2,1)S(1)}, u32[]{:S(2)}, u32[]{:S(2)}) %collective-permute-start.11) | collective-permute-done | bytes 40992 | tf_op jit(solution)/shard_map/ppermute | solution.py:558
  50.0 1.1 %collective-permute-start.12 = (bf16[32,640]{1,0:T(8,128)(2,1)S(1)}, bf16[32,640]{1,0:T(8,128)(2,1)S(1)}, u32[]{:S(2)}, u32[]{:S(2)}) collective-permute-start(bf16[32,640]{1,0:T(8,128)(2,1)S(1)} %later_latents.1.refs_0_), channel_id=1, source_target_pairs={{0,4},{2,6},{4,0},{6,2},{1,5},{3,7},{5,1},{7,3},{8,12},{10,14},{12... | collective-permute-start | bytes 122888 | tf_op jit(solution)/shard_map/ppermute | solution.py:558
  51.1 1.5 %collective-permute-start.13 = (bf16[32,640]{1,0:T(8,128)(2,1)S(1)}, bf16[32,640]{1,0:T(8,128)(2,1)S(1)}, u32[]{:S(2)}, u32[]{:S(2)}) collective-permute-start(bf16[32,640]{1,0:T(8,128)(2,1)S(1)} %later_latents.1.refs_0_), channel_id=1, source_target_pairs={{0,6},{2,4},{4,2},{6,0},{1,7},{3,5},{5,3},{7,1},{8,14},{10,12},{12... | collective-permute-start | bytes 122888 | tf_op jit(solution)/shard_map/ppermute | solution.py:558
  52.7 3.3 %collective-permute-done.12.refs_2_ = bf16[32,640]{1,0:T(8,128)(2,1)S(1)} collective-permute-done((bf16[32,640]{1,0:T(8,128)(2,1)S(1)}, bf16[32,640]{1,0:T(8,128)(2,1)S(1)}, u32[]{:S(2)}, u32[]{:S(2)}) %collective-permute-start.12) | collective-permute-done | bytes 40992 | tf_op jit(solution)/shard_map/ppermute | solution.py:558
  55.9 1.0 %collective-permute-done.13.refs_3_ = bf16[32,640]{1,0:T(8,128)(2,1)S(1)} collective-permute-done((bf16[32,640]{1,0:T(8,128)(2,1)S(1)}, bf16[32,640]{1,0:T(8,128)(2,1)S(1)}, u32[]{:S(2)}, u32[]{:S(2)}) %collective-permute-start.13) | collective-permute-done | bytes 40992 | tf_op jit(solution)/shard_map/ppermute | solution.py:558
  56.9 1.4 %collective-permute-start.19 = (bf16[2,32,256]{2,1,0:T(8,128)(2,1)S(1)}, bf16[2,32,256]{2,1,0:T(8,128)(2,1)S(1)}, u32[]{:S(2)}, u32[]{:S(2)}) collective-permute-start(bf16[2,32,256]{2,1,0:T(8,128)(2,1)S(1)} %get-tuple-element.61.refs_6_), channel_id=1, source_target_pairs={{0,1},{1,0},{2,3},{3,2},{4,5},{5,4},{6,7},{7,6},{8,9},{9,8},{10,11... | collective-permute-start | bytes 98312 | tf_op jit(solution)/shard_map/ppermute | solution.py:572
  58.3 1.9 %collective-permute-start.21 = (bf16[2,32,256]{2,1,0:T(8,128)(2,1)S(1)}, bf16[2,32,256]{2,1,0:T(8,128)(2,1)S(1)}, u32[]{:S(2)}, u32[]{:S(2)}) collective-permute-start(bf16[2,32,256]{2,1,0:T(8,128)(2,1)S(1)} %get-tuple-element.62), channel_id=1, source_target_pairs={{0,25},{1,24},{8,17},{9,16},{16,9},{17,8},{24,1},{25,0},{2,27},{3,... | collective-permute-start | bytes 98312 | tf_op jit(solution)/shard_map/ppermute | solution.py:568
  60.2 2.3 %last_results.1 = (bf16[1,4,32,1280]{3,2,1,0:T(8,128)(2,1)}, bf16[1,4,32,1280]{3,2,1,0:T(8,128)(2,1)}, f32[1,2,128,1280]{3,2,1,0:T(8,128)}) custom-call(bf16[32,640]{1,0:T(8,128)(2,1)S(1)} %later_latents.1.refs_0_, bf16[32,640]{1,0:T(8,128)(2,1)S(1)} %collective-permute-done.11.refs_1_, bf16[32,640]{1,0:T(8,128)(2,1)S(1)} %collective-permute-done.12.refs_2_, ...), custom_call_target="tpu_custom_call" | custom-call | flops 220000000 | tf_op jit(solution)/shard_map/last_results/pallas_call | solution.py:52
  62.6 1.4 %down_grads.1 = f32[1,2,640,256]{3,2,1,0:T(8,128)} custom-call(bf16[4,32,2560]{2,1,0:T(8,128)(2,1)S(1)} %get-tuple-element.52.refs_10_.refs_0_, bf16[4,32,2560]{2,1,0:T(8,128)(2,1)S(1)} %collective-permute-done.15.refs_11_.refs_0_.refs_1_, bf16[2,32,1792]{2,1,0:T(8,128)(2,1)S(1)} %get-tuple-element.55.refs_12_.refs_2_, ...), custom_call_target="tpu_custom_call" | custom-call | flops 1650000000 | tf_op jit(solution)/shard_map/down_grads/pallas_call | solution.py:52
  (46 shorter events, 2.7 us)
Async XLA Ops:
  0.6 10.6 %copy-start.5 = (f32[1,4,1280]{2,1,0:T(4,128)S(1)}, f32[1,4,1280]{2,1,0:T(4,128)}, u32[]{:S(2)}) copy-start(f32[1,4,1280]{2,1,0:T(4,128)} %refs_6_.5) | copy-start | bytes 61444
  0.6 10.6 %copy-start = (bf16[2,1,4,32,1280]{4,3,2,1,0:T(8,128)(2,1)S(1)}, bf16[2,1,4,32,1280]{4,3,2,1,0:T(8,128)(2,1)}, u32[]{:S(2)}) copy-start(bf16[2,1,4,32,1280]{4,3,2,1,0:T(8,128)(2,1)} %refs_8_.5) | copy-start | bytes 1966084
  0.7 10.6 %copy-start.3 = (bf16[1,4,32,1280]{3,2,1,0:T(8,128)(2,1)S(1)}, bf16[1,4,32,1280]{3,2,1,0:T(8,128)(2,1)}, u32[]{:S(2)}) copy-start(bf16[1,4,32,1280]{3,2,1,0:T(8,128)(2,1)} %refs_9_.3) | copy-start | bytes 983044
  5.6 8.0 %collective-permute-start = (bf16[32,1152]{1,0:T(8,128)(2,1)}, bf16[32,1152]{1,0:T(8,128)(2,1)S(1)}, u32[]{:S(2)}, u32[]{:S(2)}) collective-permute-start(bf16[32,1152]{1,0:T(8,128)(2,1)} %get-tuple-element.35.refs_4_), channel_id=1, source_target_pairs={{0,2},{2,0},{4,6},{6,4},{1,3},{3,1},{5,7},{7,5},{8,10},{10,8},{12,... | collective-permute-start | bytes 221192 | tf_op jit(solution)/shard_map/ppermute | solution.py:558
  8.6 8.0 %collective-permute-start.1 = (bf16[32,1152]{1,0:T(8,128)(2,1)}, bf16[32,1152]{1,0:T(8,128)(2,1)S(1)}, u32[]{:S(2)}, u32[]{:S(2)}) collective-permute-start(bf16[32,1152]{1,0:T(8,128)(2,1)} %get-tuple-element.37), channel_id=1, source_target_pairs={{0,4},{2,6},{4,0},{6,2},{1,5},{3,7},{5,1},{7,3},{8,12},{10,14},{12... | collective-permute-start | bytes 221192 | tf_op jit(solution)/shard_map/ppermute | solution.py:558
  11.2 6.5 %collective-permute-start.2 = (bf16[32,1152]{1,0:T(8,128)(2,1)}, bf16[32,1152]{1,0:T(8,128)(2,1)S(1)}, u32[]{:S(2)}, u32[]{:S(2)}) collective-permute-start(bf16[32,1152]{1,0:T(8,128)(2,1)} %get-tuple-element.38), channel_id=1, source_target_pairs={{0,6},{2,4},{4,2},{6,0},{1,7},{3,5},{5,3},{7,1},{8,14},{10,12},{12... | collective-permute-start | bytes 221192 | tf_op jit(solution)/shard_map/ppermute | solution.py:558
  11.2 0.9 %copy-start.8 = (bf16[32,1152]{1,0:T(8,128)(2,1)S(1)}, bf16[32,1152]{1,0:T(8,128)(2,1)}, u32[]{:S(2)}) copy-start(bf16[32,1152]{1,0:T(8,128)(2,1)} %get-tuple-element.35.refs_4_) | copy-start | bytes 221188
  12.1 0.9 %copy-start.9 = (bf16[32,1152]{1,0:T(8,128)(2,1)S(1)}, bf16[32,1152]{1,0:T(8,128)(2,1)}, u32[]{:S(2)}) copy-start(bf16[32,1152]{1,0:T(8,128)(2,1)} %get-tuple-element.34.refs_3_) | copy-start | bytes 221188
  13.1 16.5 %collective-permute-start.14 = (bf16[2,32,3840]{2,1,0:T(8,128)(2,1)S(1)}, bf16[2,32,3840]{2,1,0:T(8,128)(2,1)S(1)}, u32[]{:S(2)}, u32[]{:S(2)}) collective-permute-start(bf16[2,32,3840]{2,1,0:T(8,128)(2,1)S(1)} %get-tuple-element.51), channel_id=1, source_target_pairs={{0,24},{1,25},{8,16},{9,17},{16,8},{17,9},{24,0},{25,1},{2,26},{3,... | collective-permute-start | bytes 1474568 | tf_op jit(solution)/shard_map/ppermute | solution.py:568
  17.7 4.7 %copy-start.1 = (bf16[1,4,1280,256]{3,2,1,0:T(8,128)(2,1)S(1)}, bf16[1,4,1280,256]{3,2,1,0:T(8,128)(2,1)}, u32[]{:S(2)}) copy-start(bf16[1,4,1280,256]{3,2,1,0:T(8,128)(2,1)} %refs_0_.5) | copy-start | bytes 7864324
  17.7 4.7 %copy-start.2 = (bf16[1,4,256,1280]{3,2,1,0:T(8,128)(2,1)S(1)}, bf16[1,4,256,1280]{3,2,1,0:T(8,128)(2,1)}, u32[]{:S(2)}) copy-start(bf16[1,4,256,1280]{3,2,1,0:T(8,128)(2,1)} %refs_1_.5) | copy-start | bytes 7864324
  17.9 9.1 %copy-start.4 = (bf16[1,4,32,1280]{3,2,1,0:T(8,128)(2,1)S(1)}, bf16[1,4,32,1280]{3,2,1,0:T(8,128)(2,1)}, u32[]{:S(2)}) copy-start(bf16[1,4,32,1280]{3,2,1,0:T(8,128)(2,1)} %refs_7_.4) | copy-start | bytes 983044
  17.9 4.8 %collective-permute-start.3 = (bf16[32,1152]{1,0:T(8,128)(2,1)S(1)}, bf16[32,1152]{1,0:T(8,128)(2,1)S(1)}, u32[]{:S(2)}, u32[]{:S(2)}) collective-permute-start(bf16[32,1152]{1,0:T(8,128)(2,1)S(1)} %get-tuple-element.40.refs_2_.refs_0_), channel_id=1, source_target_pairs={{0,2},{2,0},{4,6},{6,4},{1,3},{3,1},{5,7},{7,5},{8,10},{10,8},{12,... | collective-permute-start | bytes 221192 | tf_op jit(solution)/shard_map/ppermute | solution.py:558
  19.1 6.8 %collective-permute-start.4 = (bf16[32,1152]{1,0:T(8,128)(2,1)S(1)}, bf16[32,1152]{1,0:T(8,128)(2,1)S(1)}, u32[]{:S(2)}, u32[]{:S(2)}) collective-permute-start(bf16[32,1152]{1,0:T(8,128)(2,1)S(1)} %get-tuple-element.40.refs_2_.refs_0_), channel_id=1, source_target_pairs={{0,4},{2,6},{4,0},{6,2},{1,5},{3,7},{5,1},{7,3},{8,12},{10,14},{12... | collective-permute-start | bytes 221192 | tf_op jit(solution)/shard_map/ppermute | solution.py:558
  20.8 6.3 %collective-permute-start.5 = (bf16[32,1152]{1,0:T(8,128)(2,1)S(1)}, bf16[32,1152]{1,0:T(8,128)(2,1)S(1)}, u32[]{:S(2)}, u32[]{:S(2)}) collective-permute-start(bf16[32,1152]{1,0:T(8,128)(2,1)S(1)} %get-tuple-element.40.refs_2_.refs_0_), channel_id=1, source_target_pairs={{0,6},{2,4},{4,2},{6,0},{1,7},{3,5},{5,3},{7,1},{8,14},{10,12},{12... | collective-permute-start | bytes 221192 | tf_op jit(solution)/shard_map/ppermute | solution.py:558
  27.8 8.0 %copy-start.6 = (bf16[1,2,32,1280]{3,2,1,0:T(8,128)(2,1)S(1)}, bf16[1,2,32,1280]{3,2,1,0:T(8,128)(2,1)}, u32[]{:S(2)}) copy-start(bf16[1,2,32,1280]{3,2,1,0:T(8,128)(2,1)} %refs_3_.3) | copy-start | bytes 491524
  27.8 8.0 %copy-start.7 = (bf16[1,2,32,1280]{3,2,1,0:T(8,128)(2,1)S(1)}, bf16[1,2,32,1280]{3,2,1,0:T(8,128)(2,1)}, u32[]{:S(2)}) copy-start(bf16[1,2,32,1280]{3,2,1,0:T(8,128)(2,1)} %refs_4_.3) | copy-start | bytes 491524
  28.5 2.8 %collective-permute-start.6 = (bf16[4,32,1280]{2,1,0:T(8,128)(2,1)S(1)}, bf16[4,32,1280]{2,1,0:T(8,128)(2,1)S(1)}, u32[]{:S(2)}, u32[]{:S(2)}) collective-permute-start(bf16[4,32,1280]{2,1,0:T(8,128)(2,1)S(1)} %get-tuple-element.43), channel_id=1, source_target_pairs={{0,8},{8,0},{16,24},{24,16},{1,9},{9,1},{17,25},{25,17},{2,10},{10... | collective-permute-start | bytes 983048 | tf_op jit(solution)/shard_map/ppermute | solution.py:599
  28.6 7.1 %collective-permute-start.7 = (bf16[4,32,1280]{2,1,0:T(8,128)(2,1)S(1)}, bf16[4,32,1280]{2,1,0:T(8,128)(2,1)S(1)}, u32[]{:S(2)}, u32[]{:S(2)}) collective-permute-start(bf16[4,32,1280]{2,1,0:T(8,128)(2,1)S(1)} %second_results.1.refs_10_.refs_2_), channel_id=1, source_target_pairs={{0,2},{2,0},{4,6},{6,4},{8,16},{10,18},{12,20},{14,22},{16,8},{18,... | collective-permute-start | bytes 983048 | tf_op jit(solution)/shard_map/ppermute | solution.py:595
  29.8 21.3 %collective-permute-start.15 = (bf16[4,32,2560]{2,1,0:T(8,128)(2,1)S(1)}, bf16[4,32,2560]{2,1,0:T(8,128)(2,1)S(1)}, u32[]{:S(2)}, u32[]{:S(2)}) collective-permute-start(bf16[4,32,2560]{2,1,0:T(8,128)(2,1)S(1)} %get-tuple-element.53), channel_id=1, source_target_pairs={{0,1},{1,0},{2,3},{3,2},{4,5},{5,4},{6,7},{7,6},{8,9},{9,8},{10,11... | collective-permute-start | bytes 1966088 | tf_op jit(solution)/shard_map/ppermute | solution.py:572
  37.1 6.1 %collective-permute-start.8 = (bf16[32,640]{1,0:T(8,128)(2,1)S(1)}, bf16[32,640]{1,0:T(8,128)(2,1)S(1)}, u32[]{:S(2)}, u32[]{:S(2)}) collective-permute-start(bf16[32,640]{1,0:T(8,128)(2,1)S(1)} %get-tuple-element.45), channel_id=1, source_target_pairs={{0,2},{2,0},{4,6},{6,4},{1,3},{3,1},{5,7},{7,5},{8,10},{10,8},{12,... | collective-permute-start | bytes 122888 | tf_op jit(solution)/shard_map/ppermute | solution.py:558
  38.1 5.1 %collective-permute-start.9 = (bf16[32,640]{1,0:T(8,128)(2,1)S(1)}, bf16[32,640]{1,0:T(8,128)(2,1)S(1)}, u32[]{:S(2)}, u32[]{:S(2)}) collective-permute-start(bf16[32,640]{1,0:T(8,128)(2,1)S(1)} %get-tuple-element.46), channel_id=1, source_target_pairs={{0,4},{2,6},{4,0},{6,2},{1,5},{3,7},{5,1},{7,3},{8,12},{10,14},{12... | collective-permute-start | bytes 122888 | tf_op jit(solution)/shard_map/ppermute | solution.py:558
  39.9 5.8 %collective-permute-start.10 = (bf16[32,640]{1,0:T(8,128)(2,1)S(1)}, bf16[32,640]{1,0:T(8,128)(2,1)S(1)}, u32[]{:S(2)}, u32[]{:S(2)}) collective-permute-start(bf16[32,640]{1,0:T(8,128)(2,1)S(1)} %get-tuple-element.47), channel_id=1, source_target_pairs={{0,6},{2,4},{4,2},{6,0},{1,7},{3,5},{5,3},{7,1},{8,14},{10,12},{12... | collective-permute-start | bytes 122888 | tf_op jit(solution)/shard_map/ppermute | solution.py:558
  41.6 16.7 %collective-permute-start.16 = (bf16[2,32,1792]{2,1,0:T(8,128)(2,1)S(1)}, bf16[2,32,1792]{2,1,0:T(8,128)(2,1)S(1)}, u32[]{:S(2)}, u32[]{:S(2)}) collective-permute-start(bf16[2,32,1792]{2,1,0:T(8,128)(2,1)S(1)} %get-tuple-element.56), channel_id=1, source_target_pairs={{0,1},{1,0},{2,3},{3,2},{4,5},{5,4},{6,7},{7,6},{8,9},{9,8},{10,11... | collective-permute-start | bytes 688136 | tf_op jit(solution)/shard_map/ppermute | solution.py:572
  43.2 17.0 %collective-permute-start.17 = (bf16[2,32,1792]{2,1,0:T(8,128)(2,1)S(1)}, bf16[2,32,1792]{2,1,0:T(8,128)(2,1)S(1)}, u32[]{:S(2)}, u32[]{:S(2)}) collective-permute-start(bf16[2,32,1792]{2,1,0:T(8,128)(2,1)S(1)} %get-tuple-element.57), channel_id=1, source_target_pairs={{0,24},{1,25},{8,16},{9,17},{16,8},{17,9},{24,0},{25,1},{2,26},{3,... | collective-permute-start | bytes 688136 | tf_op jit(solution)/shard_map/ppermute | solution.py:568
  43.2 17.0 %collective-permute-start.18 = (bf16[2,32,1792]{2,1,0:T(8,128)(2,1)S(1)}, bf16[2,32,1792]{2,1,0:T(8,128)(2,1)S(1)}, u32[]{:S(2)}, u32[]{:S(2)}) collective-permute-start(bf16[2,32,1792]{2,1,0:T(8,128)(2,1)S(1)} %get-tuple-element.58), channel_id=1, source_target_pairs={{0,25},{1,24},{8,17},{9,16},{16,9},{17,8},{24,1},{25,0},{2,27},{3,... | collective-permute-start | bytes 688136 | tf_op jit(solution)/shard_map/ppermute | solution.py:568
  46.0 4.0 %collective-permute-start.11 = (bf16[32,640]{1,0:T(8,128)(2,1)S(1)}, bf16[32,640]{1,0:T(8,128)(2,1)S(1)}, u32[]{:S(2)}, u32[]{:S(2)}) collective-permute-start(bf16[32,640]{1,0:T(8,128)(2,1)S(1)} %later_latents.1.refs_0_), channel_id=1, source_target_pairs={{0,2},{2,0},{4,6},{6,4},{1,3},{3,1},{5,7},{7,5},{8,10},{10,8},{12,... | collective-permute-start | bytes 122888 | tf_op jit(solution)/shard_map/ppermute | solution.py:558
  50.0 5.9 %collective-permute-start.12 = (bf16[32,640]{1,0:T(8,128)(2,1)S(1)}, bf16[32,640]{1,0:T(8,128)(2,1)S(1)}, u32[]{:S(2)}, u32[]{:S(2)}) collective-permute-start(bf16[32,640]{1,0:T(8,128)(2,1)S(1)} %later_latents.1.refs_0_), channel_id=1, source_target_pairs={{0,4},{2,6},{4,0},{6,2},{1,5},{3,7},{5,1},{7,3},{8,12},{10,14},{12... | collective-permute-start | bytes 122888 | tf_op jit(solution)/shard_map/ppermute | solution.py:558
  51.1 5.8 %collective-permute-start.13 = (bf16[32,640]{1,0:T(8,128)(2,1)S(1)}, bf16[32,640]{1,0:T(8,128)(2,1)S(1)}, u32[]{:S(2)}, u32[]{:S(2)}) collective-permute-start(bf16[32,640]{1,0:T(8,128)(2,1)S(1)} %later_latents.1.refs_0_), channel_id=1, source_target_pairs={{0,6},{2,4},{4,2},{6,0},{1,7},{3,5},{5,3},{7,1},{8,14},{10,12},{12... | collective-permute-start | bytes 122888 | tf_op jit(solution)/shard_map/ppermute | solution.py:558
  56.9 5.6 %collective-permute-start.19 = (bf16[2,32,256]{2,1,0:T(8,128)(2,1)S(1)}, bf16[2,32,256]{2,1,0:T(8,128)(2,1)S(1)}, u32[]{:S(2)}, u32[]{:S(2)}) collective-permute-start(bf16[2,32,256]{2,1,0:T(8,128)(2,1)S(1)} %get-tuple-element.61.refs_6_), channel_id=1, source_target_pairs={{0,1},{1,0},{2,3},{3,2},{4,5},{5,4},{6,7},{7,6},{8,9},{9,8},{10,11... | collective-permute-start | bytes 98312 | tf_op jit(solution)/shard_map/ppermute | solution.py:572
  58.3 4.2 %collective-permute-start.20 = (bf16[2,32,256]{2,1,0:T(8,128)(2,1)S(1)}, bf16[2,32,256]{2,1,0:T(8,128)(2,1)S(1)}, u32[]{:S(2)}, u32[]{:S(2)}) collective-permute-start(bf16[2,32,256]{2,1,0:T(8,128)(2,1)S(1)} %get-tuple-element.62), channel_id=1, source_target_pairs={{0,24},{1,25},{8,16},{9,17},{16,8},{17,9},{24,0},{25,1},{2,26},{3,... | collective-permute-start | bytes 98312 | tf_op jit(solution)/shard_map/ppermute | solution.py:568
  58.3 4.2 %collective-permute-start.21 = (bf16[2,32,256]{2,1,0:T(8,128)(2,1)S(1)}, bf16[2,32,256]{2,1,0:T(8,128)(2,1)S(1)}, u32[]{:S(2)}, u32[]{:S(2)}) collective-permute-start(bf16[2,32,256]{2,1,0:T(8,128)(2,1)S(1)} %get-tuple-element.62), channel_id=1, source_target_pairs={{0,25},{1,24},{8,17},{9,16},{16,9},{17,8},{24,1},{25,0},{2,27},{3,... | collective-permute-start | bytes 98312 | tf_op jit(solution)/shard_map/ppermute | solution.py:568

commit v5 on v3

--- a/solution.py
+++ b/solution.py
@@ -17,8 +17,8 @@
     "first_partials": 5.0,
     "early_factors": 0.3,
     "held_weights": 0.5,
-    "marker": 1.5,
-    "first_latents": 0.3,
+    "marker": 0.1,
+    "first_latents": 4,
     "second_results": 0.8,
     "first_results": 0.8,
     "later_partials": 1.3,
@@ -154,53 +154,63 @@
     )
 
 
-def early_factors(gains, kept, upstream, own, after):
+def early_factors(groups, gains, kept, upstream, own, after):
     ticks, _, slots, rows, feats = kept.shape
-    half = slots // 2
-
-    def body(gain_ref, kept_ref, dy_ref, own_ref, near, far, own_out):
+    half, wide = slots // 2, feats // groups
+
+    def body(gain_ref, kept_ref, dy_ref, own_ref, *outs):
+        *near, far, own_out = outs
         own_out[...] = own_ref[...]
+        mine = group()
         for s in range(slots):
             gain = gain_ref[0, s : s + 1, :]
-            out = near if s < half else far
             for t in range(ticks):
                 hg = kept_ref[t, 0, s].astype(F32) * gain
-                out[s % half, :, t * feats : (t + 1) * feats] = hg.astype(BF16)
-            out[s % half, :, ticks * feats :] = dy_ref[0, s]
-
-    return call(
+                if s < half:
+                    for k, out in enumerate(near):
+                        part = lane_part(hg, mine ^ k, groups).astype(BF16)
+                        out[s, :, t * wide : (t + 1) * wide] = part
+                else:
+                    far[s - half, :, t * feats : (t + 1) * feats] = hg.astype(BF16)
+            if s < half:
+                for out in near:
+                    out[s, :, ticks * wide :] = dy_ref[0, s]
+            else:
+                far[s - half, :, ticks * feats :] = dy_ref[0, s]
+
+    *near, far, own = call(
         body,
         [gains, kept, upstream, own],
-        [((half, rows, (ticks + 1) * feats), BF16)] * 2 + [(own.shape, own.dtype)],
+        [((half, rows, ticks * wide + feats), BF16)] * groups
+        + [((half, rows, (ticks + 1) * feats), BF16), (own.shape, own.dtype)],
         "early_factors",
         after=after,
     )
-
-
-def shared(name, groups, cut, near, far, after=()):
-    half, rows, width = near.shape
-    count = sum(size for _, size in cut)
-    kept = width - count + count // groups
-
-    def body(near_ref, far_ref, *outs):
+    return near, far, own
+
+
+def early_share(groups, ticks, far, after):
+    half, rows, width = far.shape
+    feats = width // (ticks + 1)
+    wide = feats // groups
+
+    def body(far_ref, *outs):
         mine = group()
-        for j in range(2 * half):
-            ref = near_ref if j < half else far_ref
-            for k, out in enumerate(outs):
-                source, target = 0, 0
-                for start, size in [*cut, (width, 0)]:
-                    plain = start - source
-                    if plain:
-                        out[j, :, target : target + plain] = ref[j % half, :, source:start]
-                    source, target = start, target + plain
-                    if size:
-                        run = ref[j % half, :, start : start + size].astype(F32)
-                        part = lane_part(run, mine ^ k, groups).astype(BF16)
-                        out[j, :, target : target + size // groups] = part
-                        source, target = start + size, target + size // groups
-
-    return call(
-        body, [near, far], [((2 * half, rows, kept), BF16)] * groups, name, after=after
+        for j in range(half):
+            for t in range(ticks):
+                hg = far_ref[j, :, t * feats : (t + 1) * feats].astype(F32)
+                for k, out in enumerate(outs):
+                    part = lane_part(hg, mine ^ k, groups).astype(BF16)
+                    out[j, :, t * wide : (t + 1) * wide] = part
+            for out in outs:
+                out[j, :, ticks * wide :] = far_ref[j, :, ticks * feats :]
+
+    return call(
+        body,
+        [far],
+        [((half, rows, ticks * wide + feats), BF16)] * groups,
+        "early_share",
+        after=after,
     )
 
 
@@ -474,17 +484,16 @@
     def body(*refs):
         ins, refs = refs[:parts], refs[parts:]
         down_ref, up_ref, gain_ref, x_ref, kept_ref, g_ref = refs[:6]
-        early, mid, refs = refs[6 : 6 + count], refs[6 + count : 6 + 3 * count], refs[6 + 3 * count :]
+        early, mid, refs = refs[6 : 6 + count], refs[6 + count : 6 + 2 * count], refs[6 + 2 * count :]
         y_hbm, dh_hbm, grad_hbm, table, y_out, dh_out, grad_out, sems = refs
         send, finish = sender(sems)
         for j in range(half):
             act, dy = [], []
-            for k, e in enumerate(early):
-                for i, m in ((j, mid[k]), (half + j, mid[count + k])):
-                    start = feats + rank
-                    for t in range(ticks):
-                        act.append(m[j, :, start + t * some : start + (t + 1) * some])
-                    dy += [e[i, :, e.shape[-1] - feats :], m[j, :, :feats]]
+            for e, m in zip(early, mid):
+                start = feats + rank
+                for t in range(ticks):
+                    act.append(m[j, :, start + t * some : start + (t + 1) * some])
+                dy += [e[j, :, e.shape[-1] - feats :], m[j, :, :feats]]
             grad_out[j] = dot(jnp.concatenate(act, axis=0), jnp.concatenate(dy, axis=0), TN)
             send(grad_out.at[j], grad_hbm.at[0, j])
         collect(ins, table)
@@ -525,15 +534,14 @@
     wide = feats // groups
 
     def body(*refs):
-        early, mid, late = refs[:count], refs[count : 3 * count], refs[3 * count : 5 * count]
-        grad_hbm, grad_out, sems = refs[5 * count :]
+        early, mid, late = refs[:count], refs[count : 2 * count], refs[2 * count : 3 * count]
+        grad_hbm, grad_out, sems = refs[3 * count :]
         send, finish = sender(sems)
         for j in range(half):
             hg, du = [], []
-            for k, e in enumerate(early):
-                for i, n in ((j, k), (half + j, count + k)):
-                    hg += [e[i, :, t * wide : (t + 1) * wide] for t in range(ticks)]
-                    du += [mid[n][j, :, feats : feats + rank], late[n][j]]
+            for e, m, l in zip(early, mid, late):
+                hg += [e[j, :, t * wide : (t + 1) * wide] for t in range(ticks)]
+                du += [m[j, :, feats : feats + rank], l[j]]
             grad_out[j] = dot(jnp.concatenate(hg, axis=0), jnp.concatenate(du, axis=0), TN)
             send(grad_out.at[j], grad_hbm.at[0, j])
         finish()
@@ -576,12 +584,13 @@
     dealt = first_partials(parts, w_down, w_up, gains, entry, kept, upstream, after=[])
     received = around(dealt)
 
-    near, far, own = early_factors(gains, kept, upstream, dealt[0], after=dealt[1:2])
+    near, far, own = early_factors(groups, gains, kept, upstream, dealt[0], after=dealt[1:2])
+    early = across(near)
     far = mirrored(far)
 
-    weights = held_weights(w_down, w_up, after=dealt[1:2])
-    message, held = first_latents(ticks, rank, [own] + received[1:], after=[near, weights[0]])
+    message, held = first_latents(ticks, rank, [own] + received[1:], after=[own])
     received = around([message] * parts)
+    weights = held_weights(w_down, w_up, after=[message])
 
     tick = (received, *weights, gains, entry, kept, upstream)
     (second,) = middle_results("second_results", odd, *tick)
@@ -598,13 +607,12 @@
     )
     from_first = lax.ppermute(first, "pipe", swap)
 
-    early = across(
-        shared("early_share", groups, [(t * feats, feats) for t in range(ticks)], near, far, [])
-    )
-    ready = marker(early[1:])
+    early += across(early_share(groups, ticks, far, after=[second]))
+    ready_near = marker(early[1:groups])
+    ready = marker(early[groups + 1 :])
 
     dealt, x, g = later_partials(
-        parts, from_first, from_second, second, fresh, arriving, *weights, gains, after=[]
+        parts, from_first, from_second, second, fresh, arriving, *weights, gains, after=ready_near
     )
     received = around(dealt)
     near, far = middle_factors(groups, ticks, factors, g, after=[])

time: 66.6 us -> 63.7 us (0.956)
  local copies, waits for them, and re-layouts: 4.39 us -> 1.8 us
  waiting for transfers between devices: 19.3 us -> 18.2 us
    unnamed x18 -> x20, local copies, waits for them, and re-layouts: 4.39 us -> 1.8 us
    ppermute x5, starting transfers between devices: 6.08 us -> 3.9 us  [mirrored(): return lax.ppermute(far, ('pipe', 'dp'), pairs)]
    ppermute x3 -> x4, starting transfers between devices: 4.51 us -> 6.15 us  [across(): lax.ppermute(arrays[k], 'dp', [(i, i ^ k) for i in range(groups)])]
    ppermute x12, starting transfers between devices: 17.1 us -> 18.5 us  [around(): lax.ppermute(arrays[k], 'tensor', [(i, i ^ k) for i in range(parts)])]
    ppermute x1, waiting for transfers between devices: 5.52 us -> 4.47 us  [per_device(): from_second = lax.ppermute(second, ('pipe', 'tensor'), cross)]
    pallas_call x14 -> x15, Pallas kernels: 12.6 us -> 12.6 us  [call(): pl.pallas_call(run, in_specs=[pl.BlockSpec(memory_space=pl.ANY)] * raw +...]
  transfers between devices with their start and end apart: 22 -> 23, of which waited for: 8 -> 9; matrix products, arithmetic and copies ran while one was open for 0% -> 0% of each run, Pallas kernels for 9% -> 10%
where the time goes in v5:
time: 63.7 us; the launch traced here: 63.1 us
  starting transfers between devices  29.6 us (46%)
  waiting for transfers between devices  18.2 us (29%)
  Pallas kernels  12.6 us (20%)
  local copies, waits for them, and re-layouts  1.8 us (3%)
  between operations  0.82 us (1%)
    ppermute x12, starting transfers between devices, around(): lax.ppermute(arrays[k], 'tensor', [(i, i ^ k) for i in range(parts)])  18.5 us
    ppermute x12, waiting for transfers between devices, around(): lax.ppermute(arrays[k], 'tensor', [(i, i ^ k) for i in range(parts)])  13.5 us
    pallas_call x15, Pallas kernels, call(): pl.pallas_call(run, in_specs=[pl.BlockSpec(memory_space=pl.ANY)] * raw +...  12.6 us
    ppermute x4, starting transfers between devices, across(): lax.ppermute(arrays[k], 'dp', [(i, i ^ k) for i in range(groups)])  6.15 us
    ppermute x1, waiting for transfers between devices, per_device(): from_second = lax.ppermute(second, ('pipe', 'tensor'), cross)  4.47 us
    ppermute x5, starting transfers between devices, mirrored(): return lax.ppermute(far, ('pipe', 'dp'), pairs)  3.9 us
    unnamed x20, local copies, waits for them, and re-layouts  1.8 us
  transfers between devices with their start and end apart: 23, of which 9 were waited for; matrix products, arithmetic and copies ran while one was open for 0% of the time, Pallas kernels for 10%

profile of v5, /device:TPU:0, one launch (start us, length us, event | category | flops | bytes accessed | tf_op | source)
XLA Modules:
  0.0 63.1 jit_solution(11755587149866088823)
XLA Ops:
  0.7 4.9 %first_partials.1 = (bf16[32,1152]{1,0:T(8,128)(2,1)}, bf16[32,1152]{1,0:T(8,128)(2,1)}, bf16[32,1152]{1,0:T(8,128)(2,1)}, bf16[32,1152]{1,0:T(8,128)(2,1)}) custom-call(bf16[1,4,1280,256]{3,2,1,0:T(8,128)(2,1)} %refs_0_.5, bf16[1,4,256,1280]{3,2,1,0:T(8,128)(2,1)} %refs_1_.5, f32[1,4,1280]{2,1,0:T(4,128)} %refs_6_.5, bf16[1,4,32,1280]{3,2,1,0:T(8,128)(2,1)} %refs_7_.4, ...), custom_call_target="tpu_custom_call" | custom-call | flops 5500000256 | tf_op jit(solution)/shard_map/first_partials/pallas_call | solution.py:52
  5.6 3.0 %collective-permute-start = (bf16[32,1152]{1,0:T(8,128)(2,1)}, bf16[32,1152]{1,0:T(8,128)(2,1)S(1)}, u32[]{:S(2)}, u32[]{:S(2)}) collective-permute-start(bf16[32,1152]{1,0:T(8,128)(2,1)} %get-tuple-element.36.refs_4_), channel_id=1, source_target_pairs={{0,2},{2,0},{4,6},{6,4},{1,3},{3,1},{5,7},{7,5},{8,10},{10,8},{12,... | collective-permute-start | bytes 221192 | tf_op jit(solution)/shard_map/ppermute | solution.py:566
  8.6 2.6 %collective-permute-start.1 = (bf16[32,1152]{1,0:T(8,128)(2,1)}, bf16[32,1152]{1,0:T(8,128)(2,1)S(1)}, u32[]{:S(2)}, u32[]{:S(2)}) collective-permute-start(bf16[32,1152]{1,0:T(8,128)(2,1)} %get-tuple-element.38), channel_id=1, source_target_pairs={{0,4},{2,6},{4,0},{6,2},{1,5},{3,7},{5,1},{7,3},{8,12},{10,14},{12... | collective-permute-start | bytes 221192 | tf_op jit(solution)/shard_map/ppermute | solution.py:566
  11.2 0.9 %copy-done.8 = bf16[32,1152]{1,0:T(8,128)(2,1)S(1)} copy-done((bf16[32,1152]{1,0:T(8,128)(2,1)S(1)}, bf16[32,1152]{1,0:T(8,128)(2,1)}, u32[]{:S(2)}) %copy-start.8) | copy-done | bytes 73752
  12.1 0.9 %copy-done.9 = bf16[32,1152]{1,0:T(8,128)(2,1)S(1)} copy-done((bf16[32,1152]{1,0:T(8,128)(2,1)S(1)}, bf16[32,1152]{1,0:T(8,128)(2,1)}, u32[]{:S(2)}) %copy-start.9) | copy-done | bytes 73752
  13.6 3.0 %collective-permute-done.1.refs_2_ = bf16[32,1152]{1,0:T(8,128)(2,1)S(1)} collective-permute-done((bf16[32,1152]{1,0:T(8,128)(2,1)}, bf16[32,1152]{1,0:T(8,128)(2,1)S(1)}, u32[]{:S(2)}, u32[]{:S(2)}) %collective-permute-start.1) | collective-permute-done | bytes 73760 | tf_op jit(solution)/shard_map/ppermute | solution.py:566
  16.6 1.1 %collective-permute-done.2.refs_3_ = bf16[32,1152]{1,0:T(8,128)(2,1)S(1)} collective-permute-done((bf16[32,1152]{1,0:T(8,128)(2,1)}, bf16[32,1152]{1,0:T(8,128)(2,1)S(1)}, u32[]{:S(2)}, u32[]{:S(2)}) %collective-permute-start.2) | collective-permute-done | bytes 73760 | tf_op jit(solution)/shard_map/ppermute | solution.py:566
  17.9 1.1 %collective-permute-start.3 = (bf16[32,1152]{1,0:T(8,128)(2,1)S(1)}, bf16[32,1152]{1,0:T(8,128)(2,1)S(1)}, u32[]{:S(2)}, u32[]{:S(2)}) collective-permute-start(bf16[32,1152]{1,0:T(8,128)(2,1)S(1)} %get-tuple-element.40.refs_2_.refs_0_), channel_id=1, source_target_pairs={{0,2},{2,0},{4,6},{6,4},{1,3},{3,1},{5,7},{7,5},{8,10},{10,8},{12,... | collective-permute-start | bytes 221192 | tf_op jit(solution)/shard_map/ppermute | solution.py:566
  19.1 1.7 %collective-permute-start.4 = (bf16[32,1152]{1,0:T(8,128)(2,1)S(1)}, bf16[32,1152]{1,0:T(8,128)(2,1)S(1)}, u32[]{:S(2)}, u32[]{:S(2)}) collective-permute-start(bf16[32,1152]{1,0:T(8,128)(2,1)S(1)} %get-tuple-element.40.refs_2_.refs_0_), channel_id=1, source_target_pairs={{0,4},{2,6},{4,0},{6,2},{1,5},{3,7},{5,1},{7,3},{8,12},{10,14},{12... | collective-permute-start | bytes 221192 | tf_op jit(solution)/shard_map/ppermute | solution.py:566
  20.8 1.6 %collective-permute-start.5 = (bf16[32,1152]{1,0:T(8,128)(2,1)S(1)}, bf16[32,1152]{1,0:T(8,128)(2,1)S(1)}, u32[]{:S(2)}, u32[]{:S(2)}) collective-permute-start(bf16[32,1152]{1,0:T(8,128)(2,1)S(1)} %get-tuple-element.40.refs_2_.refs_0_), channel_id=1, source_target_pairs={{0,6},{2,4},{4,2},{6,0},{1,7},{3,5},{5,3},{7,1},{8,14},{10,12},{12... | collective-permute-start | bytes 221192 | tf_op jit(solution)/shard_map/ppermute | solution.py:566
  22.4 1.5 %collective-permute-start.8 = (bf16[2,32,2560]{2,1,0:T(8,128)(2,1)S(1)}, bf16[2,32,2560]{2,1,0:T(8,128)(2,1)S(1)}, u32[]{:S(2)}, u32[]{:S(2)}) collective-permute-start(bf16[2,32,2560]{2,1,0:T(8,128)(2,1)S(1)} %get-tuple-element.44), channel_id=1, source_target_pairs={{0,1},{1,0},{2,3},{3,2},{4,5},{5,4},{6,7},{7,6},{8,9},{9,8},{10,11... | collective-permute-start | bytes 983048 | tf_op jit(solution)/shard_map/ppermute | solution.py:580
  24.3 1.6 %collective-permute-done.4.refs_2_ = bf16[32,1152]{1,0:T(8,128)(2,1)S(1)} collective-permute-done((bf16[32,1152]{1,0:T(8,128)(2,1)S(1)}, bf16[32,1152]{1,0:T(8,128)(2,1)S(1)}, u32[]{:S(2)}, u32[]{:S(2)}) %collective-permute-start.4) | collective-permute-done | bytes 73760 | tf_op jit(solution)/shard_map/ppermute | solution.py:566
  25.8 1.2 %collective-permute-done.5.refs_3_ = bf16[32,1152]{1,0:T(8,128)(2,1)S(1)} collective-permute-done((bf16[32,1152]{1,0:T(8,128)(2,1)S(1)}, bf16[32,1152]{1,0:T(8,128)(2,1)S(1)}, u32[]{:S(2)}, u32[]{:S(2)}) %collective-permute-start.5) | collective-permute-done | bytes 73760 | tf_op jit(solution)/shard_map/ppermute | solution.py:566
  27.8 0.7 %first_results.1 = (bf16[4,32,1280]{2,1,0:T(8,128)(2,1)S(1)}, bf16[4,32,768]{2,1,0:T(8,128)(2,1)S(1)}) custom-call(bf16[32,1152]{1,0:T(8,128)(2,1)S(1)} %get-tuple-element.40.refs_2_.refs_0_, bf16[32,1152]{1,0:T(8,128)(2,1)S(1)} %collective-permute-done.3.refs_1_, bf16[32,1152]{1,0:T(8,128)(2,1)S(1)} %collective-permute-done.4.refs_2_, ...), custom_call_target="tpu_custom_call" | custom-call | flops 880000000 | tf_op jit(solution)/shard_map/first_results/pallas_call | solution.py:52
  28.6 1.0 %collective-permute-start.7 = (bf16[4,32,1280]{2,1,0:T(8,128)(2,1)S(1)}, bf16[4,32,1280]{2,1,0:T(8,128)(2,1)S(1)}, u32[]{:S(2)}, u32[]{:S(2)}) collective-permute-start(bf16[4,32,1280]{2,1,0:T(8,128)(2,1)S(1)} %second_results.1.refs_10_.refs_2_.refs_1_), channel_id=1, source_target_pairs={{0,2},{2,0},{4,6},{6,4},{8,16},{10,18},{12,20},{14,22},{16,8},{18,... | collective-permute-start | bytes 983048 | tf_op jit(solution)/shard_map/ppermute | solution.py:604
  29.7 1.6 %collective-permute-start.13 = (bf16[2,32,2560]{2,1,0:T(8,128)(2,1)S(1)}, bf16[2,32,2560]{2,1,0:T(8,128)(2,1)S(1)}, u32[]{:S(2)}, u32[]{:S(2)}) collective-permute-start(bf16[2,32,2560]{2,1,0:T(8,128)(2,1)S(1)} %get-tuple-element.51), channel_id=1, source_target_pairs={{0,1},{1,0},{2,3},{3,2},{4,5},{5,4},{6,7},{7,6},{8,9},{9,8},{10,11... | collective-permute-start | bytes 983048 | tf_op jit(solution)/shard_map/ppermute | solution.py:580
  31.3 4.5 %collective-permute-done.7.refs_1_ = bf16[4,32,1280]{2,1,0:T(8,128)(2,1)S(1)} collective-permute-done((bf16[4,32,1280]{2,1,0:T(8,128)(2,1)S(1)}, bf16[4,32,1280]{2,1,0:T(8,128)(2,1)S(1)}, u32[]{:S(2)}, u32[]{:S(2)}) %collective-permute-start.7) | collective-permute-done | bytes 327712 | tf_op jit(solution)/shard_map/ppermute | solution.py:604
  35.7 1.3 %later_partials.1 = (bf16[32,640]{1,0:T(8,128)(2,1)S(1)}, bf16[32,640]{1,0:T(8,128)(2,1)S(1)}, bf16[32,640]{1,0:T(8,128)(2,1)S(1)}, bf16[32,640]{1,0:T(8,128)(2,...) custom-call(bf16[4,32,1280]{2,1,0:T(8,128)(2,1)S(1)} %collective-permute-done.6.refs_0_, ...), custom_call_target="tpu_custom_call" | custom-call | flops 1430000000 | tf_op jit(solution)/shard_map/later_partials/pallas_call | solution.py:52
  37.1 1.0 %collective-permute-start.9 = (bf16[32,640]{1,0:T(8,128)(2,1)S(1)}, bf16[32,640]{1,0:T(8,128)(2,1)S(1)}, u32[]{:S(2)}, u32[]{:S(2)}) collective-permute-start(bf16[32,640]{1,0:T(8,128)(2,1)S(1)} %get-tuple-element.46), channel_id=1, source_target_pairs={{0,2},{2,0},{4,6},{6,4},{1,3},{3,1},{5,7},{7,5},{8,10},{10,8},{12,... | collective-permute-start | bytes 122888 | tf_op jit(solution)/shard_map/ppermute | solution.py:566
  38.1 1.8 %collective-permute-start.10 = (bf16[32,640]{1,0:T(8,128)(2,1)S(1)}, bf16[32,640]{1,0:T(8,128)(2,1)S(1)}, u32[]{:S(2)}, u32[]{:S(2)}) collective-permute-start(bf16[32,640]{1,0:T(8,128)(2,1)S(1)} %get-tuple-element.47), channel_id=1, source_target_pairs={{0,4},{2,6},{4,0},{6,2},{1,5},{3,7},{5,1},{7,3},{8,12},{10,14},{12... | collective-permute-start | bytes 122888 | tf_op jit(solution)/shard_map/ppermute | solution.py:566
  39.9 1.6 %collective-permute-start.11 = (bf16[32,640]{1,0:T(8,128)(2,1)S(1)}, bf16[32,640]{1,0:T(8,128)(2,1)S(1)}, u32[]{:S(2)}, u32[]{:S(2)}) collective-permute-start(bf16[32,640]{1,0:T(8,128)(2,1)S(1)} %get-tuple-element.48), channel_id=1, source_target_pairs={{0,6},{2,4},{4,2},{6,0},{1,7},{3,5},{5,3},{7,1},{8,14},{10,12},{12... | collective-permute-start | bytes 122888 | tf_op jit(solution)/shard_map/ppermute | solution.py:566
  41.6 1.6 %collective-permute-start.17 = (bf16[2,32,1792]{2,1,0:T(8,128)(2,1)S(1)}, bf16[2,32,1792]{2,1,0:T(8,128)(2,1)S(1)}, u32[]{:S(2)}, u32[]{:S(2)}) collective-permute-start(bf16[2,32,1792]{2,1,0:T(8,128)(2,1)S(1)} %get-tuple-element.58), channel_id=1, source_target_pairs={{0,1},{1,0},{2,3},{3,2},{4,5},{5,4},{6,7},{7,6},{8,9},{9,8},{10,11... | collective-permute-start | bytes 688136 | tf_op jit(solution)/shard_map/ppermute | solution.py:580
  43.2 1.7 %collective-permute-start.19 = (bf16[2,32,1792]{2,1,0:T(8,128)(2,1)S(1)}, bf16[2,32,1792]{2,1,0:T(8,128)(2,1)S(1)}, u32[]{:S(2)}, u32[]{:S(2)}) collective-permute-start(bf16[2,32,1792]{2,1,0:T(8,128)(2,1)S(1)} %get-tuple-element.60), channel_id=1, source_target_pairs={{0,25},{1,24},{8,17},{9,16},{16,9},{17,8},{24,1},{25,0},{2,27},{3,... | collective-permute-start | bytes 688136 | tf_op jit(solution)/shard_map/ppermute | solution.py:576
  44.9 0.8 %collective-permute-done.11.refs_3_ = bf16[32,640]{1,0:T(8,128)(2,1)S(1)} collective-permute-done((bf16[32,640]{1,0:T(8,128)(2,1)S(1)}, bf16[32,640]{1,0:T(8,128)(2,1)S(1)}, u32[]{:S(2)}, u32[]{:S(2)}) %collective-permute-start.11) | collective-permute-done | bytes 40992 | tf_op jit(solution)/shard_map/ppermute | solution.py:566
  46.0 2.3 %collective-permute-start.15 = (bf16[32,640]{1,0:T(8,128)(2,1)S(1)}, bf16[32,640]{1,0:T(8,128)(2,1)S(1)}, u32[]{:S(2)}, u32[]{:S(2)}) collective-permute-start(bf16[32,640]{1,0:T(8,128)(2,1)S(1)} %later_latents.1.refs_0_), channel_id=1, source_target_pairs={{0,4},{2,6},{4,0},{6,2},{1,5},{3,7},{5,1},{7,3},{8,12},{10,14},{12... | collective-permute-start | bytes 122888 | tf_op jit(solution)/shard_map/ppermute | solution.py:566
  48.3 1.7 %collective-permute-done.14.refs_1_ = bf16[32,640]{1,0:T(8,128)(2,1)S(1)} collective-permute-done((bf16[32,640]{1,0:T(8,128)(2,1)S(1)}, bf16[32,640]{1,0:T(8,128)(2,1)S(1)}, u32[]{:S(2)}, u32[]{:S(2)}) %collective-permute-start.14) | collective-permute-done | bytes 40992 | tf_op jit(solution)/shard_map/ppermute | solution.py:566
  50.0 1.7 %collective-permute-start.16 = (bf16[32,640]{1,0:T(8,128)(2,1)S(1)}, bf16[32,640]{1,0:T(8,128)(2,1)S(1)}, u32[]{:S(2)}, u32[]{:S(2)}) collective-permute-start(bf16[32,640]{1,0:T(8,128)(2,1)S(1)} %later_latents.1.refs_0_), channel_id=1, source_target_pairs={{0,6},{2,4},{4,2},{6,0},{1,7},{3,5},{5,3},{7,1},{8,14},{10,12},{12... | collective-permute-start | bytes 122888 | tf_op jit(solution)/shard_map/ppermute | solution.py:566
  51.7 4.1 %collective-permute-done.16.refs_3_ = bf16[32,640]{1,0:T(8,128)(2,1)S(1)} collective-permute-done((bf16[32,640]{1,0:T(8,128)(2,1)S(1)}, bf16[32,640]{1,0:T(8,128)(2,1)S(1)}, u32[]{:S(2)}, u32[]{:S(2)}) %collective-permute-start.16) | collective-permute-done | bytes 40992 | tf_op jit(solution)/shard_map/ppermute | solution.py:566
  55.8 1.6 %collective-permute-start.20 = (bf16[2,32,256]{2,1,0:T(8,128)(2,1)S(1)}, bf16[2,32,256]{2,1,0:T(8,128)(2,1)S(1)}, u32[]{:S(2)}, u32[]{:S(2)}) collective-permute-start(bf16[2,32,256]{2,1,0:T(8,128)(2,1)S(1)} %get-tuple-element.63.refs_8_), channel_id=1, source_target_pairs={{0,1},{1,0},{2,3},{3,2},{4,5},{5,4},{6,7},{7,6},{8,9},{9,8},{10,11... | collective-permute-start | bytes 98312 | tf_op jit(solution)/shard_map/ppermute | solution.py:580
  57.4 1.7 %collective-permute-start.22 = (bf16[2,32,256]{2,1,0:T(8,128)(2,1)S(1)}, bf16[2,32,256]{2,1,0:T(8,128)(2,1)S(1)}, u32[]{:S(2)}, u32[]{:S(2)}) collective-permute-start(bf16[2,32,256]{2,1,0:T(8,128)(2,1)S(1)} %get-tuple-element.64), channel_id=1, source_target_pairs={{0,25},{1,24},{8,17},{9,16},{16,9},{17,8},{24,1},{25,0},{2,27},{3,... | collective-permute-start | bytes 98312 | tf_op jit(solution)/shard_map/ppermute | solution.py:576
  59.1 2.3 %last_results.1 = (bf16[1,4,32,1280]{3,2,1,0:T(8,128)(2,1)}, bf16[1,4,32,1280]{3,2,1,0:T(8,128)(2,1)}, f32[1,2,128,1280]{3,2,1,0:T(8,128)}) custom-call(bf16[32,640]{1,0:T(8,128)(2,1)S(1)} %later_latents.1.refs_0_, bf16[32,640]{1,0:T(8,128)(2,1)S(1)} %collective-permute-done.14.refs_1_, bf16[32,640]{1,0:T(8,128)(2,1)S(1)} %collective-permute-done.15.refs_2_, ...), custom_call_target="tpu_custom_call" | custom-call | flops 220000000 | tf_op jit(solution)/shard_map/last_results/pallas_call | solution.py:52
  61.6 1.4 %down_grads.1 = f32[1,2,640,256]{3,2,1,0:T(8,128)} custom-call(bf16[2,32,2560]{2,1,0:T(8,128)(2,1)S(1)} %get-tuple-element.54.refs_10_.refs_0_, bf16[2,32,2560]{2,1,0:T(8,128)(2,1)S(1)} %collective-permute-done.8.refs_0_.refs_11_.refs_1_, bf16[2,32,2560]{2,1,0:T(8,128)(2,1)S(1)} %get-tuple-element.55.refs_12_.refs_2_, ...), custom_call_target="tpu_custom_call" | custom-call | flops 1650000000 | tf_op jit(solution)/shard_map/down_grads/pallas_call | solution.py:52
  (49 shorter events, 2.8 us)
Async XLA Ops:
  0.6 10.6 %copy-start.5 = (f32[1,4,1280]{2,1,0:T(4,128)S(1)}, f32[1,4,1280]{2,1,0:T(4,128)}, u32[]{:S(2)}) copy-start(f32[1,4,1280]{2,1,0:T(4,128)} %refs_6_.5) | copy-start | bytes 61444
  0.6 10.6 %copy-start = (bf16[2,1,4,32,1280]{4,3,2,1,0:T(8,128)(2,1)S(1)}, bf16[2,1,4,32,1280]{4,3,2,1,0:T(8,128)(2,1)}, u32[]{:S(2)}) copy-start(bf16[2,1,4,32,1280]{4,3,2,1,0:T(8,128)(2,1)} %refs_8_.5) | copy-start | bytes 1966084
  0.7 10.6 %copy-start.3 = (bf16[1,4,32,1280]{3,2,1,0:T(8,128)(2,1)S(1)}, bf16[1,4,32,1280]{3,2,1,0:T(8,128)(2,1)}, u32[]{:S(2)}) copy-start(bf16[1,4,32,1280]{3,2,1,0:T(8,128)(2,1)} %refs_9_.3) | copy-start | bytes 983044
  5.6 8.0 %collective-permute-start = (bf16[32,1152]{1,0:T(8,128)(2,1)}, bf16[32,1152]{1,0:T(8,128)(2,1)S(1)}, u32[]{:S(2)}, u32[]{:S(2)}) collective-permute-start(bf16[32,1152]{1,0:T(8,128)(2,1)} %get-tuple-element.36.refs_4_), channel_id=1, source_target_pairs={{0,2},{2,0},{4,6},{6,4},{1,3},{3,1},{5,7},{7,5},{8,10},{10,8},{12,... | collective-permute-start | bytes 221192 | tf_op jit(solution)/shard_map/ppermute | solution.py:566
  8.6 8.0 %collective-permute-start.1 = (bf16[32,1152]{1,0:T(8,128)(2,1)}, bf16[32,1152]{1,0:T(8,128)(2,1)S(1)}, u32[]{:S(2)}, u32[]{:S(2)}) collective-permute-start(bf16[32,1152]{1,0:T(8,128)(2,1)} %get-tuple-element.38), channel_id=1, source_target_pairs={{0,4},{2,6},{4,0},{6,2},{1,5},{3,7},{5,1},{7,3},{8,12},{10,14},{12... | collective-permute-start | bytes 221192 | tf_op jit(solution)/shard_map/ppermute | solution.py:566
  11.2 6.5 %collective-permute-start.2 = (bf16[32,1152]{1,0:T(8,128)(2,1)}, bf16[32,1152]{1,0:T(8,128)(2,1)S(1)}, u32[]{:S(2)}, u32[]{:S(2)}) collective-permute-start(bf16[32,1152]{1,0:T(8,128)(2,1)} %get-tuple-element.39), channel_id=1, source_target_pairs={{0,6},{2,4},{4,2},{6,0},{1,7},{3,5},{5,3},{7,1},{8,14},{10,12},{12... | collective-permute-start | bytes 221192 | tf_op jit(solution)/shard_map/ppermute | solution.py:566
  11.2 0.9 %copy-start.8 = (bf16[32,1152]{1,0:T(8,128)(2,1)S(1)}, bf16[32,1152]{1,0:T(8,128)(2,1)}, u32[]{:S(2)}) copy-start(bf16[32,1152]{1,0:T(8,128)(2,1)} %get-tuple-element.36.refs_4_) | copy-start | bytes 221188
  13.1 16.5 %collective-permute-start.12 = (bf16[2,32,3840]{2,1,0:T(8,128)(2,1)S(1)}, bf16[2,32,3840]{2,1,0:T(8,128)(2,1)S(1)}, u32[]{:S(2)}, u32[]{:S(2)}) collective-permute-start(bf16[2,32,3840]{2,1,0:T(8,128)(2,1)S(1)} %get-tuple-element.50), channel_id=1, source_target_pairs={{0,24},{1,25},{8,16},{9,17},{16,8},{17,9},{24,0},{25,1},{2,26},{3,... | collective-permute-start | bytes 1474568 | tf_op jit(solution)/shard_map/ppermute | solution.py:576
  17.7 6.2 %copy-start.1 = (bf16[1,4,1280,256]{3,2,1,0:T(8,128)(2,1)S(1)}, bf16[1,4,1280,256]{3,2,1,0:T(8,128)(2,1)}, u32[]{:S(2)}) copy-start(bf16[1,4,1280,256]{3,2,1,0:T(8,128)(2,1)} %refs_0_.5) | copy-start | bytes 7864324
  17.7 6.2 %copy-start.2 = (bf16[1,4,256,1280]{3,2,1,0:T(8,128)(2,1)S(1)}, bf16[1,4,256,1280]{3,2,1,0:T(8,128)(2,1)}, u32[]{:S(2)}) copy-start(bf16[1,4,256,1280]{3,2,1,0:T(8,128)(2,1)} %refs_1_.5) | copy-start | bytes 7864324
  17.9 6.3 %collective-permute-start.3 = (bf16[32,1152]{1,0:T(8,128)(2,1)S(1)}, bf16[32,1152]{1,0:T(8,128)(2,1)S(1)}, u32[]{:S(2)}, u32[]{:S(2)}) collective-permute-start(bf16[32,1152]{1,0:T(8,128)(2,1)S(1)} %get-tuple-element.40.refs_2_.refs_0_), channel_id=1, source_target_pairs={{0,2},{2,0},{4,6},{6,4},{1,3},{3,1},{5,7},{7,5},{8,10},{10,8},{12,... | collective-permute-start | bytes 221192 | tf_op jit(solution)/shard_map/ppermute | solution.py:566
  19.1 6.8 %collective-permute-start.4 = (bf16[32,1152]{1,0:T(8,128)(2,1)S(1)}, bf16[32,1152]{1,0:T(8,128)(2,1)S(1)}, u32[]{:S(2)}, u32[]{:S(2)}) collective-permute-start(bf16[32,1152]{1,0:T(8,128)(2,1)S(1)} %get-tuple-element.40.refs_2_.refs_0_), channel_id=1, source_target_pairs={{0,4},{2,6},{4,0},{6,2},{1,5},{3,7},{5,1},{7,3},{8,12},{10,14},{12... | collective-permute-start | bytes 221192 | tf_op jit(solution)/shard_map/ppermute | solution.py:566
  20.8 6.3 %collective-permute-start.5 = (bf16[32,1152]{1,0:T(8,128)(2,1)S(1)}, bf16[32,1152]{1,0:T(8,128)(2,1)S(1)}, u32[]{:S(2)}, u32[]{:S(2)}) collective-permute-start(bf16[32,1152]{1,0:T(8,128)(2,1)S(1)} %get-tuple-element.40.refs_2_.refs_0_), channel_id=1, source_target_pairs={{0,6},{2,4},{4,2},{6,0},{1,7},{3,5},{5,3},{7,1},{8,14},{10,12},{12... | collective-permute-start | bytes 221192 | tf_op jit(solution)/shard_map/ppermute | solution.py:566
  22.4 4.6 %copy-start.4 = (bf16[1,4,32,1280]{3,2,1,0:T(8,128)(2,1)S(1)}, bf16[1,4,32,1280]{3,2,1,0:T(8,128)(2,1)}, u32[]{:S(2)}) copy-start(bf16[1,4,32,1280]{3,2,1,0:T(8,128)(2,1)} %refs_7_.4) | copy-start | bytes 983044
  22.4 8.9 %collective-permute-start.8 = (bf16[2,32,2560]{2,1,0:T(8,128)(2,1)S(1)}, bf16[2,32,2560]{2,1,0:T(8,128)(2,1)S(1)}, u32[]{:S(2)}, u32[]{:S(2)}) collective-permute-start(bf16[2,32,2560]{2,1,0:T(8,128)(2,1)S(1)} %get-tuple-element.44), channel_id=1, source_target_pairs={{0,1},{1,0},{2,3},{3,2},{4,5},{5,4},{6,7},{7,6},{8,9},{9,8},{10,11... | collective-permute-start | bytes 983048 | tf_op jit(solution)/shard_map/ppermute | solution.py:580
  27.8 8.0 %copy-start.6 = (bf16[1,2,32,1280]{3,2,1,0:T(8,128)(2,1)S(1)}, bf16[1,2,32,1280]{3,2,1,0:T(8,128)(2,1)}, u32[]{:S(2)}) copy-start(bf16[1,2,32,1280]{3,2,1,0:T(8,128)(2,1)} %refs_3_.3) | copy-start | bytes 491524
  27.8 8.0 %copy-start.7 = (bf16[1,2,32,1280]{3,2,1,0:T(8,128)(2,1)S(1)}, bf16[1,2,32,1280]{3,2,1,0:T(8,128)(2,1)}, u32[]{:S(2)}) copy-start(bf16[1,2,32,1280]{3,2,1,0:T(8,128)(2,1)} %refs_4_.3) | copy-start | bytes 491524
  28.5 2.7 %collective-permute-start.6 = (bf16[4,32,1280]{2,1,0:T(8,128)(2,1)S(1)}, bf16[4,32,1280]{2,1,0:T(8,128)(2,1)S(1)}, u32[]{:S(2)}, u32[]{:S(2)}) collective-permute-start(bf16[4,32,1280]{2,1,0:T(8,128)(2,1)S(1)} %get-tuple-element.43), channel_id=1, source_target_pairs={{0,8},{8,0},{16,24},{24,16},{1,9},{9,1},{17,25},{25,17},{2,10},{10... | collective-permute-start | bytes 983048 | tf_op jit(solution)/shard_map/ppermute | solution.py:608
  28.6 7.1 %collective-permute-start.7 = (bf16[4,32,1280]{2,1,0:T(8,128)(2,1)S(1)}, bf16[4,32,1280]{2,1,0:T(8,128)(2,1)S(1)}, u32[]{:S(2)}, u32[]{:S(2)}) collective-permute-start(bf16[4,32,1280]{2,1,0:T(8,128)(2,1)S(1)} %second_results.1.refs_10_.refs_2_.refs_1_), channel_id=1, source_target_pairs={{0,2},{2,0},{4,6},{6,4},{8,16},{10,18},{12,20},{14,22},{16,8},{18,... | collective-permute-start | bytes 983048 | tf_op jit(solution)/shard_map/ppermute | solution.py:604
  29.7 13.4 %collective-permute-start.13 = (bf16[2,32,2560]{2,1,0:T(8,128)(2,1)S(1)}, bf16[2,32,2560]{2,1,0:T(8,128)(2,1)S(1)}, u32[]{:S(2)}, u32[]{:S(2)}) collective-permute-start(bf16[2,32,2560]{2,1,0:T(8,128)(2,1)S(1)} %get-tuple-element.51), channel_id=1, source_target_pairs={{0,1},{1,0},{2,3},{3,2},{4,5},{5,4},{6,7},{7,6},{8,9},{9,8},{10,11... | collective-permute-start | bytes 983048 | tf_op jit(solution)/shard_map/ppermute | solution.py:580
  37.1 6.1 %collective-permute-start.9 = (bf16[32,640]{1,0:T(8,128)(2,1)S(1)}, bf16[32,640]{1,0:T(8,128)(2,1)S(1)}, u32[]{:S(2)}, u32[]{:S(2)}) collective-permute-start(bf16[32,640]{1,0:T(8,128)(2,1)S(1)} %get-tuple-element.46), channel_id=1, source_target_pairs={{0,2},{2,0},{4,6},{6,4},{1,3},{3,1},{5,7},{7,5},{8,10},{10,8},{12,... | collective-permute-start | bytes 122888 | tf_op jit(solution)/shard_map/ppermute | solution.py:566
  38.1 6.8 %collective-permute-start.10 = (bf16[32,640]{1,0:T(8,128)(2,1)S(1)}, bf16[32,640]{1,0:T(8,128)(2,1)S(1)}, u32[]{:S(2)}, u32[]{:S(2)}) collective-permute-start(bf16[32,640]{1,0:T(8,128)(2,1)S(1)} %get-tuple-element.47), channel_id=1, source_target_pairs={{0,4},{2,6},{4,0},{6,2},{1,5},{3,7},{5,1},{7,3},{8,12},{10,14},{12... | collective-permute-start | bytes 122888 | tf_op jit(solution)/shard_map/ppermute | solution.py:566
  39.9 5.8 %collective-permute-start.11 = (bf16[32,640]{1,0:T(8,128)(2,1)S(1)}, bf16[32,640]{1,0:T(8,128)(2,1)S(1)}, u32[]{:S(2)}, u32[]{:S(2)}) collective-permute-start(bf16[32,640]{1,0:T(8,128)(2,1)S(1)} %get-tuple-element.48), channel_id=1, source_target_pairs={{0,6},{2,4},{4,2},{6,0},{1,7},{3,5},{5,3},{7,1},{8,14},{10,12},{12... | collective-permute-start | bytes 122888 | tf_op jit(solution)/shard_map/ppermute | solution.py:566
  41.6 15.8 %collective-permute-start.17 = (bf16[2,32,1792]{2,1,0:T(8,128)(2,1)S(1)}, bf16[2,32,1792]{2,1,0:T(8,128)(2,1)S(1)}, u32[]{:S(2)}, u32[]{:S(2)}) collective-permute-start(bf16[2,32,1792]{2,1,0:T(8,128)(2,1)S(1)} %get-tuple-element.58), channel_id=1, source_target_pairs={{0,1},{1,0},{2,3},{3,2},{4,5},{5,4},{6,7},{7,6},{8,9},{9,8},{10,11... | collective-permute-start | bytes 688136 | tf_op jit(solution)/shard_map/ppermute | solution.py:580
  43.2 16.0 %collective-permute-start.18 = (bf16[2,32,1792]{2,1,0:T(8,128)(2,1)S(1)}, bf16[2,32,1792]{2,1,0:T(8,128)(2,1)S(1)}, u32[]{:S(2)}, u32[]{:S(2)}) collective-permute-start(bf16[2,32,1792]{2,1,0:T(8,128)(2,1)S(1)} %get-tuple-element.59), channel_id=1, source_target_pairs={{0,24},{1,25},{8,16},{9,17},{16,8},{17,9},{24,0},{25,1},{2,26},{3,... | collective-permute-start | bytes 688136 | tf_op jit(solution)/shard_map/ppermute | solution.py:576
  43.2 15.9 %collective-permute-start.19 = (bf16[2,32,1792]{2,1,0:T(8,128)(2,1)S(1)}, bf16[2,32,1792]{2,1,0:T(8,128)(2,1)S(1)}, u32[]{:S(2)}, u32[]{:S(2)}) collective-permute-start(bf16[2,32,1792]{2,1,0:T(8,128)(2,1)S(1)} %get-tuple-element.60), channel_id=1, source_target_pairs={{0,25},{1,24},{8,17},{9,16},{16,9},{17,8},{24,1},{25,0},{2,27},{3,... | collective-permute-start | bytes 688136 | tf_op jit(solution)/shard_map/ppermute | solution.py:576
  46.0 4.0 %collective-permute-start.14 = (bf16[32,640]{1,0:T(8,128)(2,1)S(1)}, bf16[32,640]{1,0:T(8,128)(2,1)S(1)}, u32[]{:S(2)}, u32[]{:S(2)}) collective-permute-start(bf16[32,640]{1,0:T(8,128)(2,1)S(1)} %later_latents.1.refs_0_), channel_id=1, source_target_pairs={{0,2},{2,0},{4,6},{6,4},{1,3},{3,1},{5,7},{7,5},{8,10},{10,8},{12,... | collective-permute-start | bytes 122888 | tf_op jit(solution)/shard_map/ppermute | solution.py:566
  46.0 5.7 %collective-permute-start.15 = (bf16[32,640]{1,0:T(8,128)(2,1)S(1)}, bf16[32,640]{1,0:T(8,128)(2,1)S(1)}, u32[]{:S(2)}, u32[]{:S(2)}) collective-permute-start(bf16[32,640]{1,0:T(8,128)(2,1)S(1)} %later_latents.1.refs_0_), channel_id=1, source_target_pairs={{0,4},{2,6},{4,0},{6,2},{1,5},{3,7},{5,1},{7,3},{8,12},{10,14},{12... | collective-permute-start | bytes 122888 | tf_op jit(solution)/shard_map/ppermute | solution.py:566
  50.0 5.8 %collective-permute-start.16 = (bf16[32,640]{1,0:T(8,128)(2,1)S(1)}, bf16[32,640]{1,0:T(8,128)(2,1)S(1)}, u32[]{:S(2)}, u32[]{:S(2)}) collective-permute-start(bf16[32,640]{1,0:T(8,128)(2,1)S(1)} %later_latents.1.refs_0_), channel_id=1, source_target_pairs={{0,6},{2,4},{4,2},{6,0},{1,7},{3,5},{5,3},{7,1},{8,14},{10,12},{12... | collective-permute-start | bytes 122888 | tf_op jit(solution)/shard_map/ppermute | solution.py:566
  55.8 5.6 %collective-permute-start.20 = (bf16[2,32,256]{2,1,0:T(8,128)(2,1)S(1)}, bf16[2,32,256]{2,1,0:T(8,128)(2,1)S(1)}, u32[]{:S(2)}, u32[]{:S(2)}) collective-permute-start(bf16[2,32,256]{2,1,0:T(8,128)(2,1)S(1)} %get-tuple-element.63.refs_8_), channel_id=1, source_target_pairs={{0,1},{1,0},{2,3},{3,2},{4,5},{5,4},{6,7},{7,6},{8,9},{9,8},{10,11... | collective-permute-start | bytes 98312 | tf_op jit(solution)/shard_map/ppermute | solution.py:580
  57.4 4.0 %collective-permute-start.21 = (bf16[2,32,256]{2,1,0:T(8,128)(2,1)S(1)}, bf16[2,32,256]{2,1,0:T(8,128)(2,1)S(1)}, u32[]{:S(2)}, u32[]{:S(2)}) collective-permute-start(bf16[2,32,256]{2,1,0:T(8,128)(2,1)S(1)} %get-tuple-element.64), channel_id=1, source_target_pairs={{0,24},{1,25},{8,16},{9,17},{16,8},{17,9},{24,0},{25,1},{2,26},{3,... | collective-permute-start | bytes 98312 | tf_op jit(solution)/shard_map/ppermute | solution.py:576
  57.4 4.2 %collective-permute-start.22 = (bf16[2,32,256]{2,1,0:T(8,128)(2,1)S(1)}, bf16[2,32,256]{2,1,0:T(8,128)(2,1)S(1)}, u32[]{:S(2)}, u32[]{:S(2)}) collective-permute-start(bf16[2,32,256]{2,1,0:T(8,128)(2,1)S(1)} %get-tuple-element.64), channel_id=1, source_target_pairs={{0,25},{1,24},{8,17},{9,16},{16,9},{17,8},{24,1},{25,0},{2,27},{3,... | collective-permute-start | bytes 98312 | tf_op jit(solution)/shard_map/ppermute | solution.py:576
  (1 other events, 0.9 us)

commit v6 on v5

--- a/solution.py
+++ b/solution.py
@@ -17,7 +17,8 @@
     "first_partials": 5.0,
     "early_factors": 0.3,
     "held_weights": 0.5,
-    "marker": 0.1,
+    "near_ready": 1,
+    "far_ready": 0.1,
     "first_latents": 4,
     "second_results": 0.8,
     "first_results": 0.8,
@@ -236,11 +237,11 @@
     )
 
 
-def marker(after):
+def marker(name, after):
     def body(out):
         out[...] = jnp.zeros(out.shape, out.dtype)
 
-    return call(body, [], [((8, LANES), F32)], "marker", after=after)
+    return call(body, [], [((8, LANES), F32)], name, after=after)
 
 
 def total(refs):
@@ -608,8 +609,8 @@
     from_first = lax.ppermute(first, "pipe", swap)
 
     early += across(early_share(groups, ticks, far, after=[second]))
-    ready_near = marker(early[1:groups])
-    ready = marker(early[groups + 1 :])
+    ready_near = marker("near_ready", [*early[1:groups], from_second])
+    ready = marker("far_ready", early[groups + 1 :])
 
     dealt, x, g = later_partials(
         parts, from_first, from_second, second, fresh, arriving, *weights, gains, after=ready_near

time: 63.7 us -> 62.9 us (0.987)
  waiting for transfers between devices: 18.2 us -> 16.9 us
    ppermute x1, waiting for transfers between devices: 4.47 us -> 2.98 us  [per_device(): from_second = lax.ppermute(second, ('pipe', 'tensor'), cross)]
    ppermute x1, starting transfers between devices: 0.07 us -> 0.74 us  [per_device(): from_first = lax.ppermute(first, 'pipe', swap)]
where the time goes in v6:
time: 62.9 us; the launch traced here: 62.2 us
  starting transfers between devices  30.1 us (48%)
  waiting for transfers between devices  16.9 us (27%)
  Pallas kernels  12.6 us (20%)
  local copies, waits for them, and re-layouts  1.8 us (3%)
  between operations  0.82 us (1%)
    ppermute x12, starting transfers between devices, around(): lax.ppermute(arrays[k], 'tensor', [(i, i ^ k) for i in range(parts)])  18.3 us
    ppermute x12, waiting for transfers between devices, around(): lax.ppermute(arrays[k], 'tensor', [(i, i ^ k) for i in range(parts)])  13.7 us
    pallas_call x15, Pallas kernels, call(): pl.pallas_call(run, in_specs=[pl.BlockSpec(memory_space=pl.ANY)] * raw +...  12.6 us
    ppermute x4, starting transfers between devices, across(): lax.ppermute(arrays[k], 'dp', [(i, i ^ k) for i in range(groups)])  6.16 us
    ppermute x5, starting transfers between devices, mirrored(): return lax.ppermute(far, ('pipe', 'dp'), pairs)  3.89 us
    ppermute x1, waiting for transfers between devices, per_device(): from_second = lax.ppermute(second, ('pipe', 'tensor'), cross)  2.98 us
    unnamed x20, local copies, waits for them, and re-layouts  1.8 us
  transfers between devices with their start and end apart: 23, of which 9 were waited for; matrix products, arithmetic and copies ran while one was open for 0% of the time, Pallas kernels for 10%

profile of v6, /device:TPU:0, one launch (start us, length us, event | category | flops | bytes accessed | tf_op | source)
XLA Modules:
  0.0 62.2 jit_solution(5363405026720005209)
XLA Ops:
  0.7 4.9 %first_partials.1 = (bf16[32,1152]{1,0:T(8,128)(2,1)}, bf16[32,1152]{1,0:T(8,128)(2,1)}, bf16[32,1152]{1,0:T(8,128)(2,1)}, bf16[32,1152]{1,0:T(8,128)(2,1)}) custom-call(bf16[1,4,1280,256]{3,2,1,0:T(8,128)(2,1)} %refs_0_.5, bf16[1,4,256,1280]{3,2,1,0:T(8,128)(2,1)} %refs_1_.5, f32[1,4,1280]{2,1,0:T(4,128)} %refs_6_.5, bf16[1,4,32,1280]{3,2,1,0:T(8,128)(2,1)} %refs_7_.4, ...), custom_call_target="tpu_custom_call" | custom-call | flops 5500000256 | tf_op jit(solution)/shard_map/first_partials/pallas_call | solution.py:53
  5.6 3.0 %collective-permute-start = (bf16[32,1152]{1,0:T(8,128)(2,1)}, bf16[32,1152]{1,0:T(8,128)(2,1)S(1)}, u32[]{:S(2)}, u32[]{:S(2)}) collective-permute-start(bf16[32,1152]{1,0:T(8,128)(2,1)} %get-tuple-element.36.refs_4_), channel_id=1, source_target_pairs={{0,2},{2,0},{4,6},{6,4},{1,3},{3,1},{5,7},{7,5},{8,10},{10,8},{12,... | collective-permute-start | bytes 221192 | tf_op jit(solution)/shard_map/ppermute | solution.py:567
  8.6 2.6 %collective-permute-start.1 = (bf16[32,1152]{1,0:T(8,128)(2,1)}, bf16[32,1152]{1,0:T(8,128)(2,1)S(1)}, u32[]{:S(2)}, u32[]{:S(2)}) collective-permute-start(bf16[32,1152]{1,0:T(8,128)(2,1)} %get-tuple-element.38), channel_id=1, source_target_pairs={{0,4},{2,6},{4,0},{6,2},{1,5},{3,7},{5,1},{7,3},{8,12},{10,14},{12... | collective-permute-start | bytes 221192 | tf_op jit(solution)/shard_map/ppermute | solution.py:567
  11.2 0.9 %copy-done.8 = bf16[32,1152]{1,0:T(8,128)(2,1)S(1)} copy-done((bf16[32,1152]{1,0:T(8,128)(2,1)S(1)}, bf16[32,1152]{1,0:T(8,128)(2,1)}, u32[]{:S(2)}) %copy-start.8) | copy-done | bytes 73752
  12.1 0.9 %copy-done.9 = bf16[32,1152]{1,0:T(8,128)(2,1)S(1)} copy-done((bf16[32,1152]{1,0:T(8,128)(2,1)S(1)}, bf16[32,1152]{1,0:T(8,128)(2,1)}, u32[]{:S(2)}) %copy-start.9) | copy-done | bytes 73752
  13.6 3.0 %collective-permute-done.1.refs_2_ = bf16[32,1152]{1,0:T(8,128)(2,1)S(1)} collective-permute-done((bf16[32,1152]{1,0:T(8,128)(2,1)}, bf16[32,1152]{1,0:T(8,128)(2,1)S(1)}, u32[]{:S(2)}, u32[]{:S(2)}) %collective-permute-start.1) | collective-permute-done | bytes 73760 | tf_op jit(solution)/shard_map/ppermute | solution.py:567
  16.6 1.1 %collective-permute-done.2.refs_3_ = bf16[32,1152]{1,0:T(8,128)(2,1)S(1)} collective-permute-done((bf16[32,1152]{1,0:T(8,128)(2,1)}, bf16[32,1152]{1,0:T(8,128)(2,1)S(1)}, u32[]{:S(2)}, u32[]{:S(2)}) %collective-permute-start.2) | collective-permute-done | bytes 73760 | tf_op jit(solution)/shard_map/ppermute | solution.py:567
  17.9 1.1 %collective-permute-start.3 = (bf16[32,1152]{1,0:T(8,128)(2,1)S(1)}, bf16[32,1152]{1,0:T(8,128)(2,1)S(1)}, u32[]{:S(2)}, u32[]{:S(2)}) collective-permute-start(bf16[32,1152]{1,0:T(8,128)(2,1)S(1)} %get-tuple-element.40.refs_2_.refs_0_), channel_id=1, source_target_pairs={{0,2},{2,0},{4,6},{6,4},{1,3},{3,1},{5,7},{7,5},{8,10},{10,8},{12,... | collective-permute-start | bytes 221192 | tf_op jit(solution)/shard_map/ppermute | solution.py:567
  19.1 1.7 %collective-permute-start.4 = (bf16[32,1152]{1,0:T(8,128)(2,1)S(1)}, bf16[32,1152]{1,0:T(8,128)(2,1)S(1)}, u32[]{:S(2)}, u32[]{:S(2)}) collective-permute-start(bf16[32,1152]{1,0:T(8,128)(2,1)S(1)} %get-tuple-element.40.refs_2_.refs_0_), channel_id=1, source_target_pairs={{0,4},{2,6},{4,0},{6,2},{1,5},{3,7},{5,1},{7,3},{8,12},{10,14},{12... | collective-permute-start | bytes 221192 | tf_op jit(solution)/shard_map/ppermute | solution.py:567
  20.8 1.6 %collective-permute-start.5 = (bf16[32,1152]{1,0:T(8,128)(2,1)S(1)}, bf16[32,1152]{1,0:T(8,128)(2,1)S(1)}, u32[]{:S(2)}, u32[]{:S(2)}) collective-permute-start(bf16[32,1152]{1,0:T(8,128)(2,1)S(1)} %get-tuple-element.40.refs_2_.refs_0_), channel_id=1, source_target_pairs={{0,6},{2,4},{4,2},{6,0},{1,7},{3,5},{5,3},{7,1},{8,14},{10,12},{12... | collective-permute-start | bytes 221192 | tf_op jit(solution)/shard_map/ppermute | solution.py:567
  22.4 1.5 %collective-permute-start.8 = (bf16[2,32,2560]{2,1,0:T(8,128)(2,1)S(1)}, bf16[2,32,2560]{2,1,0:T(8,128)(2,1)S(1)}, u32[]{:S(2)}, u32[]{:S(2)}) collective-permute-start(bf16[2,32,2560]{2,1,0:T(8,128)(2,1)S(1)} %get-tuple-element.44), channel_id=1, source_target_pairs={{0,1},{1,0},{2,3},{3,2},{4,5},{5,4},{6,7},{7,6},{8,9},{9,8},{10,11... | collective-permute-start | bytes 983048 | tf_op jit(solution)/shard_map/ppermute | solution.py:581
  24.3 1.6 %collective-permute-done.4.refs_2_ = bf16[32,1152]{1,0:T(8,128)(2,1)S(1)} collective-permute-done((bf16[32,1152]{1,0:T(8,128)(2,1)S(1)}, bf16[32,1152]{1,0:T(8,128)(2,1)S(1)}, u32[]{:S(2)}, u32[]{:S(2)}) %collective-permute-start.4) | collective-permute-done | bytes 73760 | tf_op jit(solution)/shard_map/ppermute | solution.py:567
  25.8 1.2 %collective-permute-done.5.refs_3_ = bf16[32,1152]{1,0:T(8,128)(2,1)S(1)} collective-permute-done((bf16[32,1152]{1,0:T(8,128)(2,1)S(1)}, bf16[32,1152]{1,0:T(8,128)(2,1)S(1)}, u32[]{:S(2)}, u32[]{:S(2)}) %collective-permute-start.5) | collective-permute-done | bytes 73760 | tf_op jit(solution)/shard_map/ppermute | solution.py:567
  27.8 1.0 %collective-permute-start.7 = (bf16[4,32,1280]{2,1,0:T(8,128)(2,1)S(1)}, bf16[4,32,1280]{2,1,0:T(8,128)(2,1)S(1)}, u32[]{:S(2)}, u32[]{:S(2)}) collective-permute-start(bf16[4,32,1280]{2,1,0:T(8,128)(2,1)S(1)} %second_results.1.refs_10_.refs_2_.refs_1_), channel_id=1, source_target_pairs={{0,2},{2,0},{4,6},{6,4},{8,16},{10,18},{12,20},{14,22},{16,8},{18,... | collective-permute-start | bytes 983048 | tf_op jit(solution)/shard_map/ppermute | solution.py:605
  29.5 0.7 %collective-permute-start.6 = (bf16[4,32,1280]{2,1,0:T(8,128)(2,1)S(1)}, bf16[4,32,1280]{2,1,0:T(8,128)(2,1)S(1)}, u32[]{:S(2)}, u32[]{:S(2)}) collective-permute-start(bf16[4,32,1280]{2,1,0:T(8,128)(2,1)S(1)} %get-tuple-element.43), channel_id=1, source_target_pairs={{0,8},{8,0},{16,24},{24,16},{1,9},{9,1},{17,25},{25,17},{2,10},{10... | collective-permute-start | bytes 983048 | tf_op jit(solution)/shard_map/ppermute | solution.py:609
  30.4 1.6 %collective-permute-start.13 = (bf16[2,32,2560]{2,1,0:T(8,128)(2,1)S(1)}, bf16[2,32,2560]{2,1,0:T(8,128)(2,1)S(1)}, u32[]{:S(2)}, u32[]{:S(2)}) collective-permute-start(bf16[2,32,2560]{2,1,0:T(8,128)(2,1)S(1)} %get-tuple-element.51), channel_id=1, source_target_pairs={{0,1},{1,0},{2,3},{3,2},{4,5},{5,4},{6,7},{7,6},{8,9},{9,8},{10,11... | collective-permute-start | bytes 983048 | tf_op jit(solution)/shard_map/ppermute | solution.py:581
  31.9 3.0 %collective-permute-done.7.refs_1_ = bf16[4,32,1280]{2,1,0:T(8,128)(2,1)S(1)} collective-permute-done((bf16[4,32,1280]{2,1,0:T(8,128)(2,1)S(1)}, bf16[4,32,1280]{2,1,0:T(8,128)(2,1)S(1)}, u32[]{:S(2)}, u32[]{:S(2)}) %collective-permute-start.7) | collective-permute-done | bytes 327712 | tf_op jit(solution)/shard_map/ppermute | solution.py:605
  34.9 1.3 %later_partials.1 = (bf16[32,640]{1,0:T(8,128)(2,1)S(1)}, bf16[32,640]{1,0:T(8,128)(2,1)S(1)}, bf16[32,640]{1,0:T(8,128)(2,1)S(1)}, bf16[32,640]{1,0:T(8,128)(2,...) custom-call(bf16[4,32,1280]{2,1,0:T(8,128)(2,1)S(1)} %collective-permute-done.6.refs_0_, ...), custom_call_target="tpu_custom_call" | custom-call | flops 1430000000 | tf_op jit(solution)/shard_map/later_partials/pallas_call | solution.py:53
  36.2 1.0 %collective-permute-start.9 = (bf16[32,640]{1,0:T(8,128)(2,1)S(1)}, bf16[32,640]{1,0:T(8,128)(2,1)S(1)}, u32[]{:S(2)}, u32[]{:S(2)}) collective-permute-start(bf16[32,640]{1,0:T(8,128)(2,1)S(1)} %get-tuple-element.46), channel_id=1, source_target_pairs={{0,2},{2,0},{4,6},{6,4},{1,3},{3,1},{5,7},{7,5},{8,10},{10,8},{12,... | collective-permute-start | bytes 122888 | tf_op jit(solution)/shard_map/ppermute | solution.py:567
  37.3 1.8 %collective-permute-start.10 = (bf16[32,640]{1,0:T(8,128)(2,1)S(1)}, bf16[32,640]{1,0:T(8,128)(2,1)S(1)}, u32[]{:S(2)}, u32[]{:S(2)}) collective-permute-start(bf16[32,640]{1,0:T(8,128)(2,1)S(1)} %get-tuple-element.47), channel_id=1, source_target_pairs={{0,4},{2,6},{4,0},{6,2},{1,5},{3,7},{5,1},{7,3},{8,12},{10,14},{12... | collective-permute-start | bytes 122888 | tf_op jit(solution)/shard_map/ppermute | solution.py:567
  39.1 1.6 %collective-permute-start.11 = (bf16[32,640]{1,0:T(8,128)(2,1)S(1)}, bf16[32,640]{1,0:T(8,128)(2,1)S(1)}, u32[]{:S(2)}, u32[]{:S(2)}) collective-permute-start(bf16[32,640]{1,0:T(8,128)(2,1)S(1)} %get-tuple-element.48), channel_id=1, source_target_pairs={{0,6},{2,4},{4,2},{6,0},{1,7},{3,5},{5,3},{7,1},{8,14},{10,12},{12... | collective-permute-start | bytes 122888 | tf_op jit(solution)/shard_map/ppermute | solution.py:567
  40.8 1.6 %collective-permute-start.17 = (bf16[2,32,1792]{2,1,0:T(8,128)(2,1)S(1)}, bf16[2,32,1792]{2,1,0:T(8,128)(2,1)S(1)}, u32[]{:S(2)}, u32[]{:S(2)}) collective-permute-start(bf16[2,32,1792]{2,1,0:T(8,128)(2,1)S(1)} %get-tuple-element.58), channel_id=1, source_target_pairs={{0,1},{1,0},{2,3},{3,2},{4,5},{5,4},{6,7},{7,6},{8,9},{9,8},{10,11... | collective-permute-start | bytes 688136 | tf_op jit(solution)/shard_map/ppermute | solution.py:581
  42.4 1.7 %collective-permute-start.19 = (bf16[2,32,1792]{2,1,0:T(8,128)(2,1)S(1)}, bf16[2,32,1792]{2,1,0:T(8,128)(2,1)S(1)}, u32[]{:S(2)}, u32[]{:S(2)}) collective-permute-start(bf16[2,32,1792]{2,1,0:T(8,128)(2,1)S(1)} %get-tuple-element.60), channel_id=1, source_target_pairs={{0,25},{1,24},{8,17},{9,16},{16,9},{17,8},{24,1},{25,0},{2,27},{3,... | collective-permute-start | bytes 688136 | tf_op jit(solution)/shard_map/ppermute | solution.py:577
  44.1 0.8 %collective-permute-done.11.refs_3_ = bf16[32,640]{1,0:T(8,128)(2,1)S(1)} collective-permute-done((bf16[32,640]{1,0:T(8,128)(2,1)S(1)}, bf16[32,640]{1,0:T(8,128)(2,1)S(1)}, u32[]{:S(2)}, u32[]{:S(2)}) %collective-permute-start.11) | collective-permute-done | bytes 40992 | tf_op jit(solution)/shard_map/ppermute | solution.py:567
  45.2 2.1 %collective-permute-start.15 = (bf16[32,640]{1,0:T(8,128)(2,1)S(1)}, bf16[32,640]{1,0:T(8,128)(2,1)S(1)}, u32[]{:S(2)}, u32[]{:S(2)}) collective-permute-start(bf16[32,640]{1,0:T(8,128)(2,1)S(1)} %later_latents.1.refs_0_), channel_id=1, source_target_pairs={{0,4},{2,6},{4,0},{6,2},{1,5},{3,7},{5,1},{7,3},{8,12},{10,14},{12... | collective-permute-start | bytes 122888 | tf_op jit(solution)/shard_map/ppermute | solution.py:567
  47.3 1.8 %collective-permute-done.14.refs_1_ = bf16[32,640]{1,0:T(8,128)(2,1)S(1)} collective-permute-done((bf16[32,640]{1,0:T(8,128)(2,1)S(1)}, bf16[32,640]{1,0:T(8,128)(2,1)S(1)}, u32[]{:S(2)}, u32[]{:S(2)}) %collective-permute-start.14) | collective-permute-done | bytes 40992 | tf_op jit(solution)/shard_map/ppermute | solution.py:567
  49.2 1.6 %collective-permute-start.16 = (bf16[32,640]{1,0:T(8,128)(2,1)S(1)}, bf16[32,640]{1,0:T(8,128)(2,1)S(1)}, u32[]{:S(2)}, u32[]{:S(2)}) collective-permute-start(bf16[32,640]{1,0:T(8,128)(2,1)S(1)} %later_latents.1.refs_0_), channel_id=1, source_target_pairs={{0,6},{2,4},{4,2},{6,0},{1,7},{3,5},{5,3},{7,1},{8,14},{10,12},{12... | collective-permute-start | bytes 122888 | tf_op jit(solution)/shard_map/ppermute | solution.py:567
  50.8 4.2 %collective-permute-done.16.refs_3_ = bf16[32,640]{1,0:T(8,128)(2,1)S(1)} collective-permute-done((bf16[32,640]{1,0:T(8,128)(2,1)S(1)}, bf16[32,640]{1,0:T(8,128)(2,1)S(1)}, u32[]{:S(2)}, u32[]{:S(2)}) %collective-permute-start.16) | collective-permute-done | bytes 40992 | tf_op jit(solution)/shard_map/ppermute | solution.py:567
  55.0 1.6 %collective-permute-start.20 = (bf16[2,32,256]{2,1,0:T(8,128)(2,1)S(1)}, bf16[2,32,256]{2,1,0:T(8,128)(2,1)S(1)}, u32[]{:S(2)}, u32[]{:S(2)}) collective-permute-start(bf16[2,32,256]{2,1,0:T(8,128)(2,1)S(1)} %get-tuple-element.63.refs_8_), channel_id=1, source_target_pairs={{0,1},{1,0},{2,3},{3,2},{4,5},{5,4},{6,7},{7,6},{8,9},{9,8},{10,11... | collective-permute-start | bytes 98312 | tf_op jit(solution)/shard_map/ppermute | solution.py:581
  56.6 1.7 %collective-permute-start.22 = (bf16[2,32,256]{2,1,0:T(8,128)(2,1)S(1)}, bf16[2,32,256]{2,1,0:T(8,128)(2,1)S(1)}, u32[]{:S(2)}, u32[]{:S(2)}) collective-permute-start(bf16[2,32,256]{2,1,0:T(8,128)(2,1)S(1)} %get-tuple-element.64), channel_id=1, source_target_pairs={{0,25},{1,24},{8,17},{9,16},{16,9},{17,8},{24,1},{25,0},{2,27},{3,... | collective-permute-start | bytes 98312 | tf_op jit(solution)/shard_map/ppermute | solution.py:577
  58.3 2.3 %last_results.1 = (bf16[1,4,32,1280]{3,2,1,0:T(8,128)(2,1)}, bf16[1,4,32,1280]{3,2,1,0:T(8,128)(2,1)}, f32[1,2,128,1280]{3,2,1,0:T(8,128)}) custom-call(bf16[32,640]{1,0:T(8,128)(2,1)S(1)} %later_latents.1.refs_0_, bf16[32,640]{1,0:T(8,128)(2,1)S(1)} %collective-permute-done.14.refs_1_, bf16[32,640]{1,0:T(8,128)(2,1)S(1)} %collective-permute-done.15.refs_2_, ...), custom_call_target="tpu_custom_call" | custom-call | flops 220000000 | tf_op jit(solution)/shard_map/last_results/pallas_call | solution.py:53
  60.8 1.4 %down_grads.1 = f32[1,2,640,256]{3,2,1,0:T(8,128)} custom-call(bf16[2,32,2560]{2,1,0:T(8,128)(2,1)S(1)} %get-tuple-element.54.refs_10_.refs_0_, bf16[2,32,2560]{2,1,0:T(8,128)(2,1)S(1)} %collective-permute-done.8.refs_0_.refs_11_.refs_1_, bf16[2,32,2560]{2,1,0:T(8,128)(2,1)S(1)} %get-tuple-element.55.refs_12_.refs_2_, ...), custom_call_target="tpu_custom_call" | custom-call | flops 1650000000 | tf_op jit(solution)/shard_map/down_grads/pallas_call | solution.py:53
  (49 shorter events, 3.4 us)
Async XLA Ops:
  0.6 10.6 %copy-start.5 = (f32[1,4,1280]{2,1,0:T(4,128)S(1)}, f32[1,4,1280]{2,1,0:T(4,128)}, u32[]{:S(2)}) copy-start(f32[1,4,1280]{2,1,0:T(4,128)} %refs_6_.5) | copy-start | bytes 61444
  0.6 10.6 %copy-start = (bf16[2,1,4,32,1280]{4,3,2,1,0:T(8,128)(2,1)S(1)}, bf16[2,1,4,32,1280]{4,3,2,1,0:T(8,128)(2,1)}, u32[]{:S(2)}) copy-start(bf16[2,1,4,32,1280]{4,3,2,1,0:T(8,128)(2,1)} %refs_8_.5) | copy-start | bytes 1966084
  0.7 10.6 %copy-start.3 = (bf16[1,4,32,1280]{3,2,1,0:T(8,128)(2,1)S(1)}, bf16[1,4,32,1280]{3,2,1,0:T(8,128)(2,1)}, u32[]{:S(2)}) copy-start(bf16[1,4,32,1280]{3,2,1,0:T(8,128)(2,1)} %refs_9_.3) | copy-start | bytes 983044
  5.6 8.0 %collective-permute-start = (bf16[32,1152]{1,0:T(8,128)(2,1)}, bf16[32,1152]{1,0:T(8,128)(2,1)S(1)}, u32[]{:S(2)}, u32[]{:S(2)}) collective-permute-start(bf16[32,1152]{1,0:T(8,128)(2,1)} %get-tuple-element.36.refs_4_), channel_id=1, source_target_pairs={{0,2},{2,0},{4,6},{6,4},{1,3},{3,1},{5,7},{7,5},{8,10},{10,8},{12,... | collective-permute-start | bytes 221192 | tf_op jit(solution)/shard_map/ppermute | solution.py:567
  8.6 8.0 %collective-permute-start.1 = (bf16[32,1152]{1,0:T(8,128)(2,1)}, bf16[32,1152]{1,0:T(8,128)(2,1)S(1)}, u32[]{:S(2)}, u32[]{:S(2)}) collective-permute-start(bf16[32,1152]{1,0:T(8,128)(2,1)} %get-tuple-element.38), channel_id=1, source_target_pairs={{0,4},{2,6},{4,0},{6,2},{1,5},{3,7},{5,1},{7,3},{8,12},{10,14},{12... | collective-permute-start | bytes 221192 | tf_op jit(solution)/shard_map/ppermute | solution.py:567
  11.2 6.5 %collective-permute-start.2 = (bf16[32,1152]{1,0:T(8,128)(2,1)}, bf16[32,1152]{1,0:T(8,128)(2,1)S(1)}, u32[]{:S(2)}, u32[]{:S(2)}) collective-permute-start(bf16[32,1152]{1,0:T(8,128)(2,1)} %get-tuple-element.39), channel_id=1, source_target_pairs={{0,6},{2,4},{4,2},{6,0},{1,7},{3,5},{5,3},{7,1},{8,14},{10,12},{12... | collective-permute-start | bytes 221192 | tf_op jit(solution)/shard_map/ppermute | solution.py:567
  11.2 0.9 %copy-start.8 = (bf16[32,1152]{1,0:T(8,128)(2,1)S(1)}, bf16[32,1152]{1,0:T(8,128)(2,1)}, u32[]{:S(2)}) copy-start(bf16[32,1152]{1,0:T(8,128)(2,1)} %get-tuple-element.36.refs_4_) | copy-start | bytes 221188
  13.1 17.1 %collective-permute-start.12 = (bf16[2,32,3840]{2,1,0:T(8,128)(2,1)S(1)}, bf16[2,32,3840]{2,1,0:T(8,128)(2,1)S(1)}, u32[]{:S(2)}, u32[]{:S(2)}) collective-permute-start(bf16[2,32,3840]{2,1,0:T(8,128)(2,1)S(1)} %get-tuple-element.50), channel_id=1, source_target_pairs={{0,24},{1,25},{8,16},{9,17},{16,8},{17,9},{24,0},{25,1},{2,26},{3,... | collective-permute-start | bytes 1474568 | tf_op jit(solution)/shard_map/ppermute | solution.py:577
  17.7 6.2 %copy-start.1 = (bf16[1,4,1280,256]{3,2,1,0:T(8,128)(2,1)S(1)}, bf16[1,4,1280,256]{3,2,1,0:T(8,128)(2,1)}, u32[]{:S(2)}) copy-start(bf16[1,4,1280,256]{3,2,1,0:T(8,128)(2,1)} %refs_0_.5) | copy-start | bytes 7864324
  17.7 6.2 %copy-start.2 = (bf16[1,4,256,1280]{3,2,1,0:T(8,128)(2,1)S(1)}, bf16[1,4,256,1280]{3,2,1,0:T(8,128)(2,1)}, u32[]{:S(2)}) copy-start(bf16[1,4,256,1280]{3,2,1,0:T(8,128)(2,1)} %refs_1_.5) | copy-start | bytes 7864324
  17.9 6.3 %collective-permute-start.3 = (bf16[32,1152]{1,0:T(8,128)(2,1)S(1)}, bf16[32,1152]{1,0:T(8,128)(2,1)S(1)}, u32[]{:S(2)}, u32[]{:S(2)}) collective-permute-start(bf16[32,1152]{1,0:T(8,128)(2,1)S(1)} %get-tuple-element.40.refs_2_.refs_0_), channel_id=1, source_target_pairs={{0,2},{2,0},{4,6},{6,4},{1,3},{3,1},{5,7},{7,5},{8,10},{10,8},{12,... | collective-permute-start | bytes 221192 | tf_op jit(solution)/shard_map/ppermute | solution.py:567
  19.1 6.8 %collective-permute-start.4 = (bf16[32,1152]{1,0:T(8,128)(2,1)S(1)}, bf16[32,1152]{1,0:T(8,128)(2,1)S(1)}, u32[]{:S(2)}, u32[]{:S(2)}) collective-permute-start(bf16[32,1152]{1,0:T(8,128)(2,1)S(1)} %get-tuple-element.40.refs_2_.refs_0_), channel_id=1, source_target_pairs={{0,4},{2,6},{4,0},{6,2},{1,5},{3,7},{5,1},{7,3},{8,12},{10,14},{12... | collective-permute-start | bytes 221192 | tf_op jit(solution)/shard_map/ppermute | solution.py:567
  20.8 6.3 %collective-permute-start.5 = (bf16[32,1152]{1,0:T(8,128)(2,1)S(1)}, bf16[32,1152]{1,0:T(8,128)(2,1)S(1)}, u32[]{:S(2)}, u32[]{:S(2)}) collective-permute-start(bf16[32,1152]{1,0:T(8,128)(2,1)S(1)} %get-tuple-element.40.refs_2_.refs_0_), channel_id=1, source_target_pairs={{0,6},{2,4},{4,2},{6,0},{1,7},{3,5},{5,3},{7,1},{8,14},{10,12},{12... | collective-permute-start | bytes 221192 | tf_op jit(solution)/shard_map/ppermute | solution.py:567
  22.4 4.6 %copy-start.4 = (bf16[1,4,32,1280]{3,2,1,0:T(8,128)(2,1)S(1)}, bf16[1,4,32,1280]{3,2,1,0:T(8,128)(2,1)}, u32[]{:S(2)}) copy-start(bf16[1,4,32,1280]{3,2,1,0:T(8,128)(2,1)} %refs_7_.4) | copy-start | bytes 983044
  22.4 9.5 %collective-permute-start.8 = (bf16[2,32,2560]{2,1,0:T(8,128)(2,1)S(1)}, bf16[2,32,2560]{2,1,0:T(8,128)(2,1)S(1)}, u32[]{:S(2)}, u32[]{:S(2)}) collective-permute-start(bf16[2,32,2560]{2,1,0:T(8,128)(2,1)S(1)} %get-tuple-element.44), channel_id=1, source_target_pairs={{0,1},{1,0},{2,3},{3,2},{4,5},{5,4},{6,7},{7,6},{8,9},{9,8},{10,11... | collective-permute-start | bytes 983048 | tf_op jit(solution)/shard_map/ppermute | solution.py:581
  27.8 7.1 %collective-permute-start.7 = (bf16[4,32,1280]{2,1,0:T(8,128)(2,1)S(1)}, bf16[4,32,1280]{2,1,0:T(8,128)(2,1)S(1)}, u32[]{:S(2)}, u32[]{:S(2)}) collective-permute-start(bf16[4,32,1280]{2,1,0:T(8,128)(2,1)S(1)} %second_results.1.refs_10_.refs_2_.refs_1_), channel_id=1, source_target_pairs={{0,2},{2,0},{4,6},{6,4},{8,16},{10,18},{12,20},{14,22},{16,8},{18,... | collective-permute-start | bytes 983048 | tf_op jit(solution)/shard_map/ppermute | solution.py:605
  29.5 5.4 %copy-start.6 = (bf16[1,2,32,1280]{3,2,1,0:T(8,128)(2,1)S(1)}, bf16[1,2,32,1280]{3,2,1,0:T(8,128)(2,1)}, u32[]{:S(2)}) copy-start(bf16[1,2,32,1280]{3,2,1,0:T(8,128)(2,1)} %refs_3_.3) | copy-start | bytes 491524
  29.5 5.4 %copy-start.7 = (bf16[1,2,32,1280]{3,2,1,0:T(8,128)(2,1)S(1)}, bf16[1,2,32,1280]{3,2,1,0:T(8,128)(2,1)}, u32[]{:S(2)}) copy-start(bf16[1,2,32,1280]{3,2,1,0:T(8,128)(2,1)} %refs_4_.3) | copy-start | bytes 491524
  29.5 5.4 %collective-permute-start.6 = (bf16[4,32,1280]{2,1,0:T(8,128)(2,1)S(1)}, bf16[4,32,1280]{2,1,0:T(8,128)(2,1)S(1)}, u32[]{:S(2)}, u32[]{:S(2)}) collective-permute-start(bf16[4,32,1280]{2,1,0:T(8,128)(2,1)S(1)} %get-tuple-element.43), channel_id=1, source_target_pairs={{0,8},{8,0},{16,24},{24,16},{1,9},{9,1},{17,25},{25,17},{2,10},{10... | collective-permute-start | bytes 983048 | tf_op jit(solution)/shard_map/ppermute | solution.py:609
  30.4 12.0 %collective-permute-start.13 = (bf16[2,32,2560]{2,1,0:T(8,128)(2,1)S(1)}, bf16[2,32,2560]{2,1,0:T(8,128)(2,1)S(1)}, u32[]{:S(2)}, u32[]{:S(2)}) collective-permute-start(bf16[2,32,2560]{2,1,0:T(8,128)(2,1)S(1)} %get-tuple-element.51), channel_id=1, source_target_pairs={{0,1},{1,0},{2,3},{3,2},{4,5},{5,4},{6,7},{7,6},{8,9},{9,8},{10,11... | collective-permute-start | bytes 983048 | tf_op jit(solution)/shard_map/ppermute | solution.py:581
  36.2 6.1 %collective-permute-start.9 = (bf16[32,640]{1,0:T(8,128)(2,1)S(1)}, bf16[32,640]{1,0:T(8,128)(2,1)S(1)}, u32[]{:S(2)}, u32[]{:S(2)}) collective-permute-start(bf16[32,640]{1,0:T(8,128)(2,1)S(1)} %get-tuple-element.46), channel_id=1, source_target_pairs={{0,2},{2,0},{4,6},{6,4},{1,3},{3,1},{5,7},{7,5},{8,10},{10,8},{12,... | collective-permute-start | bytes 122888 | tf_op jit(solution)/shard_map/ppermute | solution.py:567
  37.3 6.8 %collective-permute-start.10 = (bf16[32,640]{1,0:T(8,128)(2,1)S(1)}, bf16[32,640]{1,0:T(8,128)(2,1)S(1)}, u32[]{:S(2)}, u32[]{:S(2)}) collective-permute-start(bf16[32,640]{1,0:T(8,128)(2,1)S(1)} %get-tuple-element.47), channel_id=1, source_target_pairs={{0,4},{2,6},{4,0},{6,2},{1,5},{3,7},{5,1},{7,3},{8,12},{10,14},{12... | collective-permute-start | bytes 122888 | tf_op jit(solution)/shard_map/ppermute | solution.py:567
  39.1 5.8 %collective-permute-start.11 = (bf16[32,640]{1,0:T(8,128)(2,1)S(1)}, bf16[32,640]{1,0:T(8,128)(2,1)S(1)}, u32[]{:S(2)}, u32[]{:S(2)}) collective-permute-start(bf16[32,640]{1,0:T(8,128)(2,1)S(1)} %get-tuple-element.48), channel_id=1, source_target_pairs={{0,6},{2,4},{4,2},{6,0},{1,7},{3,5},{5,3},{7,1},{8,14},{10,12},{12... | collective-permute-start | bytes 122888 | tf_op jit(solution)/shard_map/ppermute | solution.py:567
  40.8 15.8 %collective-permute-start.17 = (bf16[2,32,1792]{2,1,0:T(8,128)(2,1)S(1)}, bf16[2,32,1792]{2,1,0:T(8,128)(2,1)S(1)}, u32[]{:S(2)}, u32[]{:S(2)}) collective-permute-start(bf16[2,32,1792]{2,1,0:T(8,128)(2,1)S(1)} %get-tuple-element.58), channel_id=1, source_target_pairs={{0,1},{1,0},{2,3},{3,2},{4,5},{5,4},{6,7},{7,6},{8,9},{9,8},{10,11... | collective-permute-start | bytes 688136 | tf_op jit(solution)/shard_map/ppermute | solution.py:581
  42.3 15.9 %collective-permute-start.18 = (bf16[2,32,1792]{2,1,0:T(8,128)(2,1)S(1)}, bf16[2,32,1792]{2,1,0:T(8,128)(2,1)S(1)}, u32[]{:S(2)}, u32[]{:S(2)}) collective-permute-start(bf16[2,32,1792]{2,1,0:T(8,128)(2,1)S(1)} %get-tuple-element.59), channel_id=1, source_target_pairs={{0,24},{1,25},{8,16},{9,17},{16,8},{17,9},{24,0},{25,1},{2,26},{3,... | collective-permute-start | bytes 688136 | tf_op jit(solution)/shard_map/ppermute | solution.py:577
  42.4 15.9 %collective-permute-start.19 = (bf16[2,32,1792]{2,1,0:T(8,128)(2,1)S(1)}, bf16[2,32,1792]{2,1,0:T(8,128)(2,1)S(1)}, u32[]{:S(2)}, u32[]{:S(2)}) collective-permute-start(bf16[2,32,1792]{2,1,0:T(8,128)(2,1)S(1)} %get-tuple-element.60), channel_id=1, source_target_pairs={{0,25},{1,24},{8,17},{9,16},{16,9},{17,8},{24,1},{25,0},{2,27},{3,... | collective-permute-start | bytes 688136 | tf_op jit(solution)/shard_map/ppermute | solution.py:577
  45.2 4.0 %collective-permute-start.14 = (bf16[32,640]{1,0:T(8,128)(2,1)S(1)}, bf16[32,640]{1,0:T(8,128)(2,1)S(1)}, u32[]{:S(2)}, u32[]{:S(2)}) collective-permute-start(bf16[32,640]{1,0:T(8,128)(2,1)S(1)} %later_latents.1.refs_0_), channel_id=1, source_target_pairs={{0,2},{2,0},{4,6},{6,4},{1,3},{3,1},{5,7},{7,5},{8,10},{10,8},{12,... | collective-permute-start | bytes 122888 | tf_op jit(solution)/shard_map/ppermute | solution.py:567
  45.2 5.6 %collective-permute-start.15 = (bf16[32,640]{1,0:T(8,128)(2,1)S(1)}, bf16[32,640]{1,0:T(8,128)(2,1)S(1)}, u32[]{:S(2)}, u32[]{:S(2)}) collective-permute-start(bf16[32,640]{1,0:T(8,128)(2,1)S(1)} %later_latents.1.refs_0_), channel_id=1, source_target_pairs={{0,4},{2,6},{4,0},{6,2},{1,5},{3,7},{5,1},{7,3},{8,12},{10,14},{12... | collective-permute-start | bytes 122888 | tf_op jit(solution)/shard_map/ppermute | solution.py:567
  49.2 5.8 %collective-permute-start.16 = (bf16[32,640]{1,0:T(8,128)(2,1)S(1)}, bf16[32,640]{1,0:T(8,128)(2,1)S(1)}, u32[]{:S(2)}, u32[]{:S(2)}) collective-permute-start(bf16[32,640]{1,0:T(8,128)(2,1)S(1)} %later_latents.1.refs_0_), channel_id=1, source_target_pairs={{0,6},{2,4},{4,2},{6,0},{1,7},{3,5},{5,3},{7,1},{8,14},{10,12},{12... | collective-permute-start | bytes 122888 | tf_op jit(solution)/shard_map/ppermute | solution.py:567
  55.0 5.6 %collective-permute-start.20 = (bf16[2,32,256]{2,1,0:T(8,128)(2,1)S(1)}, bf16[2,32,256]{2,1,0:T(8,128)(2,1)S(1)}, u32[]{:S(2)}, u32[]{:S(2)}) collective-permute-start(bf16[2,32,256]{2,1,0:T(8,128)(2,1)S(1)} %get-tuple-element.63.refs_8_), channel_id=1, source_target_pairs={{0,1},{1,0},{2,3},{3,2},{4,5},{5,4},{6,7},{7,6},{8,9},{9,8},{10,11... | collective-permute-start | bytes 98312 | tf_op jit(solution)/shard_map/ppermute | solution.py:581
  56.6 4.0 %collective-permute-start.21 = (bf16[2,32,256]{2,1,0:T(8,128)(2,1)S(1)}, bf16[2,32,256]{2,1,0:T(8,128)(2,1)S(1)}, u32[]{:S(2)}, u32[]{:S(2)}) collective-permute-start(bf16[2,32,256]{2,1,0:T(8,128)(2,1)S(1)} %get-tuple-element.64), channel_id=1, source_target_pairs={{0,24},{1,25},{8,16},{9,17},{16,8},{17,9},{24,0},{25,1},{2,26},{3,... | collective-permute-start | bytes 98312 | tf_op jit(solution)/shard_map/ppermute | solution.py:577
  56.6 4.2 %collective-permute-start.22 = (bf16[2,32,256]{2,1,0:T(8,128)(2,1)S(1)}, bf16[2,32,256]{2,1,0:T(8,128)(2,1)S(1)}, u32[]{:S(2)}, u32[]{:S(2)}) collective-permute-start(bf16[2,32,256]{2,1,0:T(8,128)(2,1)S(1)} %get-tuple-element.64), channel_id=1, source_target_pairs={{0,25},{1,24},{8,17},{9,16},{16,9},{17,8},{24,1},{25,0},{2,27},{3,... | collective-permute-start | bytes 98312 | tf_op jit(solution)/shard_map/ppermute | solution.py:577
  (1 other events, 0.9 us)
